TPU v7x, 32 devices: a whole 2x2x4 slice. The times are simulated.
32 devices in a mesh: dp: 8 (over y, x, core), tensor: 4 (over z).
Axes of the slice: x: 2, y: 2, z: 4, core: 2. Of those that a mesh axis runs over, the one named last changes fastest.
Arguments:
- tokens: bfloat16 [16, 512, 2048], P('dp', 'tensor'), may hold values from -6 to 6
- lengths: int32 [16], P('dp'), may hold values from 128 to 512, as said below
- norm_gain: bfloat16 [2048], P('dp'), may hold values from 0.5 to 1.5
- mixer_in: bfloat16 [2048, 3, 2048], P('dp', None, 'tensor'), may hold values from -0.125 to 0.125
- lower_bound: bfloat16 [2048], P(('tensor', 'dp')), may hold values from 0.049804688 to 0.98828125
- head_gain: bfloat16 [128], P('dp'), may hold values from 0.5 to 1.5
- head_merge: bfloat16 [2048, 2048], P(('tensor', 'dp')), may hold values from -0.125 to 0.125
- feed_gain: bfloat16 [2048], P('dp'), may hold values from 0.5 to 1.5
- gate_up: bfloat16 [2048, 2, 5632], P('dp', None, 'tensor'), may hold values from -0.125 to 0.125
- down_weight: bfloat16 [5632, 2048], P(('tensor', 'dp')), may hold values from -0.078125 to 0.078125
- out_grad: bfloat16 [16, 512, 2048], P('dp', 'tensor'), may hold values from -6 to 6
Outputs:
- block_out: bfloat16 [16, 512, 2048], P('dp', 'tensor')
- input_grad: bfloat16 [16, 512, 2048], P('dp', 'tensor')
- norm_grad: float32 [2048], P('dp')
- mixer_grad: float32 [2048, 3, 2048], P('dp', None, 'tensor')
- bound_grad: float32 [2048], P(('tensor', 'dp'))
- head_grad: float32 [128], P('dp')
- merge_grad: float32 [2048, 2048], P(('tensor', 'dp'))
- feed_grad: float32 [2048], P('dp')
- gates_grad: float32 [2048, 2, 5632], P('dp', None, 'tensor')
- down_grad: float32 [5632, 2048], P(('tensor', 'dp'))
Inputs may be any that keep to these rules, and one draw needn't show every extreme that they name: Slots 0 to lengths[s] - 1 of sequence s are valid; some sequence has exactly 512 valid slots and some other exactly 128.
All inputs are finite; a program needn't handle non-finite values.
Results may differ from a plain program's by a relative error of at most 0.024.
Values may be sent and summed in bfloat16 or wider, within the bound.
No kernel may reach another device: no remote copies, remote signals or barrier semaphores. Data moves between devices by JAX's collectives and lax.ppermute only.
A program may use at most 256 MiB of HBM per device.

v0:
```python
import jax
import jax.numpy as jnp
from jax import lax
from jax.sharding import PartitionSpec as P

GROUP = 32


EPS = 1e-06
HIGH = lax.Precision.HIGHEST


def group_step(state, block):
    queries, keys_in, values_in, log_gate = block
    cumulative = jnp.cumsum(log_gate, axis=0)
    group_end = cumulative[-1]
    carried_in = jnp.einsum("the,hef->thf", queries * jnp.exp(cumulative), state, precision=HIGH)
    length = cumulative.shape[0]
    causal = jnp.arange(length)[:, None] >= jnp.arange(length)[None, :]
    causal_four = causal[:, :, None, None]
    spread = jnp.where(causal_four, cumulative[:, None] - cumulative[None, :], -60.0)
    decays = jnp.exp(spread) * causal_four.astype(jnp.float32)
    scores = jnp.sum(queries[:, None] * keys_in[None, :] * decays, axis=-1)
    within = jnp.einsum("tsh,shf->thf", scores, values_in, precision=HIGH)
    carried = keys_in * jnp.exp(group_end[None] - cumulative)
    update = jnp.einsum("she,shf->hef", carried, values_in, precision=HIGH)
    new_state = jnp.exp(group_end)[:, :, None] * state + update
    return (new_state, carried_in + within)


def recurrence(queries, keys_in, values_in, log_gate):
    total_rows, head_count, head_width = queries.shape
    blocks = total_rows // GROUP
    stacked = tuple(
        (
            member.reshape(blocks, GROUP, head_count, head_width)
            for member in (queries, keys_in, values_in, log_gate)
        )
    )
    initial = jnp.zeros((head_count, head_width, head_width), jnp.float32)
    last_state, outputs = lax.scan(jax.checkpoint(group_step), initial, stacked)
    return outputs.reshape(total_rows, head_count, head_width)


def rounded(values):
    return lax.optimization_barrier(values.astype(jnp.bfloat16)).astype(jnp.float32)


def rms_rows(values, gain_vec):
    scaling = lax.rsqrt(jnp.mean(values * values, axis=-1, keepdims=True) + EPS)
    return (values * scaling * gain_vec, scaling)


def norm_back(values, scaling, gain_vec, upstream):
    weighted = gain_vec * upstream
    along = jnp.mean(weighted * values, axis=-1, keepdims=True)
    return (
        scaling * weighted - values * (scaling * scaling * scaling) * along,
        upstream * values * scaling,
    )


def contract_rows(first_mat, second_mat):
    return lax.dot_general(
        first_mat, second_mat, (((0,), (0,)), ((), ())), preferred_element_type=jnp.float32
    )


def contract_cols(first_mat, second_mat):
    return lax.dot_general(
        first_mat, second_mat, (((1,), (1,)), ((), ())), preferred_element_type=jnp.float32
    )


def unpack(gathered):
    norm_full, mixer_full, bound_full, head_full, merge_full, feed_full, gates_full, down_full = (
        gathered
    )
    return (
        norm_full.astype(jnp.float32),
        mixer_full.reshape(mixer_full.shape[0], -1),
        bound_full.astype(jnp.float32),
        head_full.astype(jnp.float32),
        merge_full,
        feed_full.astype(jnp.float32),
        gates_full.reshape(gates_full.shape[0], -1),
        down_full,
    )


def forward_pass(weights, rows_in, valid_rows):
    norm_vec, mixer_mat, bound_vec, head_vec, merge_mat, feed_vec, gates_mat, down_mat = weights
    rows_dev = rows_in.shape[0]
    full_rows = rows_dev * lax.axis_size("tensor")
    col_count = bound_vec.shape[0]
    head_width = head_vec.shape[0]
    head_shape = (full_rows, col_count // head_width, head_width)
    masked = rows_in.astype(jnp.float32) * valid_rows[:, None]
    normed, scale_one = rms_rows(masked, norm_vec)
    first_in = lax.all_gather(normed.astype(jnp.bfloat16), "tensor", axis=0, tiled=True)
    projected = jnp.dot(first_in, mixer_mat, preferred_element_type=jnp.float32)
    query_pre = projected[:, :col_count]
    forget_pre = projected[:, col_count : 2 * col_count]
    value_pre = projected[:, 2 * col_count :]
    queries = rounded(jax.nn.silu(query_pre))
    forget_sig = jax.nn.sigmoid(forget_pre)
    forget = bound_vec + (1.0 - bound_vec) * forget_sig
    keys_in = rounded(1.0 - forget)
    values_in = rounded(value_pre)
    log_gate = jnp.log(forget)
    mixed_rows, recur_back = jax.vjp(
        recurrence,
        queries.reshape(head_shape),
        keys_in.reshape(head_shape),
        values_in.reshape(head_shape),
        log_gate.reshape(head_shape),
    )
    scale_head = lax.rsqrt(jnp.mean(mixed_rows * mixed_rows, axis=-1, keepdims=True) + EPS)
    head_out = (
        (mixed_rows * scale_head * head_vec).reshape(full_rows, col_count).astype(jnp.bfloat16)
    )
    attn_part = lax.psum_scatter(
        jnp.dot(head_out, merge_mat, preferred_element_type=jnp.float32).astype(jnp.bfloat16),
        "tensor",
        scatter_dimension=0,
        tiled=True,
    ).astype(jnp.float32)
    middle = masked + attn_part
    normed_two, scale_two = rms_rows(middle, feed_vec)
    second_in = lax.all_gather(normed_two.astype(jnp.bfloat16), "tensor", axis=0, tiled=True)
    gate_pre = jnp.dot(second_in, gates_mat, preferred_element_type=jnp.float32)
    hidden_cols = down_mat.shape[0]
    gate_part = gate_pre[:, :hidden_cols]
    up_part = gate_pre[:, hidden_cols:]
    hidden = (jax.nn.silu(gate_part) * up_part).astype(jnp.bfloat16)
    feed_out = lax.psum_scatter(
        jnp.dot(hidden, down_mat, preferred_element_type=jnp.float32).astype(jnp.bfloat16),
        "tensor",
        scatter_dimension=0,
        tiled=True,
    ).astype(jnp.float32)
    output = (valid_rows[:, None] * (middle + feed_out)).astype(jnp.bfloat16)
    kept_state = (
        masked,
        scale_one,
        first_in,
        query_pre,
        forget_sig,
        forget,
        recur_back,
        mixed_rows,
        scale_head,
        head_out,
        middle,
        scale_two,
        second_in,
        gate_part,
        up_part,
        hidden,
    )
    return (output, kept_state)


def backward_pass(weights, kept_state, grad_in_rows, valid_rows):
    norm_vec, mixer_mat, bound_vec, head_vec, merge_mat, feed_vec, gates_mat, down_mat = weights
    (
        masked,
        scale_one,
        first_in,
        query_pre,
        forget_sig,
        forget,
        recur_back,
        mixed_rows,
        scale_head,
        head_out,
        middle,
        scale_two,
        second_in,
        gate_part,
        up_part,
        hidden,
    ) = kept_state
    full_rows = first_in.shape[0]
    col_count = bound_vec.shape[0]
    upstream = grad_in_rows.astype(jnp.float32) * valid_rows[:, None]
    branch_in = lax.all_gather(upstream.astype(jnp.bfloat16), "tensor", axis=0, tiled=True)
    hidden_grad = contract_cols(branch_in, down_mat)
    down_acc = contract_rows(hidden, branch_in)
    sig_gate = jax.nn.sigmoid(gate_part)
    silu_gate = gate_part * sig_gate
    gate_grad = hidden_grad * up_part * sig_gate * (1.0 + gate_part * (1.0 - sig_gate))
    up_grad = hidden_grad * silu_gate
    both_grad = jnp.concatenate([gate_grad, up_grad], axis=1).astype(jnp.bfloat16)
    gates_acc = contract_rows(second_in, both_grad)
    second_grad = lax.psum_scatter(
        contract_cols(both_grad, gates_mat).astype(jnp.bfloat16),
        "tensor",
        scatter_dimension=0,
        tiled=True,
    ).astype(jnp.float32)
    middle_grad, feed_terms = norm_back(middle, scale_two, feed_vec, second_grad)
    middle_grad = middle_grad + upstream
    attn_in = lax.all_gather(middle_grad.astype(jnp.bfloat16), "tensor", axis=0, tiled=True)
    out_head = contract_cols(attn_in, merge_mat)
    merge_acc = contract_rows(head_out, attn_in)
    head_rows = out_head.reshape(mixed_rows.shape)
    weighted = head_vec * head_rows
    along = jnp.mean(weighted * mixed_rows, axis=-1, keepdims=True)
    mixed_grad = scale_head * weighted - mixed_rows * (scale_head * scale_head * scale_head) * along
    head_terms = jnp.sum(head_rows * mixed_rows * scale_head, axis=(0, 1))
    query_grad, keys_grad, values_grad, log_grad = recur_back(mixed_grad)
    query_grad = query_grad.reshape(full_rows, col_count)
    keys_grad = keys_grad.reshape(full_rows, col_count)
    values_grad = values_grad.reshape(full_rows, col_count)
    log_grad = log_grad.reshape(full_rows, col_count)
    forget_grad = log_grad / forget - keys_grad
    sig_query = jax.nn.sigmoid(query_pre)
    query_back = query_grad * sig_query * (1.0 + query_pre * (1.0 - sig_query))
    forget_back = forget_grad * (1.0 - bound_vec) * forget_sig * (1.0 - forget_sig)
    bound_terms = jnp.sum(forget_grad * (1.0 - forget_sig), axis=0)
    proj_grad = jnp.concatenate([query_back, forget_back, values_grad], axis=1).astype(jnp.bfloat16)
    mixer_acc = contract_rows(first_in, proj_grad)
    first_grad = lax.psum_scatter(
        contract_cols(proj_grad, mixer_mat).astype(jnp.bfloat16),
        "tensor",
        scatter_dimension=0,
        tiled=True,
    ).astype(jnp.float32)
    masked_grad, norm_terms = norm_back(masked, scale_one, norm_vec, first_grad)
    input_rows = (valid_rows[:, None] * (masked_grad + middle_grad)).astype(jnp.bfloat16)
    model_width = mixer_acc.shape[0]
    local_grads = (
        jnp.sum(norm_terms, axis=0),
        mixer_acc.reshape(model_width, 3, col_count),
        bound_terms,
        head_terms,
        merge_acc,
        jnp.sum(feed_terms, axis=0),
        gates_acc.reshape(model_width, 2, -1),
        down_acc,
    )
    return (input_rows, local_grads)


def local(
    tokens,
    lengths,
    norm_gain,
    mixer_in,
    lower_bound,
    head_gain,
    head_merge,
    feed_gain,
    gate_up,
    down_weight,
    out_grad,
):
    batches = tokens.shape[0]
    rows_dev = tokens.shape[1]
    positions = lax.axis_index("tensor") * rows_dev + jnp.arange(rows_dev, dtype=jnp.int32)
    out_list = []
    grad_list = []
    summed = None
    pending = None
    for batch_id in range(batches):
        weights = unpack(
            (
                lax.all_gather(norm_gain, "dp", axis=0, tiled=True),
                lax.all_gather(mixer_in, "dp", axis=0, tiled=True),
                lax.all_gather(lower_bound, "dp", axis=0, tiled=True),
                lax.all_gather(head_gain, "dp", axis=0, tiled=True),
                lax.all_gather(head_merge, "dp", axis=0, tiled=True),
                lax.all_gather(feed_gain, "dp", axis=0, tiled=True),
                lax.all_gather(gate_up, "dp", axis=0, tiled=True),
                lax.all_gather(down_weight, "dp", axis=0, tiled=True),
            )
        )
        valid_rows = (positions < lengths[batch_id]).astype(jnp.float32)
        block_rows, kept_state = forward_pass(weights, tokens[batch_id], valid_rows)
        input_rows, local_grads = backward_pass(weights, kept_state, out_grad[batch_id], valid_rows)
        out_list.append(block_rows)
        grad_list.append(input_rows)
        pending = (
            local_grads
            if pending is None
            else tuple((running + addend for running, addend in zip(pending, local_grads)))
        )
    summed = (
        lax.psum_scatter(
            pending[0].astype(jnp.bfloat16), "dp", scatter_dimension=0, tiled=True
        ).astype(jnp.float32),
        lax.psum_scatter(
            pending[1].astype(jnp.bfloat16), "dp", scatter_dimension=0, tiled=True
        ).astype(jnp.float32),
        lax.psum_scatter(
            pending[2].astype(jnp.bfloat16), "dp", scatter_dimension=0, tiled=True
        ).astype(jnp.float32),
        lax.psum_scatter(
            pending[3].astype(jnp.bfloat16), "dp", scatter_dimension=0, tiled=True
        ).astype(jnp.float32),
        lax.psum_scatter(
            pending[4].astype(jnp.bfloat16), "dp", scatter_dimension=0, tiled=True
        ).astype(jnp.float32),
        lax.psum_scatter(
            pending[5].astype(jnp.bfloat16), "dp", scatter_dimension=0, tiled=True
        ).astype(jnp.float32),
        lax.psum_scatter(
            pending[6].astype(jnp.bfloat16), "dp", scatter_dimension=0, tiled=True
        ).astype(jnp.float32),
        lax.psum_scatter(
            pending[7].astype(jnp.bfloat16), "dp", scatter_dimension=0, tiled=True
        ).astype(jnp.float32),
    )
    norm_share, head_share, feed_share = lax.psum((summed[0], summed[3], summed[5]), "tensor")
    block_out = jnp.stack(out_list, axis=0)
    input_grad = jnp.stack(grad_list, axis=0)
    return (
        block_out,
        input_grad,
        norm_share,
        summed[1],
        summed[2],
        head_share,
        summed[4],
        feed_share,
        summed[6],
        summed[7],
    )


def solution(mesh):
    return jax.shard_map(
        local,
        mesh=mesh,
        in_specs=(
            P("dp", "tensor", None),
            P("dp"),
            P("dp"),
            P("dp", None, "tensor"),
            P(("tensor", "dp")),
            P("dp"),
            P(("tensor", "dp"), None),
            P("dp"),
            P("dp", None, "tensor"),
            P(("tensor", "dp"), None),
            P("dp", "tensor", None),
        ),
        out_specs=(
            P("dp", "tensor", None),
            P("dp", "tensor", None),
            P("dp"),
            P("dp", None, "tensor"),
            P(("tensor", "dp")),
            P("dp"),
            P(("tensor", "dp"), None),
            P("dp"),
            P("dp", None, "tensor"),
            P(("tensor", "dp"), None),
        ),
        check_vma=False,
    )
```

profile of v0, /device:TPU:0, one launch (start us, length us, event | category | flops | bytes accessed | tf_op | source)
XLA Modules:
  0.0 1691.3 jit_solution(4498520034669441687)
XLA Ops:
  45.1 27.5 %all-gather.27.cloned.1.call-done = bf16[512,2048]{1,0:T(8,128)(2,1)} async-done(((bf16[128,2048]{1,0:T(8,128)(2,1)}), bf16[512,2048]{1,0:T(8,128)(2,1)}) %all-gather.27.cloned.1.call-update) | async-done | bytes 2097168 | tf_op jit(solution)/shard_map/all_gather | solution.py:100
  72.6 47.9 %all-gather.17.cloned.1.call-done = bf16[2048,3,512]{0,2,1:T(8,128)(2,1)} async-done(((bf16[256,3,512]{0,2,1:T(8,128)(2,1)}), bf16[2048,3,512]{0,2,1:T(8,128)(2,1)}) %all-gather.17.cloned.1.call-update) | async-done | bytes 6291472 | tf_op jit(solution)/shard_map/all_gather | solution.py:270
  128.5 40.1 %all-gather.15.cloned.1.call-done = bf16[512,2048]{1,0:T(8,128)(2,1)} async-done(((bf16[128,2048]{1,0:T(8,128)(2,1)}), bf16[512,2048]{1,0:T(8,128)(2,1)}) %all-gather.15.cloned.1.call-update) | async-done | bytes 2097168 | tf_op jit(solution)/shard_map/all_gather | solution.py:100
  187.5 106.1 %while.79 = (s32[]{:T(128)}, f32[4,128,128]{2,1,0:T(8,128)S(1)}, f32[16,32,4,128]{3,1,2,0:T(8,128)S(1)}, f32[16,4,128,128]{3,2,1,0:T(8,128)}, f32[16,32,4,128]{3...) while((s32[]{:T(128)}, f32[4,128,128]{2,1,0:T(8,128)S(1)}, ...), condition=%wide.region_13.14_spmd.clone, body=%wide.region_10.13_spmd.clone.sunk | while | flops 60667904 | bytes 2988177 | solution.py:41
  302.7 106.1 %while.78 = (s32[]{:T(128)}, f32[4,128,128]{2,1,0:T(8,128)S(1)}, f32[16,32,4,128]{3,1,2,0:T(8,128)S(1)}, f32[16,4,128,128]{3,2,1,0:T(8,128)}, f32[16,32,4,128]{3...) while((s32[]{:T(128)}, f32[4,128,128]{2,1,0:T(8,128)S(1)}, ...), condition=%wide.region_4.5_spmd.clone, body=%wide.region_1.4_spmd.clone.sunk | while | flops 60667904 | bytes 2988177 | solution.py:41
  438.1 29.4 %reduce-scatter.12.cloned.1.call-done = bf16[128,2048]{1,0:T(8,128)(2,1)} async-done(((bf16[512,2048]{1,0:T(8,128)(2,1)}), bf16[128,2048]{1,0:T(8,128)(2,1)}) %reduce-scatter.12.cloned.1.call-update) | async-done | bytes 524304 | tf_op jit(solution)/shard_map/reduce_scatter | solution.py:122
  467.4 45.5 %reduce-scatter.16.cloned.1.call-done = bf16[128,2048]{1,0:T(8,128)(2,1)} async-done(((bf16[512,2048]{1,0:T(8,128)(2,1)}), bf16[128,2048]{1,0:T(8,128)(2,1)}) %reduce-scatter.16.cloned.1.call-update) | async-done | bytes 524304 | tf_op jit(solution)/shard_map/reduce_scatter | solution.py:122
  519.3 62.6 %all-gather.23.cloned.1.call-done = bf16[2048,2,1408]{2,1,0:T(2,128)(2,1)} async-done(((bf16[256,2,1408]{2,1,0:T(2,128)(2,1)}), bf16[2048,2,1408]{2,1,0:T(2,128)(2,1)}) %all-gather.23.cloned.1.call-update) | async-done | bytes 11534352 | tf_op jit(solution)/shard_map/all_gather | solution.py:275
  593.5 36.5 %all-gather.21.cloned.1.call-done = bf16[512,2048]{1,0:T(8,128)(2,1)} async-done(((bf16[128,2048]{1,0:T(8,128)(2,1)}), bf16[512,2048]{1,0:T(8,128)(2,1)}) %all-gather.21.cloned.1.call-update) | async-done | bytes 2097168 | tf_op jit(solution)/shard_map/all_gather | solution.py:130
  642.4 31.5 %all-gather.25.cloned.1.call-done = bf16[1408,2048]{1,0:T(8,128)(2,1)} async-done(((bf16[176,2048]{1,0:T(8,128)(2,1)}), bf16[1408,2048]{1,0:T(8,128)(2,1)}) %all-gather.25.cloned.1.call-update) | async-done | bytes 5767184 | tf_op jit(solution)/shard_map/all_gather | solution.py:276
  673.9 48.0 %all-gather.31.cloned.1.call-done = bf16[512,2048]{1,0:T(8,128)(2,1)} async-done(((bf16[128,2048]{1,0:T(8,128)(2,1)}), bf16[512,2048]{1,0:T(8,128)(2,1)}) %all-gather.31.cloned.1.call-update) | async-done | bytes 2097168 | tf_op jit(solution)/shard_map/all_gather | solution.py:187
  743.9 24.3 %all-gather.29.cloned.1.call-done = bf16[512,2048]{1,0:T(8,128)(2,1)} async-done(((bf16[128,2048]{1,0:T(8,128)(2,1)}), bf16[512,2048]{1,0:T(8,128)(2,1)}) %all-gather.29.cloned.1.call-update) | async-done | bytes 2097168 | tf_op jit(solution)/shard_map/all_gather | solution.py:130
  780.8 34.0 %all-gather.35.cloned.1.call-done = bf16[512,2048]{1,0:T(8,128)(2,1)} async-done(((bf16[128,2048]{1,0:T(8,128)(2,1)}), bf16[512,2048]{1,0:T(8,128)(2,1)}) %all-gather.35.cloned.1.call-update) | async-done | bytes 2097168 | tf_op jit(solution)/shard_map/all_gather | solution.py:187
  860.7 45.5 %reduce-scatter.24.cloned.1.call-done = bf16[128,2048]{1,0:T(8,128)(2,1)} async-done(((bf16[512,2048]{1,0:T(8,128)(2,1)}), bf16[128,2048]{1,0:T(8,128)(2,1)}) %reduce-scatter.24.cloned.1.call-update) | async-done | bytes 524304 | tf_op jit(solution)/shard_map/reduce_scatter | solution.py:196
  906.2 45.4 %reduce-scatter.14.cloned.1.call-done = bf16[128,2048]{1,0:T(8,128)(2,1)} async-done(((bf16[512,2048]{1,0:T(8,128)(2,1)}), bf16[128,2048]{1,0:T(8,128)(2,1)}) %reduce-scatter.14.cloned.1.call-update) | async-done | bytes 524304 | tf_op jit(solution)/shard_map/reduce_scatter | solution.py:136
  955.3 41.7 %reduce-scatter.18.cloned.1.call-done = bf16[128,2048]{1,0:T(8,128)(2,1)} async-done(((bf16[512,2048]{1,0:T(8,128)(2,1)}), bf16[128,2048]{1,0:T(8,128)(2,1)}) %reduce-scatter.18.cloned.1.call-update) | async-done | bytes 524304 | tf_op jit(solution)/shard_map/reduce_scatter | solution.py:136
  1015.2 14.2 add_convert_fusion
  1029.4 22.5 %convert_element_type.339 = bf16[2048,2,1408]{2,1,0:T(2,128)(2,1)} reshape(bf16[2048,2816]{1,0:T(8,128)(2,1)} %add_convert_fusion) | data formatting | bytes 23068672 | tf_op jit(solution)/shard_map/convert_element_type | solution.py:309
  1073.4 19.5 %all-gather.37.cloned.1.call-done = bf16[512,2048]{1,0:T(8,128)(2,1)} async-done(((bf16[128,2048]{1,0:T(8,128)(2,1)}), bf16[512,2048]{1,0:T(8,128)(2,1)}) %all-gather.37.cloned.1.call-update) | async-done | bytes 2097168 | tf_op jit(solution)/shard_map/all_gather | solution.py:204
  1110.1 197.0 %while.80 = (s32[]{:T(128)}, f32[4,128,128]{2,1,0:T(8,128)S(1)}, f32[16,32,4,128]{3,2,1,0:T(4,128)}, f32[16,32,4,128]{3,2,1,0:T(4,128)}, bf16[16,32,4,128]{3,1,2...) while((s32[]{:T(128)}, f32[4,128,128]{2,1,0:T(8,128)S(1)}, ...), condition=%wide.region_31.32_spmd.clone, body=%wide.region_21.31_spmd.clone.sunk | while | flops 123812864 | bytes 7069903 | solution.py:41
  1317.1 196.5 %while.81 = (s32[]{:T(128)}, f32[4,128,128]{2,1,0:T(8,128)S(1)}, f32[16,32,4,128]{3,2,1,0:T(4,128)}, f32[16,32,4,128]{3,2,1,0:T(4,128)}, bf16[16,32,4,128]{3,1,2...) while((s32[]{:T(128)}, f32[4,128,128]{2,1,0:T(8,128)S(1)}, ...), condition=%wide.region_47.48_spmd.clone, body=%wide.region_37.47_spmd.clone.sunk | while | flops 123812864 | bytes 7069903 | solution.py:41
  1576.3 40.6 %reduce-scatter.26.cloned.1.call-done = bf16[128,2048]{1,0:T(8,128)(2,1)} async-done(((bf16[512,2048]{1,0:T(8,128)(2,1)}), bf16[128,2048]{1,0:T(8,128)(2,1)}) %reduce-scatter.26.cloned.1.call-update) | async-done | bytes 524304 | tf_op jit(solution)/shard_map/reduce_scatter | solution.py:224
  1619.0 13.9 all-reduce.10
  1647.7 33.9 %reduce-scatter.28.cloned.1.call-done = bf16[256,3,512]{2,0,1:T(8,128)(2,1)} async-done(((bf16[2048,3,512]{2,0,1:T(8,128)(2,1)}), bf16[256,3,512]{2,0,1:T(8,128)(2,1)}) %reduce-scatter.28.cloned.1.call-update) | async-done | bytes 786448 | tf_op jit(solution)/shard_map/reduce_scatter | solution.py:293
  (1624 shorter events, 962.6 us)
Async XLA Ops:
  7.2 65.5 %all-gather.27.cloned.1.call-start = ((), (), s32[]{:S(2)}) async-start(), calls=%async_computation.19 | async-start | bytes 2621440 | tf_op jit(solution)/shard_map/all_gather | solution.py:100
  26.2 94.3 %all-gather.17.cloned.1.call-start = ((), (), s32[]{:S(2)}) async-start(), calls=%async_computation.12 | async-start | bytes 7077888 | tf_op jit(solution)/shard_map/all_gather | solution.py:270
  27.5 141.1 %all-gather.15.cloned.1.call-start = ((), (), s32[]{:S(2)}) async-start(), calls=%async_computation.11 | async-start | bytes 2621440 | tf_op jit(solution)/shard_map/all_gather | solution.py:100
  28.2 392.0 %all-gather.19.cloned.1.call-start = ((), (), s32[]{:S(2)}) async-start(), calls=%async_computation.13 | async-start | bytes 2359296 | tf_op jit(solution)/shard_map/all_gather | solution.py:273
  28.8 438.6 %reduce-scatter.12.cloned.1.call-start = ((), (), s32[]{:S(2)}) async-start(), calls=%async_computation.14 | async-start | bytes 2621440 | tf_op jit(solution)/shard_map/reduce_scatter | solution.py:122
  424.7 88.2 %reduce-scatter.16.cloned.1.call-start = ((), (), s32[]{:S(2)}) async-start(), calls=%async_computation.20 | async-start | bytes 2621440 | tf_op jit(solution)/shard_map/reduce_scatter | solution.py:122
  428.4 153.5 %all-gather.23.cloned.1.call-start = ((), (), s32[]{:S(2)}) async-start(), calls=%async_computation.16 | async-start | bytes 12976128 | tf_op jit(solution)/shard_map/all_gather | solution.py:275
  429.2 200.8 %all-gather.21.cloned.1.call-start = ((), (), s32[]{:S(2)}) async-start(), calls=%async_computation.15 | async-start | bytes 2621440 | tf_op jit(solution)/shard_map/all_gather | solution.py:130
  516.6 157.3 %all-gather.25.cloned.1.call-start = ((), (), s32[]{:S(2)}) async-start(), calls=%async_computation.17 | async-start | bytes 6488064 | tf_op jit(solution)/shard_map/all_gather | solution.py:276
  517.4 204.5 %all-gather.31.cloned.1.call-start = ((), (), s32[]{:S(2)}) async-start(), calls=%async_computation.23 | async-start | bytes 2621440 | tf_op jit(solution)/shard_map/all_gather | solution.py:187
  517.9 250.2 %all-gather.29.cloned.1.call-start = ((), (), s32[]{:S(2)}) async-start(), calls=%async_computation.21 | async-start | bytes 2621440 | tf_op jit(solution)/shard_map/all_gather | solution.py:130
  518.7 296.1 %all-gather.35.cloned.1.call-start = ((), (), s32[]{:S(2)}) async-start(), calls=%async_computation.27 | async-start | bytes 2621440 | tf_op jit(solution)/shard_map/all_gather | solution.py:187
  519.3 341.5 %reduce-scatter.20.cloned.1.call-start = ((), (), s32[]{:S(2)}) async-start(), calls=%async_computation.24 | async-start | bytes 2621440 | tf_op jit(solution)/shard_map/reduce_scatter | solution.py:196
  743.9 162.3 %reduce-scatter.24.cloned.1.call-start = ((), (), s32[]{:S(2)}) async-start(), calls=%async_computation.28 | async-start | bytes 2621440 | tf_op jit(solution)/shard_map/reduce_scatter | solution.py:196
  836.9 114.6 %reduce-scatter.14.cloned.1.call-start = ((), (), s32[]{:S(2)}) async-start(), calls=%async_computation.18 | async-start | bytes 2621440 | tf_op jit(solution)/shard_map/reduce_scatter | solution.py:136
  845.0 152.1 %reduce-scatter.18.cloned.1.call-start = ((), (), s32[]{:S(2)}) async-start(), calls=%async_computation.22 | async-start | bytes 2621440 | tf_op jit(solution)/shard_map/reduce_scatter | solution.py:136
  853.4 210.8 %all-gather.33.cloned.1.call-start = ((), (), s32[]{:S(2)}) async-start(), calls=%async_computation.25 | async-start | bytes 2621440 | tf_op jit(solution)/shard_map/all_gather | solution.py:204
  1001.4 91.5 %all-gather.37.cloned.1.call-start = ((), (), s32[]{:S(2)}) async-start(), calls=%async_computation.29 | async-start | bytes 2621440 | tf_op jit(solution)/shard_map/all_gather | solution.py:204
  1002.0 566.0 %all-reduce.14.cloned.1.call-start = ((), (), s32[]{:S(2)}) async-start(), calls=%async_computation.34 | async-start | bytes 23068672
  1051.9 520.1 %reduce-scatter.32.cloned.1.call-start = ((), (), s32[]{:S(2)}) async-start(), calls=%async_computation.33 | async-start | bytes 6488064 | tf_op jit(solution)/shard_map/reduce_scatter | solution.py:311
  1064.1 510.5 %reduce-scatter.30.cloned.1.call-start = ((), (), s32[]{:S(2)}) async-start(), calls=%async_computation.32 | async-start | bytes 2359296 | tf_op jit(solution)/shard_map/reduce_scatter | solution.py:302
  1313.3 263.1 %reduce-scatter.22.cloned.1.call-start = ((), (), s32[]{:S(2)}) async-start(), calls=%async_computation.26 | async-start | bytes 2621440 | tf_op jit(solution)/shard_map/reduce_scatter | solution.py:224
  1529.1 87.8 %reduce-scatter.26.cloned.1.call-start = ((), (), s32[]{:S(2)}) async-start(), calls=%async_computation.30 | async-start | bytes 2621440 | tf_op jit(solution)/shard_map/reduce_scatter | solution.py:224
  1537.3 144.4 %reduce-scatter.28.cloned.1.call-start = ((), (), s32[]{:S(2)}) async-start(), calls=%async_computation.31 | async-start | bytes 7077888 | tf_op jit(solution)/shard_map/reduce_scatter | solution.py:293
  (80 other events, 1388.8 us)
Sparse Core Ops, SparseCore 0:
  26.4 46.2 all-gather.26
  75.1 45.3 all-gather.16
  122.7 45.9 all-gather.14
  170.4 26.6 all-gather.18
  424.8 42.5 reduce-scatter.11
  469.7 43.1 reduce-scatter.15
  514.8 67.0 all-gather.22
  584.0 45.9 all-gather.20
  631.9 42.0 all-gather.24
  675.9 45.9 all-gather.30
  723.5 44.6 all-gather.28
  770.2 44.6 all-gather.34
  817.7 42.9 reduce-scatter.19
  863.0 43.1 reduce-scatter.23
  908.3 43.1 reduce-scatter.13
  953.8 43.1 reduce-scatter.17
  1001.5 45.2 all-gather.32
  1048.2 44.6 all-gather.36
  1096.4 159.5 all-reduce.13
  1259.6 59.1 reduce-scatter.31
  1322.2 41.1 reduce-scatter.29
  1529.3 42.0 reduce-scatter.21
  1573.6 43.2 reduce-scatter.25
  1620.6 61.0 reduce-scatter.27
where the time goes:
time: 1710 us; the launch traced here: 1690 us
  waiting for transfers between devices  666 us (39%)
  matrix products  363 us (21%)
  local copies, waits for them, and re-layouts  294 us (17%)
  other arithmetic  284 us (17%)
  blocking collectives  57.8 us (3%)
  between operations  18.9 us (1%)
    squeeze x160, local copies, waits for them, and re-layouts, recurrence(): last_state, outputs = lax.scan(jax.checkpoint(group_step), initial, stacked)  113 us
    reduce_scatter x2, waiting for transfers between devices, forward_pass(): lax.psum_scatter(jnp.dot(hidden, down_mat, preferred_element_type=jnp.flo...  87.1 us
    reduce_sum x32, other arithmetic, group_step(): cumulative[:, None] - cumulative[None, :]  82.1 us
    all_gather x2, waiting for transfers between devices, backward_pass(): lax.all_gather(upstream.astype(jnp.bfloat16), 'tensor', axis=0, tiled=True)  82 us
    dot_general x96, matrix products, group_step(): update = jnp.einsum('she,shf->hef', carried, values_in, precision=HIGH)  76 us
    reduce_scatter x2, waiting for transfers between devices, forward_pass(): lax.psum_scatter(jnp.dot(head_out, merge_mat, preferred_element_type=jnp....  74.8 us
    all_gather x2, waiting for transfers between devices, forward_pass(): lax.all_gather(normed.astype(jnp.bfloat16), 'tensor', axis=0, tiled=True)  67.7 us
    dot_general x8, matrix products, contract_cols(): lax.dot_general(first_mat, second_mat, (((1,), (1,)), ((), ())), preferre...  65.9 us
  transfers between devices with their start and end apart: 24, of which 18 were waited for; matrix products, arithmetic and copies ran while one was open for 54% of the time, Pallas kernels for 0%

commit v1 on v0

v1 whole, which is shorter than its diff:
```python
import functools

import jax
import jax.numpy as jnp
import numpy as np
from jax import lax
from jax.experimental import pallas as pl
from jax.experimental.pallas import tpu as pltpu
from jax.sharding import PartitionSpec as P

EPS = 1e-06
CHUNK = 32
BF = jnp.bfloat16
F32 = jnp.float32


def mm(first_mat, second_mat, first_dim, second_dim):
    return lax.dot_general(
        first_mat, second_mat, (((first_dim,), (second_dim,)), ((), ())), preferred_element_type=F32
    )


def split_sum(mask_two, values):
    high = values.astype(BF)
    rest = (values - high.astype(F32)).astype(BF)
    return mm(mask_two, jnp.concatenate([high, rest], axis=0), 1, 0)


def order_masks(size, keep):
    row = lax.broadcasted_iota(jnp.int32, (size, 2 * size), 0)
    col = lax.broadcasted_iota(jnp.int32, (size, 2 * size), 1)
    col = jnp.where(col >= size, col - size, col)
    return keep(row, col).astype(F32).astype(BF)


def causal_of(size):
    row = lax.broadcasted_iota(jnp.int32, (size, size), 0)
    col = lax.broadcasted_iota(jnp.int32, (size, size), 1)
    return col <= row


def gates_of(proj, bound, width):
    query_pre = proj[:, :width]
    sig_query = jax.nn.sigmoid(query_pre)
    sig_forget = jax.nn.sigmoid(proj[:, width : 2 * width])
    forget = bound + (1.0 - bound) * sig_forget
    queries = (query_pre * sig_query).astype(BF).astype(F32)
    keys = (1.0 - forget).astype(BF).astype(F32)
    values = proj[:, 2 * width :].astype(BF)
    return query_pre, sig_query, sig_forget, forget, queries, keys, values


def forward_body(own_ref, proj_ref, bound_ref, gain_ref, mixed_ref, head_ref, states_ref, state_ref):
    seqs = proj_ref.shape[1]
    width = proj_ref.shape[3] // 3
    hd = gain_ref.shape[1]
    heads = width // hd
    mid = CHUNK // 2 - 1

    @pl.when(pl.program_id(0) == 0)
    def _():
        state_ref[...] = jnp.zeros_like(state_ref)

    tri = order_masks(CHUNK, lambda row, col: col <= row)
    causal = causal_of(CHUNK)
    gain = gain_ref[...]
    for seq in range(seqs):
        _, _, _, forget, queries, keys, values = gates_of(proj_ref[0, seq], bound_ref[...], width)
        total = split_sum(tri, jnp.log(forget))
        middle = total[mid : mid + 1]
        end = total[CHUNK - 1 : CHUNK]
        query_near = queries * jnp.exp(total - middle)
        key_near = keys * jnp.exp(middle - total)
        query_far = (query_near * jnp.exp(middle)).astype(BF)
        key_far = (key_near * jnp.exp(end - middle)).astype(BF)
        query_near = query_near.astype(BF)
        key_near = key_near.astype(BF)
        decay = jnp.exp(end)
        for head in range(heads):
            cut = slice(head * hd, (head + 1) * hd)
            at = seq * heads + head
            state = state_ref[at]
            state_low = state.astype(BF)
            states_ref[0, at] = state_low
            scores = mm(query_near[:, cut], key_near[:, cut], 1, 1)
            scores = jnp.where(causal, scores, 0.0).astype(BF)
            mixed = mm(query_far[:, cut], state_low, 1, 1) + mm(scores, values[:, cut], 1, 0)
            state_ref[at] = state * decay[:, cut] + mm(values[:, cut], key_far[:, cut], 0, 0)
            scale = lax.rsqrt(jnp.mean(mixed * mixed, axis=-1, keepdims=True) + EPS)
            mixed_ref[0, seq, :, cut] = mixed
            head_ref[0, seq, :, cut] = (mixed * scale * gain).astype(BF)


def backward_body(
    own_ref,
    proj_ref,
    mixed_ref,
    out_ref,
    states_ref,
    bound_ref,
    gain_ref,
    grad_ref,
    bound_sum_ref,
    head_sum_ref,
    back_ref,
):
    seqs = proj_ref.shape[1]
    width = proj_ref.shape[3] // 3
    hd = gain_ref.shape[1]
    heads = width // hd
    mid = CHUNK // 2 - 1

    @pl.when(pl.program_id(0) == 0)
    def _():
        back_ref[...] = jnp.zeros_like(back_ref)
        bound_sum_ref[...] = jnp.zeros_like(bound_sum_ref)
        head_sum_ref[...] = jnp.zeros_like(head_sum_ref)

    tri = order_masks(CHUNK, lambda row, col: col <= row)
    tri_up = order_masks(CHUNK, lambda row, col: col >= row)
    tri_under = order_masks(CHUNK, lambda row, col: col < row)
    causal = causal_of(CHUNK)
    gain = gain_ref[...]
    bound = bound_ref[...]
    head_sum = jnp.zeros((1, hd), F32)
    bound_sum = jnp.zeros((1, width), F32)
    for seq in range(seqs):
        query_pre, sig_query, sig_forget, forget, queries, keys, values = gates_of(
            proj_ref[0, seq], bound, width
        )
        total = split_sum(tri, jnp.log(forget))
        middle = total[mid : mid + 1]
        end = total[CHUNK - 1 : CHUNK]
        exp_query = jnp.exp(total - middle)
        exp_key = jnp.exp(middle - total)
        query_near_f = queries * exp_query
        key_near_f = keys * exp_key
        exp_mid = jnp.exp(middle)
        exp_rest = jnp.exp(end - middle)
        query_far = (query_near_f * exp_mid).astype(BF)
        key_far = (key_near_f * exp_rest).astype(BF)
        query_near = query_near_f.astype(BF)
        key_near = key_near_f.astype(BF)
        decay = jnp.exp(end)
        later_parts = []
        sooner_parts = []
        edge_parts = []
        query_parts = []
        key_parts = []
        value_parts = []
        for head in range(heads):
            cut = slice(head * hd, (head + 1) * hd)
            at = seq * heads + head
            mixed = mixed_ref[0, seq, :, cut]
            out_head = out_ref[0, seq, :, cut].astype(F32)
            scale = lax.rsqrt(jnp.mean(mixed * mixed, axis=-1, keepdims=True) + EPS)
            weighted = gain * out_head
            along = jnp.mean(weighted * mixed, axis=-1, keepdims=True)
            grad = (scale * weighted - mixed * ((scale * scale * scale) * along)).astype(BF)
            head_sum = head_sum + jnp.sum(out_head * mixed * scale, axis=0, keepdims=True)
            state_low = states_ref[0, at]
            back = back_ref[at]
            back_low = back.astype(BF)
            value = values[:, cut]
            scores = mm(query_near[:, cut], key_near[:, cut], 1, 1)
            scores = jnp.where(causal, scores, 0.0).astype(BF)
            cross = mm(grad, value, 1, 1)
            cross = jnp.where(causal, cross, 0.0).astype(BF)
            query_far_grad = exp_mid[:, cut] * mm(grad, state_low, 1, 0)
            query_near_grad = mm(cross, key_near[:, cut], 1, 0)
            key_far_grad = exp_rest[:, cut] * mm(value, back_low, 1, 0)
            key_near_grad = mm(cross, query_near[:, cut], 0, 0)
            query_low = query_near[:, cut].astype(F32)
            key_low = key_near[:, cut].astype(F32)
            later_parts.append(query_low * (query_far_grad + query_near_grad) - key_low * key_near_grad)
            sooner_parts.append(key_low * key_far_grad)
            edge_parts.append(
                decay[:, cut] * jnp.sum(state_low.astype(F32) * back, axis=0, keepdims=True)
            )
            query_parts.append(exp_query[:, cut] * (query_far_grad + query_near_grad))
            key_parts.append(exp_key[:, cut] * (key_far_grad + key_near_grad))
            value_parts.append(mm(key_far[:, cut], back_low, 1, 1) + mm(scores, grad, 0, 0))
            back_ref[at] = back * decay[:, cut] + mm(grad, query_far[:, cut], 0, 0)
        query_grad = jnp.concatenate(query_parts, axis=1)
        key_grad = jnp.concatenate(key_parts, axis=1)
        log_grad = (
            split_sum(tri_up, jnp.concatenate(later_parts, axis=1))
            + split_sum(tri_under, jnp.concatenate(sooner_parts, axis=1))
            + jnp.concatenate(edge_parts, axis=1)
        )
        forget_grad = log_grad / forget - key_grad
        bound_sum = bound_sum + jnp.sum(forget_grad * (1.0 - sig_forget), axis=0, keepdims=True)
        grad_ref[0, seq, :, :width] = (
            query_grad * sig_query * (1.0 + query_pre * (1.0 - sig_query))
        ).astype(BF)
        grad_ref[0, seq, :, width : 2 * width] = (
            forget_grad * (1.0 - bound) * sig_forget * (1.0 - sig_forget)
        ).astype(BF)
        grad_ref[0, seq, :, 2 * width :] = jnp.concatenate(value_parts, axis=1).astype(BF)
    bound_sum_ref[...] += bound_sum
    head_sum_ref[...] += head_sum


def place_of(chunk, own, per_piece):
    return lax.bitwise_xor(chunk // per_piece, own), chunk % per_piece


def recur_forward(own, proj, bound, gain):
    pieces, seqs, rows, three = proj.shape
    width = three // 3
    hd = gain.shape[1]
    per = rows // CHUNK
    chunks = pieces * per
    many = seqs * width // hd

    def rows_at(chunk, own_ref):
        piece, block = place_of(chunk, own_ref[0], per)
        return (piece, 0, block, 0)

    return pl.pallas_call(
        forward_body,
        grid_spec=pltpu.PrefetchScalarGridSpec(
            num_scalar_prefetch=1,
            grid=(chunks,),
            in_specs=[
                pl.BlockSpec((1, seqs, CHUNK, three), rows_at),
                pl.BlockSpec((1, width), lambda chunk, own_ref: (0, 0)),
                pl.BlockSpec((1, hd), lambda chunk, own_ref: (0, 0)),
            ],
            out_specs=[
                pl.BlockSpec((1, seqs, CHUNK, width), rows_at),
                pl.BlockSpec((1, seqs, CHUNK, width), rows_at),
                pl.BlockSpec((1, many, hd, hd), lambda chunk, own_ref: (chunk, 0, 0, 0)),
            ],
            scratch_shapes=[pltpu.VMEM((many, hd, hd), F32)],
        ),
        out_shape=[
            jax.ShapeDtypeStruct((pieces, seqs, rows, width), F32),
            jax.ShapeDtypeStruct((pieces, seqs, rows, width), BF),
            jax.ShapeDtypeStruct((chunks, many, hd, hd), BF),
        ],
        compiler_params=pltpu.CompilerParams(
            dimension_semantics=("arbitrary",), vmem_limit_bytes=32 * 1024 * 1024
        ),
        name="recur_forward",
    )(own, proj, bound, gain)


def recur_backward(own, proj, mixed, out_head, states, bound, gain):
    pieces, seqs, rows, three = proj.shape
    width = three // 3
    hd = gain.shape[1]
    per = rows // CHUNK
    chunks = pieces * per
    many = seqs * width // hd

    def rows_at(step, own_ref):
        piece, block = place_of(chunks - 1 - step, own_ref[0], per)
        return (piece, 0, block, 0)

    return pl.pallas_call(
        backward_body,
        grid_spec=pltpu.PrefetchScalarGridSpec(
            num_scalar_prefetch=1,
            grid=(chunks,),
            in_specs=[
                pl.BlockSpec((1, seqs, CHUNK, three), rows_at),
                pl.BlockSpec((1, seqs, CHUNK, width), rows_at),
                pl.BlockSpec((1, seqs, CHUNK, width), rows_at),
                pl.BlockSpec((1, many, hd, hd), lambda step, own_ref: (chunks - 1 - step, 0, 0, 0)),
                pl.BlockSpec((1, width), lambda step, own_ref: (0, 0)),
                pl.BlockSpec((1, hd), lambda step, own_ref: (0, 0)),
            ],
            out_specs=[
                pl.BlockSpec((1, seqs, CHUNK, three), rows_at),
                pl.BlockSpec((1, width), lambda step, own_ref: (0, 0)),
                pl.BlockSpec((1, hd), lambda step, own_ref: (0, 0)),
            ],
            scratch_shapes=[pltpu.VMEM((many, hd, hd), F32)],
        ),
        out_shape=[
            jax.ShapeDtypeStruct((pieces, seqs, rows, three), BF),
            jax.ShapeDtypeStruct((1, width), F32),
            jax.ShapeDtypeStruct((1, hd), F32),
        ],
        compiler_params=pltpu.CompilerParams(
            dimension_semantics=("arbitrary",), vmem_limit_bytes=32 * 1024 * 1024
        ),
        name="recur_backward",
    )(own, proj, mixed, out_head, states, bound, gain)


def rms_rows(values, gain_vec):
    scaling = lax.rsqrt(jnp.mean(values * values, axis=-1, keepdims=True) + EPS)
    return values * scaling * gain_vec, scaling


def norm_back(values, scaling, gain_vec, upstream):
    weighted = gain_vec * upstream
    along = jnp.mean(weighted * values, axis=-1, keepdims=True)
    return (
        scaling * weighted - values * (scaling * scaling * scaling) * along,
        upstream * values * scaling,
    )


def assemble_body(count, at_ref, *refs):
    pieces, out_ref, held, in_sems, out_sems = refs[:count], refs[count], *refs[count + 1 :]
    rows = pieces[0].shape[0]
    loads = [pltpu.make_async_copy(pieces[i], held.at[i], in_sems.at[i]) for i in range(count)]
    for load in loads:
        load.start()
    stores = []
    for i in range(count):
        start = pl.multiple_of(at_ref[i] * rows, rows)
        loads[i].wait()
        stores.append(
            pltpu.make_async_copy(held.at[i], out_ref.at[pl.ds(start, rows), :], out_sems.at[i])
        )
        stores[i].start()
    for store in stores:
        store.wait()


def assemble(at, pieces):
    count = len(pieces)
    rows, cols = pieces[0].shape
    if rows % 16:
        whole = jnp.zeros((count * rows, cols), pieces[0].dtype)
        for i, piece in enumerate(pieces):
            whole = lax.dynamic_update_slice_in_dim(whole, piece, at[i] * rows, 0)
        return whole
    return pl.pallas_call(
        functools.partial(assemble_body, count),
        in_specs=[pl.BlockSpec(memory_space=pltpu.SMEM)] + [pl.BlockSpec(memory_space=pl.ANY)] * count,
        out_specs=pl.BlockSpec(memory_space=pl.ANY),
        out_shape=jax.ShapeDtypeStruct((count * rows, cols), pieces[0].dtype),
        scratch_shapes=[
            pltpu.VMEM((count, rows, cols), pieces[0].dtype),
            pltpu.SemaphoreType.DMA((count,)),
            pltpu.SemaphoreType.DMA((count,)),
        ],
        compiler_params=pltpu.CompilerParams(vmem_limit_bytes=32 * 1024 * 1024),
        name="assemble",
    )(at, *pieces)


AXES = ("dp", "tensor")


def make_local(dp_size, tensor_size):
    columns = dp_size // 2
    bits = [1 << i for i in range(columns.bit_length() - 1)]

    def route(step, invert=False):
        pairs = []
        for dp in range(dp_size):
            for z in range(tensor_size):
                col, core, place = step(dp >> 1, dp & 1, z)
                pair = (dp * tensor_size + z, (col * 2 + core) * tensor_size + place)
                pairs.append(pair[::-1] if invert else pair)
        return sorted(pairs)

    def spread(flip):
        return lambda col, core, z: (col, z & 1, 2 * (core ^ flip) + (z >> 1))

    spreads = [route(spread(flip)) for flip in (0, 1)]
    returns = [route(spread(flip), True) for flip in (0, 1)]
    core_swap = route(lambda col, core, z: (col, core ^ 1, z))
    z_swap = route(lambda col, core, z: (col, core, z ^ 1))
    col_swap = {bit: route(lambda col, core, z, bit=bit: (col ^ bit, core, z)) for bit in bits}
    orders = [bits, bits[::-1]]

    def move(array, pairs):
        return lax.ppermute(array, AXES, pairs)

    def sum_all(array):
        total = dp_size * tensor_size
        for step in range(total.bit_length() - 1):
            array = array + move(array, [(at, at ^ (1 << step)) for at in range(total)])
        return array

    def gather_weight(shard, places):
        pieces = []
        spots = []
        for half in range(2):
            held = [(0, move(shard, spreads[half]))]
            for bit in orders[half]:
                held = held + [(at ^ bit, move(piece, col_swap[bit])) for at, piece in held]
            for at, piece in held:
                pieces.append(piece)
                spots.append(places(at, half))
        return assemble(jnp.stack(spots).astype(jnp.int32), pieces)

    def scatter_grad(piece_of):
        total = None
        for half in range(2):
            held = {at: piece_of(at, half) for at in range(columns)}
            for bit in orders[half][::-1]:
                for at in sorted(held):
                    if at & bit:
                        arrived = move(held.pop(at), col_swap[bit])
                        held[at ^ bit] = (
                            held[at ^ bit].astype(F32) + arrived.astype(F32)
                        ).astype(BF)
            back = move(held[0], returns[half]).astype(F32)
            total = back if total is None else total + back
        return total

    def gather_rows(own):
        near = move(own, core_swap)
        far = move(own, z_swap)
        return jnp.stack([own, near, far, move(far, core_swap)])

    def scatter_rows(far_pair, own_pair):
        far = far_pair[0].astype(F32) + move(far_pair[1], core_swap).astype(F32)
        far = move(far.astype(BF), z_swap)
        return own_pair[0].astype(F32) + move(own_pair[1], core_swap).astype(F32) + far.astype(F32)

    def split_rows(compute, *arrays):
        half = arrays[0].shape[0] // 2
        return [compute(*(array[at:to] for array in arrays)) for at, to in ((half, 2 * half), (0, half))]

    def dot_rows(first_mat, second_mat, second_dim):
        return lax.dot_general(
            first_mat,
            second_mat,
            (((first_mat.ndim - 1,), (second_dim,)), ((), ())),
            preferred_element_type=F32,
        )

    def local(
        tokens,
        lengths,
        norm_gain,
        mixer_in,
        lower_bound,
        head_gain,
        head_merge,
        feed_gain,
        gate_up,
        down_weight,
        out_grad,
    ):
        seqs, rows, model = tokens.shape
        dp_at = lax.axis_index("dp")
        z_at = lax.axis_index("tensor")
        col = dp_at // 2
        half_at = z_at // 2
        role = 2 * (z_at % 2) + dp_at % 2

        def places(at, half):
            return lax.bitwise_xor(col, at) * 2 + (half_at if half == 0 else 1 - half_at)

        lens = move(lengths, spreads[0])
        tok = move(tokens, spreads[0])
        mixer_mat = gather_weight(mixer_in.reshape(mixer_in.shape[0], -1), places)
        merge_mat = gather_weight(head_merge, places)
        gates_mat = gather_weight(gate_up.reshape(gate_up.shape[0], -1), places)
        down_mat = gather_weight(down_weight, places)
        out_rows = move(out_grad, spreads[0])

        vectors = [norm_gain, feed_gain, head_gain, lower_bound]
        vector_ends = np.cumsum([vector.shape[0] for vector in vectors])
        packed = jnp.zeros((dp_size * tensor_size, vector_ends[-1]), BF)
        packed = lax.dynamic_update_slice_in_dim(
            packed, jnp.concatenate(vectors)[None], dp_at * tensor_size + z_at, 0
        )
        packed = sum_all(packed).reshape(dp_size, tensor_size, -1).astype(F32)
        norm_vec = packed[:, 0, : vector_ends[0]].reshape(-1)
        feed_vec = packed[:, 0, vector_ends[0] : vector_ends[1]].reshape(-1)
        head_vec = packed[:, 0, vector_ends[1] : vector_ends[2]].reshape(1, -1)
        bound_vec = lax.dynamic_index_in_dim(packed, role, 1, False)[:, vector_ends[2] :].reshape(1, -1)

        positions = role * rows + jnp.arange(rows, dtype=jnp.int32)
        valid = (positions[None, :] < lens[:, None]).astype(F32)[:, :, None]
        own = role.astype(jnp.int32).reshape(1)

        masked = tok.astype(F32) * valid
        normed, scale_one = rms_rows(masked, norm_vec)
        first_in = gather_rows(normed.astype(BF))
        projected = dot_rows(first_in, mixer_mat, 0)
        mixed, head_out, states = recur_forward(own, projected, bound_vec, head_vec)
        attn = scatter_rows(*split_rows(lambda part: dot_rows(part, merge_mat, 0).astype(BF), head_out))
        middle = masked + attn
        normed_two, scale_two = rms_rows(middle, feed_vec)
        second_in = gather_rows(normed_two.astype(BF))
        gate_pre = dot_rows(second_in, gates_mat, 0)
        hidden_cols = down_mat.shape[0]
        gate_part = gate_pre[..., :hidden_cols]
        up_part = gate_pre[..., hidden_cols:]
        sig_gate = jax.nn.sigmoid(gate_part)
        hidden = (gate_part * sig_gate * up_part).astype(BF)
        feed_out = scatter_rows(*split_rows(lambda part: dot_rows(part, down_mat, 0).astype(BF), hidden))
        block_out = move((valid * (middle + feed_out)).astype(BF), returns[0])

        upstream = out_rows.astype(F32) * valid
        branch_in = gather_rows(upstream.astype(BF))
        hidden_grad = dot_rows(branch_in, down_mat, 1)
        gate_grad = hidden_grad * up_part * sig_gate * (1.0 + gate_part * (1.0 - sig_gate))
        up_grad = hidden_grad * gate_part * sig_gate
        both_grad = jnp.concatenate([gate_grad, up_grad], axis=-1).astype(BF)
        second_grad = scatter_rows(
            *split_rows(lambda part: dot_rows(part, gates_mat, 1).astype(BF), both_grad)
        )
        middle_grad, feed_terms = norm_back(middle, scale_two, feed_vec, second_grad)
        middle_grad = middle_grad + upstream
        attn_in = gather_rows(middle_grad.astype(BF))
        out_head = dot_rows(attn_in, merge_mat, 1)
        proj_grad, bound_sum, head_sum = recur_backward(
            own, projected, mixed, out_head, states, bound_vec, head_vec
        )
        first_grad = scatter_rows(
            *split_rows(lambda part: dot_rows(part, mixer_mat, 1).astype(BF), proj_grad)
        )
        masked_grad, norm_terms = norm_back(masked, scale_one, norm_vec, first_grad)
        input_grad = move((valid * (masked_grad + middle_grad)).astype(BF), returns[0])

        def weight_grad(first_mat, second_mat):
            return lax.dot_general(
                first_mat.reshape(-1, first_mat.shape[-1]),
                second_mat.reshape(-1, second_mat.shape[-1]),
                (((0,), (0,)), ((), ())),
                preferred_element_type=F32,
            ).astype(BF)

        def by_rows(whole, count):
            return lambda at, half: lax.dynamic_slice_in_dim(whole, places(at, half) * count, count, 0)

        down_grad = scatter_grad(by_rows(weight_grad(hidden, branch_in), down_weight.shape[0]))
        gates_grad = scatter_grad(by_rows(weight_grad(second_in, both_grad), gate_up.shape[0]))
        merge_grad = scatter_grad(by_rows(weight_grad(head_out, attn_in), head_merge.shape[0]))
        mixer_grad = scatter_grad(by_rows(weight_grad(first_in, proj_grad), mixer_in.shape[0]))

        bound_all = jnp.zeros((tensor_size, bound_sum.shape[1]), F32)
        bound_all = lax.dynamic_update_slice_in_dim(bound_all, bound_sum, role, 0)
        sums = [
            jnp.sum(norm_terms, axis=(0, 1)),
            jnp.sum(feed_terms, axis=(0, 1)),
            head_sum.reshape(-1),
            bound_all.reshape(-1),
        ]
        ends = np.cumsum([part.shape[0] for part in sums])
        summed = sum_all(jnp.concatenate(sums))

        def shard_of(vector, count, at):
            return lax.dynamic_slice_in_dim(vector, at * count, count, 0)

        return (
            block_out,
            input_grad,
            shard_of(summed[: ends[0]], norm_gain.shape[0], dp_at),
            mixer_grad.reshape(mixer_in.shape),
            shard_of(summed[ends[2] :], lower_bound.shape[0], z_at * dp_size + dp_at),
            shard_of(summed[ends[1] : ends[2]], head_gain.shape[0], dp_at),
            merge_grad,
            shard_of(summed[ends[0] : ends[1]], feed_gain.shape[0], dp_at),
            gates_grad.reshape(gate_up.shape),
            down_grad,
        )

    return local


def solution(mesh):
    rows_spec = P("dp", "tensor", None)
    wide_spec = P("dp", None, "tensor")
    tall_spec = P(("tensor", "dp"), None)
    return jax.shard_map(
        make_local(mesh.shape["dp"], mesh.shape["tensor"]),
        mesh=mesh,
        in_specs=(
            rows_spec,
            P("dp"),
            P("dp"),
            wide_spec,
            P(("tensor", "dp")),
            P("dp"),
            tall_spec,
            P("dp"),
            wide_spec,
            tall_spec,
            rows_spec,
        ),
        out_specs=(
            rows_spec,
            rows_spec,
            P("dp"),
            wide_spec,
            P(("tensor", "dp")),
            P("dp"),
            tall_spec,
            P("dp"),
            wide_spec,
            tall_spec,
        ),
        check_vma=False,
    )
```

time: 1710 us -> 1030 us (0.60)
  starting transfers between devices: 2.01 us -> 298 us
  waiting for transfers between devices: 666 us -> 410 us
  other arithmetic: 284 us -> 40.6 us
  local copies, waits for them, and re-layouts: 294 us -> 59.1 us
  matrix products: 363 us -> 141 us
  Pallas kernels: 0 us -> 68.9 us
  blocking collectives: 57.8 us -> 0 us
    ppermute x0 -> x103, waiting for transfers between devices: none -> 410 us  [move(): return lax.ppermute(array, AXES, pairs)]
    all_gather x12 -> x0, waiting for transfers between devices: 372 us -> none  [the longest x2 82 us: backward_pass(): lax.all_gather(upstream.astype(jnp.bfloat16), 'tensor', axis=0, tiled=True)]
    ppermute x0 -> x103, starting transfers between devices: none -> 298 us  [move(): return lax.ppermute(array, AXES, pairs)]
    reduce_scatter x11 -> x0, waiting for transfers between devices: 289 us -> none  [the longest x2 87.1 us: forward_pass(): lax.psum_scatter(jnp.dot(hidden, down_mat, preferred_element_type=jnp.flo...]
    dot_general x312 -> x16, matrix products: 363 us -> 141 us  [the longest x12 96.5 us: dot_rows(): lax.dot_general(first_mat, second_mat, (((first_mat.ndim - 1,), (second_d...]
    reduce_sum x104 -> x2, other arithmetic: 138 us -> 2.01 us  [the longest x1 1.05 us: local(): jnp.sum(norm_terms, axis=(0, 1))]
    squeeze x192 -> x8, local copies, waits for them, and re-layouts: 113 us -> 5.65 us  [the longest x4 3.29 us: scatter_rows(): far = far_pair[0].astype(F32) + move(far_pair[1], core_swap).astype(F32)]
    pallas_call x0 -> x6, Pallas kernels: none -> 68.9 us  [the longest x1 31.3 us: recur_backward(): pl.pallas_call(backward_body, grid_spec=pltpu.PrefetchScalarGridSpec(num_...]
  transfers between devices with their start and end apart: 24 -> 103, of which waited for: 18 -> 39; matrix products, arithmetic and copies ran while one was open for 54% -> 11% of each run, Pallas kernels for 0% -> 5%
where the time goes in v1:
time: 1030 us; the launch traced here: 1020 us
  waiting for transfers between devices  410 us (40%)
  starting transfers between devices  298 us (29%)
  matrix products  141 us (14%)
  Pallas kernels  68.9 us (7%)
  local copies, waits for them, and re-layouts  59.1 us (6%)
  other arithmetic  40.6 us (4%)
    ppermute x103, waiting for transfers between devices, move(): return lax.ppermute(array, AXES, pairs)  410 us
    ppermute x103, starting transfers between devices, move(): return lax.ppermute(array, AXES, pairs)  298 us
    dot_general x12, matrix products, dot_rows(): lax.dot_general(first_mat, second_mat, (((first_mat.ndim - 1,), (second_d...  96.5 us
    dot_general x4, matrix products, weight_grad(): lax.dot_general(first_mat.reshape(-1, first_mat.shape[-1]), second_mat.re...  44 us
    unnamed x199, local copies, waits for them, and re-layouts  37.8 us
    pallas_call x1, Pallas kernels, recur_backward(): pl.pallas_call(backward_body, grid_spec=pltpu.PrefetchScalarGridSpec(num_...  31.3 us
    pallas_call x1, Pallas kernels, recur_forward(): pl.pallas_call(forward_body, grid_spec=pltpu.PrefetchScalarGridSpec(num_s...  20.9 us
  transfers between devices with their start and end apart: 103, of which 39 were waited for; matrix products, arithmetic and copies ran while one was open for 11% of the time, Pallas kernels for 5%

profile of v1, /device:TPU:0, one launch (start us, length us, event | category | flops | bytes accessed | tf_op | source)
XLA Modules:
  0.0 1018.7 jit_solution(2073886726279869966)
XLA Ops:
  6.5 12.9 %collective-permute-done.2 = bf16[32,592]{1,0:T(8,128)(2,1)S(1)} collective-permute-done((bf16[32,592]{1,0:T(8,128)(2,1)S(1)}, bf16[32,592]{1,0:T(8,128)(2,1)S(1)}, u32[]{:S(2)}, u32[]{:S(2)}) %collective-permute-start.2) | collective-permute-done | bytes 37920 | tf_op jit(solution)/shard_map/ppermute | solution.py:375
  48.2 30.3 %collective-permute-start.22 = (bf16[64,2048]{1,0:T(8,128)(2,1)}, bf16[64,2048]{1,0:T(8,128)(2,1)S(1)}, u32[]{:S(2)}, u32[]{:S(2)}) collective-permute-start(bf16[64,2048]{1,0:T(8,128)(2,1)} %param.17), channel_id=1, source_target_pairs={{0,2},{1,6},{2,3},{3,7},{4,0},{5,4},{6,1},{7,5},{8,10},{9,14},{10,... | collective-permute-start | bytes 786440 | tf_op jit(solution)/shard_map/ppermute | solution.py:375
  121.8 13.9 %collective-permute-done.15.refs_5_ = bf16[256,1536]{1,0:T(8,128)(2,1)} collective-permute-done((bf16[256,1536]{1,0:T(8,128)(2,1)}, bf16[256,1536]{1,0:T(8,128)(2,1)}, u32[]{:S(2)}, u32[]{:S(2)}) %collective-permute-start.15) | collective-permute-done | bytes 786464 | tf_op jit(solution)/shard_map/ppermute | solution.py:375
  170.0 20.9 %recur_forward.1 = (f32[4,2,128,512]{3,2,1,0:T(8,128)S(1)}, bf16[4,2,128,512]{3,2,1,0:T(8,128)(2,1)S(1)}, bf16[16,8,128,128]{3,2,1,0:T(8,128)(2,1)S(1)}) custom-call(s32[1]{0:T(128)} %bitcast.own_ref, f32[4,2,128,1536]{3,2,1,0:T(8,128)S(1)} %fusion.10.proj_ref, f32[1,512]{1,0:T(1,128)S(1)} %reshape.144.bound_ref, f32[1,128]{1,0:T(1,128)S(1)} %reshape_squeeze.3.gain_ref), custom_call_target="tpu_custom_call" | custom-call | tf_op jit(solution)/shard_map/recur_forward/pallas_call | solution.py:220
  210.9 38.4 %collective-permute-start.26 = (bf16[2,128,2048]{2,1,0:T(8,128)(2,1)S(1)}, bf16[2,128,2048]{2,1,0:T(8,128)(2,1)S(1)}, u32[]{:S(2)}, u32[]{:S(2)}) collective-permute-start(bf16[2,128,2048]{2,1,0:T(8,128)(2,1)S(1)} %slice_bitcast_fusion.14), channel_id=1, source_target_pairs={{0,4},{1,5},{2,6},{3,7},{4,0},{5,1},{6,2},{7,3},{8,12},{9,13},{10,... | collective-permute-start | bytes 3145736 | tf_op jit(solution)/shard_map/ppermute | solution.py:375
  250.4 59.3 %collective-permute-start.28 = (bf16[2,128,2048]{2,1,0:T(8,128)(2,1)S(1)}, bf16[2,128,2048]{2,1,0:T(8,128)(2,1)S(1)}, u32[]{:S(2)}, u32[]{:S(2)}) collective-permute-start(bf16[2,128,2048]{2,1,0:T(8,128)(2,1)S(1)} %fusion.45), channel_id=1, source_target_pairs={{0,1},{1,0},{2,3},{3,2},{4,5},{5,4},{6,7},{7,6},{8,9},{9,8},{10,11... | collective-permute-start | bytes 3145736 | tf_op jit(solution)/shard_map/ppermute | solution.py:375
  314.0 12.4 %collective-permute-done.41.refs_1_ = bf16[176,2048]{1,0:T(8,128)(2,1)S(1)} collective-permute-done((bf16[176,2048]{1,0:T(8,128)(2,1)S(1)}, bf16[176,2048]{1,0:T(8,128)(2,1)S(1)}, u32[]{:S(2)}, u32[]{:S(2)}) %collective-permute-start.41) | collective-permute-done | bytes 720928 | tf_op jit(solution)/shard_map/ppermute | solution.py:375
  346.9 29.5 %collective-permute-done.46.refs_6_ = bf16[176,2048]{1,0:T(8,128)(2,1)S(1)} collective-permute-done((bf16[176,2048]{1,0:T(8,128)(2,1)S(1)}, bf16[176,2048]{1,0:T(8,128)(2,1)S(1)}, u32[]{:S(2)}, u32[]{:S(2)}) %collective-permute-start.46) | collective-permute-done | bytes 720928 | tf_op jit(solution)/shard_map/ppermute | solution.py:375
  376.9 15.2 %collective-permute-done.43.refs_3_ = bf16[176,2048]{1,0:T(8,128)(2,1)S(1)} collective-permute-done((bf16[176,2048]{1,0:T(8,128)(2,1)S(1)}, bf16[176,2048]{1,0:T(8,128)(2,1)S(1)}, u32[]{:S(2)}, u32[]{:S(2)}) %collective-permute-start.43) | collective-permute-done | bytes 720928 | tf_op jit(solution)/shard_map/ppermute | solution.py:375
  407.2 15.8 %collective-permute-done.34.refs_2_ = bf16[256,2816]{1,0:T(8,128)(2,1)S(1)} collective-permute-done((bf16[256,2816]{1,0:T(8,128)(2,1)S(1)}, bf16[256,2816]{1,0:T(8,128)(2,1)S(1)}, u32[]{:S(2)}, u32[]{:S(2)}) %collective-permute-start.34) | collective-permute-done | bytes 1441824 | tf_op jit(solution)/shard_map/ppermute | solution.py:375
  459.6 18.4 %fusion.4 = f32[4,2,128,2816]{3,2,1,0:T(8,128)} fusion(bf16[2048,2816]{1,0:T(8,128)(2,1)} %assemble.6, bf16[1,2,128,2048]{3,2,1,0:T(8,128)(2,1)} %bitcast.28, bf16[1,2,128,2048]{3,2,1,0:T(8,128)(2,1)} %bitcast.27, bf16[1,2,128,2048]{3,2,1,0:T(8,128)(2,1)} %bitcast.26, bf16[1,2,128,2048]{3,2,1,0:T(8,128)(2,1)S(1)} %fusion.78), kind=kOutput, calls=%fused_computation.7 | convolution fusion | flops 11817451520 | bytes 27262976 | tf_op jit(solution)/shard_map/dot_general | solution.py:425
  478.0 14.5 %multiply_convert_fusion.1 = (bf16[4,2,128,1408]{3,2,1,0:T(8,128)(2,1)}, bf16[4,2,128,1408]{3,2,1,0:T(8,128)(2,1)}, bf16[4,2,128,1408]{3,2,1,0:T(8,128)(2,1)}) fusion(f32[4,2,128,2816]{3,2,1,0:T(8,128)} %fusion.4, bf16[1408,2048]{1,0:T(8,128)(2,1)S(1)} %assemble.7, bf16[1,2,128,2048]{3,2,1,0:T(8,128)(2,1)} %bitcast.41, ...), kind=kOutput, calls=%fused_computation.23 | convolution fusion | flops 5934940160 | bytes 30146560 | tf_op jit(solution)/shard_map/dot_general | solution.py:425
  512.7 13.2 %fusion.27 = bf16[2,2,128,2048]{3,2,1,0:T(8,128)(2,1)} fusion(bf16[4,2,128,1408]{3,2,1,0:T(8,128)(2,1)S(1)} %copy-done.84, bf16[1408,2048]{1,0:T(8,128)(2,1)S(1)} %assemble.7), kind=kOutput, calls=%fused_computation.34 | convolution fusion | flops 2953838592 | bytes 10747904 | tf_op jit(solution)/shard_map/dot_general | solution.py:425
  530.5 18.2 %bitcast_convert_fusion = bf16[2048,2816]{1,0:T(8,128)(2,1)} fusion(bf16[4,2,128,1408]{3,2,1,0:T(8,128)(2,1)} %get-tuple-element.51, bf16[4,2,128,1408]{3,2,1,0:T(8,128)(2,1)} %get-tuple-element.50, bf16[1,2,128,2048]{3,2,1,0:T(8,128)(2,1)} %bitcast.28, bf16[1,2,128,2048]{3,2,1,0:T(8,128)(2,1)} %bitcast.27, bf16[1,2,128,2048]{3,2,1,0:T(8,128)(2,1)} %bitcast.26, ...), kind=kOutput, calls=%fused_computation | convolution fusion | flops 11834753024 | bytes 21495808 | tf_op jit(solution)/shard_map/dot_general | solution.py:520
  569.1 13.9 %collective-permute-done.96 = bf16[176,2048]{1,0:T(8,128)(2,1)} collective-permute-done((bf16[176,2048]{1,0:T(8,128)(2,1)}, bf16[176,2048]{1,0:T(8,128)(2,1)}, u32[]{:S(2)}, u32[]{:S(2)}) %collective-permute-start.96) | collective-permute-done | bytes 720928 | tf_op jit(solution)/shard_map/ppermute | solution.py:375
  590.4 23.4 %collective-permute-done.88 = bf16[256,2816]{1,0:T(8,128)(2,1)S(1)} collective-permute-done((bf16[256,2816]{1,0:T(8,128)(2,1)S(1)}, bf16[256,2816]{1,0:T(8,128)(2,1)S(1)}, u32[]{:S(2)}, u32[]{:S(2)}) %collective-permute-start.88) | collective-permute-done | bytes 1441824 | tf_op jit(solution)/shard_map/ppermute | solution.py:375
  650.5 18.1 %collective-permute-done.50 = bf16[2,128,2048]{2,1,0:T(8,128)(2,1)S(1)} collective-permute-done((bf16[2,128,2048]{2,1,0:T(8,128)(2,1)S(1)}, bf16[2,128,2048]{2,1,0:T(8,128)(2,1)S(1)}, u32[]{:S(2)}, u32[]{:S(2)}) %collective-permute-start.50) | collective-permute-done | bytes 1048608 | tf_op jit(solution)/shard_map/ppermute | solution.py:375
  672.1 19.0 %collective-permute-done.99 = bf16[176,2048]{1,0:T(8,128)(2,1)} collective-permute-done((bf16[176,2048]{1,0:T(8,128)(2,1)S(1)}, bf16[176,2048]{1,0:T(8,128)(2,1)}, u32[]{:S(2)}, u32[]{:S(2)}) %collective-permute-start.99) | collective-permute-done | bytes 720928 | tf_op jit(solution)/shard_map/ppermute | solution.py:375
  698.0 22.9 %collective-permute-done.89 = bf16[256,2816]{1,0:T(8,128)(2,1)} collective-permute-done((bf16[256,2816]{1,0:T(8,128)(2,1)}, bf16[256,2816]{1,0:T(8,128)(2,1)}, u32[]{:S(2)}, u32[]{:S(2)}) %collective-permute-start.89) | collective-permute-done | bytes 1441824 | tf_op jit(solution)/shard_map/ppermute | solution.py:375
  733.6 17.8 %collective-permute-done.102 = bf16[176,2048]{1,0:T(8,128)(2,1)S(1)} collective-permute-done((bf16[176,2048]{1,0:T(8,128)(2,1)S(1)}, bf16[176,2048]{1,0:T(8,128)(2,1)S(1)}, u32[]{:S(2)}, u32[]{:S(2)}) %collective-permute-start.102) | collective-permute-done | bytes 720928 | tf_op jit(solution)/shard_map/ppermute | solution.py:375
  760.1 31.3 %recur_backward.1 = (bf16[4,2,128,1536]{3,2,1,0:T(8,128)(2,1)S(1)}, f32[1,512]{1,0:T(1,128)S(1)}, f32[1,128]{1,0:T(1,128)S(1)}) custom-call(s32[1]{0:T(128)} %bitcast.own_ref, f32[4,2,128,1536]{3,2,1,0:T(8,128)S(1)} %bitcast.185, f32[4,2,128,512]{3,2,1,0:T(8,128)S(1)} %copy-done.5, f32[4,2,128,512]{3,2,1,0:T(8,128)S(1)} %fusion.48.out_ref, ...), custom_call_target="tpu_custom_call" | custom-call | tf_op jit(solution)/shard_map/recur_backward/pallas_call | solution.py:261
  849.3 17.0 %collective-permute-done.85 = bf16[64,2048]{1,0:T(8,128)(2,1)S(1)} collective-permute-done((bf16[64,2048]{1,0:T(8,128)(2,1)S(1)}, bf16[64,2048]{1,0:T(8,128)(2,1)S(1)}, u32[]{:S(2)}, u32[]{:S(2)}) %collective-permute-start.85) | collective-permute-done | bytes 262176 | tf_op jit(solution)/shard_map/ppermute | solution.py:375
  903.0 41.7 %collective-permute-done.67 = f32[6272]{0:T(1024)S(1)} collective-permute-done((f32[6272]{0:T(1024)S(1)}, f32[6272]{0:T(1024)S(1)}, u32[]{:S(2)}, u32[]{:S(2)}) %collective-permute-start.67) | collective-permute-done | bytes 25120 | tf_op jit(solution)/shard_map/ppermute | solution.py:375
  974.0 37.5 %collective-permute-done.78 = bf16[256,1536]{1,0:T(8,128)(2,1)} collective-permute-done((bf16[256,1536]{1,0:T(8,128)(2,1)}, bf16[256,1536]{1,0:T(8,128)(2,1)}, u32[]{:S(2)}, u32[]{:S(2)}) %collective-permute-start.78) | collective-permute-done | bytes 786464 | tf_op jit(solution)/shard_map/ppermute | solution.py:375
  (490 shorter events, 461.1 us)
Async XLA Ops:
  0.7 80.0 %collective-permute-start.1 = (bf16[2,128,2048]{2,1,0:T(8,128)(2,1)}, bf16[2,128,2048]{2,1,0:T(8,128)(2,1)S(1)}, u32[]{:S(2)}, u32[]{:S(2)}) collective-permute-start(bf16[2,128,2048]{2,1,0:T(8,128)(2,1)} %param.11), channel_id=1, source_target_pairs={{0,0},{1,4},{2,1},{3,5},{4,2},{5,6},{6,3},{7,7},{8,8},{9,12},{10,9... | collective-permute-start | bytes 3145736 | tf_op jit(solution)/shard_map/ppermute | solution.py:375
  35.7 59.3 %collective-permute-start.10 = (bf16[256,1536]{1,0:T(8,128)(2,1)}, bf16[256,1536]{1,0:T(8,128)(2,1)S(1)}, u32[]{:S(2)}, u32[]{:S(2)}) collective-permute-start(bf16[256,1536]{1,0:T(8,128)(2,1)} %copy.28), channel_id=1, source_target_pairs={{0,0},{1,4},{2,1},{3,5},{4,2},{5,6},{6,3},{7,7},{8,8},{9,12},{10,9... | collective-permute-start | bytes 2359304 | tf_op jit(solution)/shard_map/ppermute | solution.py:375
  37.4 62.6 %collective-permute-start.14 = (bf16[256,1536]{1,0:T(8,128)(2,1)}, bf16[256,1536]{1,0:T(8,128)(2,1)}, u32[]{:S(2)}, u32[]{:S(2)}) collective-permute-start(bf16[256,1536]{1,0:T(8,128)(2,1)} %copy.28), channel_id=1, source_target_pairs={{0,2},{1,6},{2,3},{3,7},{4,0},{5,4},{6,1},{7,5},{8,10},{9,14},{10,... | collective-permute-start | bytes 2359304 | tf_op jit(solution)/shard_map/ppermute | solution.py:375
  195.8 115.4 %collective-permute-start.32 = (bf16[256,2816]{1,0:T(8,128)(2,1)S(1)}, bf16[256,2816]{1,0:T(8,128)(2,1)S(1)}, u32[]{:S(2)}, u32[]{:S(2)}) collective-permute-start(bf16[256,2816]{1,0:T(8,128)(2,1)S(1)} %bitcast.197), channel_id=1, source_target_pairs={{0,0},{1,4},{2,1},{3,5},{4,2},{5,6},{6,3},{7,7},{8,8},{9,12},{10,9... | collective-permute-start | bytes 4325384 | tf_op jit(solution)/shard_map/ppermute | solution.py:375
  196.6 115.9 %collective-permute-start.36 = (bf16[256,2816]{1,0:T(8,128)(2,1)S(1)}, bf16[256,2816]{1,0:T(8,128)(2,1)S(1)}, u32[]{:S(2)}, u32[]{:S(2)}) collective-permute-start(bf16[256,2816]{1,0:T(8,128)(2,1)S(1)} %bitcast.198), channel_id=1, source_target_pairs={{0,2},{1,6},{2,3},{3,7},{4,0},{5,4},{6,1},{7,5},{8,10},{9,14},{10,... | collective-permute-start | bytes 4325384 | tf_op jit(solution)/shard_map/ppermute | solution.py:375
  209.6 100.1 %collective-permute-start.52 = (bf16[2,128,2048]{2,1,0:T(8,128)(2,1)S(1)}, bf16[2,128,2048]{2,1,0:T(8,128)(2,1)S(1)}, u32[]{:S(2)}, u32[]{:S(2)}) collective-permute-start(bf16[2,128,2048]{2,1,0:T(8,128)(2,1)S(1)} %copy-done.81), channel_id=1, source_target_pairs={{0,0},{1,4},{2,1},{3,5},{4,2},{5,6},{6,3},{7,7},{8,8},{9,12},{10,9... | collective-permute-start | bytes 3145736 | tf_op jit(solution)/shard_map/ppermute | solution.py:375
  210.9 120.8 %collective-permute-start.26 = (bf16[2,128,2048]{2,1,0:T(8,128)(2,1)S(1)}, bf16[2,128,2048]{2,1,0:T(8,128)(2,1)S(1)}, u32[]{:S(2)}, u32[]{:S(2)}) collective-permute-start(bf16[2,128,2048]{2,1,0:T(8,128)(2,1)S(1)} %slice_bitcast_fusion.14), channel_id=1, source_target_pairs={{0,4},{1,5},{2,6},{3,7},{4,0},{5,1},{6,2},{7,3},{8,12},{9,13},{10,... | collective-permute-start | bytes 3145736 | tf_op jit(solution)/shard_map/ppermute | solution.py:375
  250.4 82.8 %collective-permute-start.28 = (bf16[2,128,2048]{2,1,0:T(8,128)(2,1)S(1)}, bf16[2,128,2048]{2,1,0:T(8,128)(2,1)S(1)}, u32[]{:S(2)}, u32[]{:S(2)}) collective-permute-start(bf16[2,128,2048]{2,1,0:T(8,128)(2,1)S(1)} %fusion.45), channel_id=1, source_target_pairs={{0,1},{1,0},{2,3},{3,2},{4,5},{5,4},{6,7},{7,6},{8,9},{9,8},{10,11... | collective-permute-start | bytes 3145736 | tf_op jit(solution)/shard_map/ppermute | solution.py:375
  326.4 78.8 %collective-permute-start.33 = (bf16[256,2816]{1,0:T(8,128)(2,1)S(1)}, bf16[256,2816]{1,0:T(8,128)(2,1)}, u32[]{:S(2)}, u32[]{:S(2)}) collective-permute-start(bf16[256,2816]{1,0:T(8,128)(2,1)S(1)} %collective-permute-done.32.refs_0_), channel_id=1, source_target_pairs={{0,8},{1,9},{2,10},{3,11},{4,12},{5,13},{6,14},{7,15},{8,0},{9,1},... | collective-permute-start | bytes 4325384 | tf_op jit(solution)/shard_map/ppermute | solution.py:375
  331.1 74.5 %collective-permute-start.37 = (bf16[256,2816]{1,0:T(8,128)(2,1)S(1)}, bf16[256,2816]{1,0:T(8,128)(2,1)}, u32[]{:S(2)}, u32[]{:S(2)}) collective-permute-start(bf16[256,2816]{1,0:T(8,128)(2,1)S(1)} %collective-permute-done.36.refs_4_), channel_id=1, source_target_pairs={{0,16},{1,17},{2,18},{3,19},{4,20},{5,21},{6,22},{7,23},{8,24},{9,... | collective-permute-start | bytes 4325384 | tf_op jit(solution)/shard_map/ppermute | solution.py:375
  333.2 58.8 %collective-permute-start.43 = (bf16[176,2048]{1,0:T(8,128)(2,1)S(1)}, bf16[176,2048]{1,0:T(8,128)(2,1)S(1)}, u32[]{:S(2)}, u32[]{:S(2)}) collective-permute-start(bf16[176,2048]{1,0:T(8,128)(2,1)S(1)} %collective-permute-done.41.refs_1_), channel_id=1, source_target_pairs={{0,16},{1,17},{2,18},{3,19},{4,20},{5,21},{6,22},{7,23},{8,24},{9,... | collective-permute-start | bytes 2162696 | tf_op jit(solution)/shard_map/ppermute | solution.py:375
  345.7 48.2 %collective-permute-start.47 = (bf16[176,2048]{1,0:T(8,128)(2,1)S(1)}, bf16[176,2048]{1,0:T(8,128)(2,1)S(1)}, u32[]{:S(2)}, u32[]{:S(2)}) collective-permute-start(bf16[176,2048]{1,0:T(8,128)(2,1)S(1)} %collective-permute-done.45.refs_5_), channel_id=1, source_target_pairs={{0,8},{1,9},{2,10},{3,11},{4,12},{5,13},{6,14},{7,15},{8,0},{9,1},... | collective-permute-start | bytes 2162696 | tf_op jit(solution)/shard_map/ppermute | solution.py:375
  560.5 80.4 %collective-permute-start.56 = (bf16[2,128,2048]{2,1,0:T(8,128)(2,1)}, bf16[2,128,2048]{2,1,0:T(8,128)(2,1)S(1)}, u32[]{:S(2)}, u32[]{:S(2)}) collective-permute-start(bf16[2,128,2048]{2,1,0:T(8,128)(2,1)} %slice_bitcast_fusion.6), channel_id=1, source_target_pairs={{0,4},{1,5},{2,6},{3,7},{4,0},{5,1},{6,2},{7,3},{8,12},{9,13},{10,... | collective-permute-start | bytes 3145736 | tf_op jit(solution)/shard_map/ppermute | solution.py:375
  628.9 66.1 %collective-permute-start.87 = (bf16[256,2816]{1,0:T(8,128)(2,1)}, bf16[256,2816]{1,0:T(8,128)(2,1)}, u32[]{:S(2)}, u32[]{:S(2)}) collective-permute-start(bf16[256,2816]{1,0:T(8,128)(2,1)} %get-tuple-element.54), channel_id=1, source_target_pairs={{0,16},{1,17},{2,18},{3,19},{4,20},{5,21},{6,22},{7,23},{8,24},{9,... | collective-permute-start | bytes 4325384 | tf_op jit(solution)/shard_map/ppermute | solution.py:375
  640.9 56.4 %collective-permute-start.92 = (bf16[256,2816]{1,0:T(8,128)(2,1)}, bf16[256,2816]{1,0:T(8,128)(2,1)}, u32[]{:S(2)}, u32[]{:S(2)}) collective-permute-start(bf16[256,2816]{1,0:T(8,128)(2,1)} %get-tuple-element.55), channel_id=1, source_target_pairs={{0,8},{1,9},{2,10},{3,11},{4,12},{5,13},{6,14},{7,15},{8,0},{9,1},... | collective-permute-start | bytes 4325384 | tf_op jit(solution)/shard_map/ppermute | solution.py:375
  648.9 72.0 %collective-permute-start.89 = (bf16[256,2816]{1,0:T(8,128)(2,1)}, bf16[256,2816]{1,0:T(8,128)(2,1)}, u32[]{:S(2)}, u32[]{:S(2)}) collective-permute-start(bf16[256,2816]{1,0:T(8,128)(2,1)} %add_convert_fusion.4), channel_id=1, source_target_pairs={{0,8},{1,9},{2,10},{3,11},{4,12},{5,13},{6,14},{7,15},{8,0},{9,1},... | collective-permute-start | bytes 4325384 | tf_op jit(solution)/shard_map/ppermute | solution.py:375
  695.0 59.4 %collective-permute-start.59 = (bf16[2,128,2048]{2,1,0:T(8,128)(2,1)}, bf16[2,128,2048]{2,1,0:T(8,128)(2,1)S(1)}, u32[]{:S(2)}, u32[]{:S(2)}) collective-permute-start(bf16[2,128,2048]{2,1,0:T(8,128)(2,1)} %get-tuple-element.46), channel_id=1, source_target_pairs={{0,4},{1,5},{2,6},{3,7},{4,0},{5,1},{6,2},{7,3},{8,12},{9,13},{10,... | collective-permute-start | bytes 3145736 | tf_op jit(solution)/shard_map/ppermute | solution.py:375
  697.3 57.0 %collective-permute-start.51 = (bf16[2,128,2048]{2,1,0:T(8,128)(2,1)S(1)}, bf16[2,128,2048]{2,1,0:T(8,128)(2,1)S(1)}, u32[]{:S(2)}, u32[]{:S(2)}) collective-permute-start(bf16[2,128,2048]{2,1,0:T(8,128)(2,1)S(1)} %copy-done.67), channel_id=1, source_target_pairs={{0,0},{1,2},{2,4},{3,6},{4,1},{5,3},{6,5},{7,7},{8,8},{9,10},{10,1... | collective-permute-start | bytes 3145736 | tf_op jit(solution)/shard_map/ppermute | solution.py:375
  733.2 108.7 %collective-permute-start.91 = (bf16[256,2816]{1,0:T(8,128)(2,1)}, bf16[256,2816]{1,0:T(8,128)(2,1)}, u32[]{:S(2)}, u32[]{:S(2)}) collective-permute-start(bf16[256,2816]{1,0:T(8,128)(2,1)} %get-tuple-element.56), channel_id=1, source_target_pairs={{0,8},{1,9},{2,10},{3,11},{4,12},{5,13},{6,14},{7,15},{8,0},{9,1},... | collective-permute-start | bytes 4325384 | tf_op jit(solution)/shard_map/ppermute | solution.py:375
  751.4 92.1 %collective-permute-start.93 = (bf16[256,2816]{1,0:T(8,128)(2,1)}, bf16[256,2816]{1,0:T(8,128)(2,1)}, u32[]{:S(2)}, u32[]{:S(2)}) collective-permute-start(bf16[256,2816]{1,0:T(8,128)(2,1)} %get-tuple-element.53), channel_id=1, source_target_pairs={{0,16},{1,17},{2,18},{3,19},{4,20},{5,21},{6,22},{7,23},{8,24},{9,... | collective-permute-start | bytes 4325384 | tf_op jit(solution)/shard_map/ppermute | solution.py:375
  873.8 94.7 %collective-permute-start.90 = (bf16[256,2816]{1,0:T(8,128)(2,1)S(1)}, bf16[256,2816]{1,0:T(8,128)(2,1)S(1)}, u32[]{:S(2)}, u32[]{:S(2)}) collective-permute-start(bf16[256,2816]{1,0:T(8,128)(2,1)S(1)} %copy-done.61), channel_id=1, source_target_pairs={{0,0},{1,2},{2,4},{3,6},{4,1},{5,3},{6,5},{7,7},{8,8},{9,10},{10,1... | collective-permute-start | bytes 4325384 | tf_op jit(solution)/shard_map/ppermute | solution.py:375
  886.5 70.7 %collective-permute-start.75 = (bf16[256,1536]{1,0:T(8,128)(2,1)S(1)}, bf16[256,1536]{1,0:T(8,128)(2,1)S(1)}, u32[]{:S(2)}, u32[]{:S(2)}) collective-permute-start(bf16[256,1536]{1,0:T(8,128)(2,1)S(1)} %get-tuple-element.63), channel_id=1, source_target_pairs={{0,8},{1,9},{2,10},{3,11},{4,12},{5,13},{6,14},{7,15},{8,0},{9,1},... | collective-permute-start | bytes 2359304 | tf_op jit(solution)/shard_map/ppermute | solution.py:375
  888.1 80.3 %collective-permute-start.94 = (bf16[256,2816]{1,0:T(8,128)(2,1)S(1)}, bf16[256,2816]{1,0:T(8,128)(2,1)S(1)}, u32[]{:S(2)}, u32[]{:S(2)}) collective-permute-start(bf16[256,2816]{1,0:T(8,128)(2,1)S(1)} %add_convert_fusion), channel_id=1, source_target_pairs={{0,4},{1,6},{2,0},{3,2},{4,5},{5,7},{6,1},{7,3},{8,12},{9,14},{10,... | collective-permute-start | bytes 4325384 | tf_op jit(solution)/shard_map/ppermute | solution.py:375
  902.6 64.1 %collective-permute-start.77 = (bf16[256,1536]{1,0:T(8,128)(2,1)S(1)}, bf16[256,1536]{1,0:T(8,128)(2,1)S(1)}, u32[]{:S(2)}, u32[]{:S(2)}) collective-permute-start(bf16[256,1536]{1,0:T(8,128)(2,1)S(1)} %get-tuple-element.60), channel_id=1, source_target_pairs={{0,16},{1,17},{2,18},{3,19},{4,20},{5,21},{6,22},{7,23},{8,24},{9,... | collective-permute-start | bytes 2359304 | tf_op jit(solution)/shard_map/ppermute | solution.py:375
  (175 other events, 3886.7 us)

commit v2 on v1

--- a/solution.py
+++ b/solution.py
@@ -242,6 +242,7 @@
         compiler_params=pltpu.CompilerParams(
             dimension_semantics=("arbitrary",), vmem_limit_bytes=32 * 1024 * 1024
         ),
+        cost_estimate=pl.CostEstimate(flops=1, bytes_accessed=1, transcendentals=0),
         name="recur_forward",
     )(own, proj, bound, gain)
 
@@ -286,6 +287,7 @@
         compiler_params=pltpu.CompilerParams(
             dimension_semantics=("arbitrary",), vmem_limit_bytes=32 * 1024 * 1024
         ),
+        cost_estimate=pl.CostEstimate(flops=1, bytes_accessed=1, transcendentals=0),
         name="recur_backward",
     )(own, proj, mixed, out_head, states, bound, gain)
 
@@ -304,53 +306,12 @@
     )
 
 
-def assemble_body(count, at_ref, *refs):
-    pieces, out_ref, held, in_sems, out_sems = refs[:count], refs[count], *refs[count + 1 :]
-    rows = pieces[0].shape[0]
-    loads = [pltpu.make_async_copy(pieces[i], held.at[i], in_sems.at[i]) for i in range(count)]
-    for load in loads:
-        load.start()
-    stores = []
-    for i in range(count):
-        start = pl.multiple_of(at_ref[i] * rows, rows)
-        loads[i].wait()
-        stores.append(
-            pltpu.make_async_copy(held.at[i], out_ref.at[pl.ds(start, rows), :], out_sems.at[i])
-        )
-        stores[i].start()
-    for store in stores:
-        store.wait()
-
-
-def assemble(at, pieces):
-    count = len(pieces)
-    rows, cols = pieces[0].shape
-    if rows % 16:
-        whole = jnp.zeros((count * rows, cols), pieces[0].dtype)
-        for i, piece in enumerate(pieces):
-            whole = lax.dynamic_update_slice_in_dim(whole, piece, at[i] * rows, 0)
-        return whole
-    return pl.pallas_call(
-        functools.partial(assemble_body, count),
-        in_specs=[pl.BlockSpec(memory_space=pltpu.SMEM)] + [pl.BlockSpec(memory_space=pl.ANY)] * count,
-        out_specs=pl.BlockSpec(memory_space=pl.ANY),
-        out_shape=jax.ShapeDtypeStruct((count * rows, cols), pieces[0].dtype),
-        scratch_shapes=[
-            pltpu.VMEM((count, rows, cols), pieces[0].dtype),
-            pltpu.SemaphoreType.DMA((count,)),
-            pltpu.SemaphoreType.DMA((count,)),
-        ],
-        compiler_params=pltpu.CompilerParams(vmem_limit_bytes=32 * 1024 * 1024),
-        name="assemble",
-    )(at, *pieces)
-
-
 AXES = ("dp", "tensor")
 
 
 def make_local(dp_size, tensor_size):
     columns = dp_size // 2
-    bits = [1 << i for i in range(columns.bit_length() - 1)]
+    groups = [[2 * col + core for col in range(columns)] for core in range(2)]
 
     def route(step, invert=False):
         pairs = []
@@ -368,54 +329,58 @@
     returns = [route(spread(flip), True) for flip in (0, 1)]
     core_swap = route(lambda col, core, z: (col, core ^ 1, z))
     z_swap = route(lambda col, core, z: (col, core, z ^ 1))
-    col_swap = {bit: route(lambda col, core, z, bit=bit: (col ^ bit, core, z)) for bit in bits}
-    orders = [bits, bits[::-1]]
 
     def move(array, pairs):
         return lax.ppermute(array, AXES, pairs)
 
-    def sum_all(array):
+    def sum_steps(array, steps):
         total = dp_size * tensor_size
-        for step in range(total.bit_length() - 1):
+        for step in steps:
             array = array + move(array, [(at, at ^ (1 << step)) for at in range(total)])
         return array
 
-    def gather_weight(shard, places):
-        pieces = []
-        spots = []
-        for half in range(2):
-            held = [(0, move(shard, spreads[half]))]
-            for bit in orders[half]:
-                held = held + [(at ^ bit, move(piece, col_swap[bit])) for at, piece in held]
-            for at, piece in held:
-                pieces.append(piece)
-                spots.append(places(at, half))
-        return assemble(jnp.stack(spots).astype(jnp.int32), pieces)
-
-    def scatter_grad(piece_of):
-        total = None
-        for half in range(2):
-            held = {at: piece_of(at, half) for at in range(columns)}
-            for bit in orders[half][::-1]:
-                for at in sorted(held):
-                    if at & bit:
-                        arrived = move(held.pop(at), col_swap[bit])
-                        held[at ^ bit] = (
-                            held[at ^ bit].astype(F32) + arrived.astype(F32)
-                        ).astype(BF)
-            back = move(held[0], returns[half]).astype(F32)
-            total = back if total is None else total + back
-        return total
+    low_steps = range(tensor_size.bit_length() - 1)
+    high_steps = range(tensor_size.bit_length() - 1, (dp_size * tensor_size).bit_length() - 1)
+
+    def after(array, *earlier):
+        return lax.optimization_barrier((array, *earlier))[0]
+
+    def ordered(first, second, swap):
+        return jnp.where(swap, second, first), jnp.where(swap, first, second)
+
+    def spread_weight(shard):
+        return move(shard, spreads[0]), move(shard, spreads[1])
+
+    def joined(pair, swap):
+        return jnp.concatenate(ordered(*pair, swap), axis=0)
+
+    def gather_weight(pair):
+        return lax.all_gather(pair, "dp", axis=0, tiled=True, axis_index_groups=groups)
+
+    def scatter_grad(whole):
+        return lax.psum_scatter(
+            whole, "dp", scatter_dimension=0, tiled=True, axis_index_groups=groups
+        )
+
+    def return_grad(pair, swap):
+        rows = pair.shape[0] // 2
+        first, second = ordered(pair[:rows], pair[rows:], swap)
+        return move(first, returns[0]).astype(F32) + move(second, returns[1]).astype(F32)
 
     def gather_rows(own):
         near = move(own, core_swap)
         far = move(own, z_swap)
         return jnp.stack([own, near, far, move(far, core_swap)])
 
+    def scatter_far(far_pair):
+        return (far_pair[0].astype(F32) + move(far_pair[1], core_swap).astype(F32)).astype(BF)
+
+    def scatter_own(far, own_pair):
+        near = own_pair[0].astype(F32) + move(own_pair[1], core_swap).astype(F32)
+        return near + move(far, z_swap).astype(F32)
+
     def scatter_rows(far_pair, own_pair):
-        far = far_pair[0].astype(F32) + move(far_pair[1], core_swap).astype(F32)
-        far = move(far.astype(BF), z_swap)
-        return own_pair[0].astype(F32) + move(own_pair[1], core_swap).astype(F32) + far.astype(F32)
+        return scatter_own(scatter_far(far_pair), own_pair)
 
     def split_rows(compute, *arrays):
         half = arrays[0].shape[0] // 2
@@ -445,76 +410,8 @@
         seqs, rows, model = tokens.shape
         dp_at = lax.axis_index("dp")
         z_at = lax.axis_index("tensor")
-        col = dp_at // 2
         half_at = z_at // 2
         role = 2 * (z_at % 2) + dp_at % 2
-
-        def places(at, half):
-            return lax.bitwise_xor(col, at) * 2 + (half_at if half == 0 else 1 - half_at)
-
-        lens = move(lengths, spreads[0])
-        tok = move(tokens, spreads[0])
-        mixer_mat = gather_weight(mixer_in.reshape(mixer_in.shape[0], -1), places)
-        merge_mat = gather_weight(head_merge, places)
-        gates_mat = gather_weight(gate_up.reshape(gate_up.shape[0], -1), places)
-        down_mat = gather_weight(down_weight, places)
-        out_rows = move(out_grad, spreads[0])
-
-        vectors = [norm_gain, feed_gain, head_gain, lower_bound]
-        vector_ends = np.cumsum([vector.shape[0] for vector in vectors])
-        packed = jnp.zeros((dp_size * tensor_size, vector_ends[-1]), BF)
-        packed = lax.dynamic_update_slice_in_dim(
-            packed, jnp.concatenate(vectors)[None], dp_at * tensor_size + z_at, 0
-        )
-        packed = sum_all(packed).reshape(dp_size, tensor_size, -1).astype(F32)
-        norm_vec = packed[:, 0, : vector_ends[0]].reshape(-1)
-        feed_vec = packed[:, 0, vector_ends[0] : vector_ends[1]].reshape(-1)
-        head_vec = packed[:, 0, vector_ends[1] : vector_ends[2]].reshape(1, -1)
-        bound_vec = lax.dynamic_index_in_dim(packed, role, 1, False)[:, vector_ends[2] :].reshape(1, -1)
-
-        positions = role * rows + jnp.arange(rows, dtype=jnp.int32)
-        valid = (positions[None, :] < lens[:, None]).astype(F32)[:, :, None]
-        own = role.astype(jnp.int32).reshape(1)
-
-        masked = tok.astype(F32) * valid
-        normed, scale_one = rms_rows(masked, norm_vec)
-        first_in = gather_rows(normed.astype(BF))
-        projected = dot_rows(first_in, mixer_mat, 0)
-        mixed, head_out, states = recur_forward(own, projected, bound_vec, head_vec)
-        attn = scatter_rows(*split_rows(lambda part: dot_rows(part, merge_mat, 0).astype(BF), head_out))
-        middle = masked + attn
-        normed_two, scale_two = rms_rows(middle, feed_vec)
-        second_in = gather_rows(normed_two.astype(BF))
-        gate_pre = dot_rows(second_in, gates_mat, 0)
-        hidden_cols = down_mat.shape[0]
-        gate_part = gate_pre[..., :hidden_cols]
-        up_part = gate_pre[..., hidden_cols:]
-        sig_gate = jax.nn.sigmoid(gate_part)
-        hidden = (gate_part * sig_gate * up_part).astype(BF)
-        feed_out = scatter_rows(*split_rows(lambda part: dot_rows(part, down_mat, 0).astype(BF), hidden))
-        block_out = move((valid * (middle + feed_out)).astype(BF), returns[0])
-
-        upstream = out_rows.astype(F32) * valid
-        branch_in = gather_rows(upstream.astype(BF))
-        hidden_grad = dot_rows(branch_in, down_mat, 1)
-        gate_grad = hidden_grad * up_part * sig_gate * (1.0 + gate_part * (1.0 - sig_gate))
-        up_grad = hidden_grad * gate_part * sig_gate
-        both_grad = jnp.concatenate([gate_grad, up_grad], axis=-1).astype(BF)
-        second_grad = scatter_rows(
-            *split_rows(lambda part: dot_rows(part, gates_mat, 1).astype(BF), both_grad)
-        )
-        middle_grad, feed_terms = norm_back(middle, scale_two, feed_vec, second_grad)
-        middle_grad = middle_grad + upstream
-        attn_in = gather_rows(middle_grad.astype(BF))
-        out_head = dot_rows(attn_in, merge_mat, 1)
-        proj_grad, bound_sum, head_sum = recur_backward(
-            own, projected, mixed, out_head, states, bound_vec, head_vec
-        )
-        first_grad = scatter_rows(
-            *split_rows(lambda part: dot_rows(part, mixer_mat, 1).astype(BF), proj_grad)
-        )
-        masked_grad, norm_terms = norm_back(masked, scale_one, norm_vec, first_grad)
-        input_grad = move((valid * (masked_grad + middle_grad)).astype(BF), returns[0])
 
         def weight_grad(first_mat, second_mat):
             return lax.dot_general(
@@ -524,13 +421,91 @@
                 preferred_element_type=F32,
             ).astype(BF)
 
-        def by_rows(whole, count):
-            return lambda at, half: lax.dynamic_slice_in_dim(whole, places(at, half) * count, count, 0)
-
-        down_grad = scatter_grad(by_rows(weight_grad(hidden, branch_in), down_weight.shape[0]))
-        gates_grad = scatter_grad(by_rows(weight_grad(second_in, both_grad), gate_up.shape[0]))
-        merge_grad = scatter_grad(by_rows(weight_grad(head_out, attn_in), head_merge.shape[0]))
-        mixer_grad = scatter_grad(by_rows(weight_grad(first_in, proj_grad), mixer_in.shape[0]))
+        swap = half_at == 1
+        lens = move(lengths, spreads[0])
+        mixer_pair = spread_weight(mixer_in.reshape(mixer_in.shape[0], -1))
+        vectors = [norm_gain, feed_gain, head_gain, lower_bound]
+        vector_ends = np.cumsum([vector.shape[0] for vector in vectors])
+        packed = jnp.zeros((dp_size, vector_ends[-1]), BF)
+        packed = lax.dynamic_update_slice_in_dim(packed, jnp.concatenate(vectors)[None], dp_at, 0)
+        packed = sum_steps(packed, high_steps)
+        tok = move(after(tokens, packed), spreads[0])
+        merge_pair = spread_weight(after(head_merge, tok))
+
+        bounds = jnp.zeros((tensor_size, dp_size, lower_bound.shape[0]), BF)
+        bounds = lax.dynamic_update_slice_in_dim(bounds, packed[None, :, vector_ends[2] :], z_at, 0)
+        bounds = sum_steps(bounds, low_steps)
+        vector_rows = packed.astype(F32)
+        norm_vec = vector_rows[:, : vector_ends[0]].reshape(-1)
+        feed_vec = vector_rows[:, vector_ends[0] : vector_ends[1]].reshape(-1)
+        head_vec = vector_rows[:, vector_ends[1] : vector_ends[2]].reshape(1, -1)
+        bound_vec = lax.dynamic_index_in_dim(bounds, role, 0, False).astype(F32).reshape(1, -1)
+
+        positions = role * rows + jnp.arange(rows, dtype=jnp.int32)
+        valid = (positions[None, :] < lens[:, None]).astype(F32)[:, :, None]
+        own = role.astype(jnp.int32).reshape(1)
+
+        masked = tok.astype(F32) * valid
+        normed, scale_one = rms_rows(masked, norm_vec)
+        normed = normed.astype(BF)
+        gates_pair = spread_weight(after(gate_up.reshape(gate_up.shape[0], -1), normed, *merge_pair))
+        down_pair = spread_weight(after(down_weight, *gates_pair))
+        out_rows = move(after(out_grad, *down_pair), spreads[0])
+        mixer_mat = gather_weight(joined(mixer_pair, swap))
+        merge_mat = gather_weight(joined(merge_pair, swap))
+        first_in = gather_rows(normed)
+        gates_mat = gather_weight(joined([after(part, first_in) for part in gates_pair], swap))
+        down_mat = gather_weight(joined(down_pair, swap))
+        projected = dot_rows(first_in, mixer_mat, 0)
+        mixed, head_out, states = recur_forward(own, projected, bound_vec, head_vec)
+        attn = scatter_rows(*split_rows(lambda part: dot_rows(part, merge_mat, 0).astype(BF), head_out))
+        middle = masked + attn
+        normed_two, scale_two = rms_rows(middle, feed_vec)
+        upstream = out_rows.astype(F32) * valid
+        branch_in = gather_rows(upstream.astype(BF))
+        second_in = after(gather_rows(normed_two.astype(BF)), branch_in)
+        gate_pre = dot_rows(second_in, gates_mat, 0)
+        hidden_cols = down_mat.shape[0]
+        gate_part = gate_pre[..., :hidden_cols]
+        up_part = gate_pre[..., hidden_cols:]
+        sig_gate = jax.nn.sigmoid(gate_part)
+        hidden = (gate_part * sig_gate * up_part).astype(BF)
+        down_whole = weight_grad(hidden, branch_in)
+        down_pair = scatter_grad(down_whole)
+        down_grad = return_grad(down_pair, swap)
+        hidden_grad = dot_rows(after(branch_in, down_whole), down_mat, 1)
+        gate_grad = hidden_grad * up_part * sig_gate * (1.0 + gate_part * (1.0 - sig_gate))
+        up_grad = hidden_grad * gate_part * sig_gate
+        both_grad = jnp.concatenate([gate_grad, up_grad], axis=-1).astype(BF)
+        second_parts = split_rows(lambda part: dot_rows(part, gates_mat, 1).astype(BF), both_grad)
+        second_far = scatter_far(second_parts[0])
+        second_grad = scatter_own(second_far, second_parts[1])
+        gates_whole = weight_grad(second_in, after(both_grad, second_far, *second_parts))
+        second_grad = after(second_grad, gates_whole)
+        middle_grad, feed_terms = norm_back(middle, scale_two, feed_vec, second_grad)
+        middle_grad = middle_grad + upstream
+        feed_parts = split_rows(lambda part: dot_rows(part, down_mat, 0).astype(BF), hidden)
+        attn_in = after(gather_rows(middle_grad.astype(BF)), *feed_parts)
+        feed_out = scatter_rows(*feed_parts)
+        block_out = move((valid * (middle + feed_out)).astype(BF), returns[0])
+        out_head = dot_rows(after(attn_in, down_grad), merge_mat, 1)
+        proj_grad, bound_sum, head_sum = recur_backward(
+            own, projected, mixed, out_head, states, bound_vec, head_vec
+        )
+        first_parts = split_rows(lambda part: dot_rows(part, mixer_mat, 1).astype(BF), proj_grad)
+        first_grad = scatter_rows(*first_parts)
+        merge_whole = weight_grad(head_out, attn_in)
+        mixer_whole = weight_grad(first_in, proj_grad)
+        first_grad = after(first_grad, merge_whole, mixer_whole)
+        masked_grad, norm_terms = norm_back(masked, scale_one, norm_vec, first_grad)
+        input_grad = move((valid * (masked_grad + middle_grad)).astype(BF), returns[0])
+
+        gates_pair = scatter_grad(after(gates_whole, down_pair))
+        mixer_pair = scatter_grad(after(mixer_whole, gates_pair, *first_parts))
+        merge_pair = scatter_grad(after(merge_whole, mixer_pair))
+        gates_grad = return_grad(gates_pair, swap)
+        merge_grad = return_grad(merge_pair, swap)
+        mixer_grad = return_grad(mixer_pair, swap)
 
         bound_all = jnp.zeros((tensor_size, bound_sum.shape[1]), F32)
         bound_all = lax.dynamic_update_slice_in_dim(bound_all, bound_sum, role, 0)
@@ -541,7 +516,7 @@
             bound_all.reshape(-1),
         ]
         ends = np.cumsum([part.shape[0] for part in sums])
-        summed = sum_all(jnp.concatenate(sums))
+        summed = sum_steps(after(jnp.concatenate(sums), down_grad, gates_grad), [*low_steps, *high_steps])
 
         def shard_of(vector, count, at):
             return lax.dynamic_slice_in_dim(vector, at * count, count, 0)

time: 1030 us -> 823 us (0.80)
  starting transfers between devices: 298 us -> 157 us
  waiting for transfers between devices: 410 us -> 380 us
  local copies, waits for them, and re-layouts: 59.1 us -> 34 us
  Pallas kernels: 68.9 us -> 52.2 us
  matrix products: 141 us -> 125 us
  between operations: 2.17 us -> 15.7 us
    ppermute x103 -> x55, starting transfers between devices: 298 us -> 155 us  [move(): return lax.ppermute(array, AXES, pairs)]
    ppermute x103 -> x55, waiting for transfers between devices: 410 us -> 311 us  [move(): return lax.ppermute(array, AXES, pairs)]
    reduce_scatter x0 -> x4, waiting for transfers between devices: none -> 69.3 us  [scatter_grad(): lax.psum_scatter(whole, 'dp', scatter_dimension=0, tiled=True, axis_index...]
    convert_element_type x20 -> x10, other arithmetic: 27.5 us -> 10.4 us  [the longest x4 4.73 us: scatter_far(): (far_pair[0].astype(F32) + move(far_pair[1], core_swap).astype(F32)).asty...]
    pallas_call x4 -> x0, Pallas kernels: 16.6 us -> none  [assemble(): pl.pallas_call(functools.partial(assemble_body, count), in_specs=[pl.Bloc...]
    unnamed x199 -> x143, local copies, waits for them, and re-layouts: 37.8 us -> 21.3 us
  transfers between devices with their start and end apart: 103 -> 63, of which waited for: 39 -> 26; matrix products, arithmetic and copies ran while one was open for 11% -> 23% of each run, Pallas kernels for 5% -> 6%
where the time goes in v2:
time: 823 us; the launch traced here: 812 us
  waiting for transfers between devices  380 us (46%)
  starting transfers between devices  157 us (19%)
  matrix products  125 us (15%)
  Pallas kernels  52.2 us (6%)
  other arithmetic  48.1 us (6%)
  local copies, waits for them, and re-layouts  34 us (4%)
  between operations  15.7 us (2%)
    ppermute x55, waiting for transfers between devices, move(): return lax.ppermute(array, AXES, pairs)  311 us
    ppermute x55, starting transfers between devices, move(): return lax.ppermute(array, AXES, pairs)  155 us
    dot_general x12, matrix products, dot_rows(): lax.dot_general(first_mat, second_mat, (((first_mat.ndim - 1,), (second_d...  87.3 us
    reduce_scatter x4, waiting for transfers between devices, scatter_grad(): lax.psum_scatter(whole, 'dp', scatter_dimension=0, tiled=True, axis_index...  69.3 us
    dot_general x4, matrix products, weight_grad(): lax.dot_general(first_mat.reshape(-1, first_mat.shape[-1]), second_mat.re...  37.4 us
    pallas_call x1, Pallas kernels, recur_backward(): pl.pallas_call(backward_body, grid_spec=pltpu.PrefetchScalarGridSpec(num_...  31.3 us
    unnamed x143, local copies, waits for them, and re-layouts  21.3 us
    pallas_call x1, Pallas kernels, recur_forward(): pl.pallas_call(forward_body, grid_spec=pltpu.PrefetchScalarGridSpec(num_s...  20.9 us
  transfers between devices with their start and end apart: 63, of which 26 were waited for; matrix products, arithmetic and copies ran while one was open for 23% of the time, Pallas kernels for 6%

profile of v2, /device:TPU:0, one launch (start us, length us, event | category | flops | bytes accessed | tf_op | source)
XLA Modules:
  0.0 811.9 jit_solution(14514771091839126984)
XLA Ops:
  13.7 14.4 %collective-permute-done.8 = bf16[256,1536]{1,0:T(8,128)(2,1)S(1)} collective-permute-done((bf16[256,1536]{1,0:T(8,128)(2,1)S(1)}, bf16[256,1536]{1,0:T(8,128)(2,1)S(1)}, u32[]{:S(2)}, u32[]{:S(2)}) %collective-permute-start.8) | collective-permute-done | bytes 786464 | tf_op jit(solution)/shard_map/ppermute | solution.py:334
  43.9 41.9 %collective-permute-start.12 = (bf16[64,2048]{1,0:T(8,128)(2,1)}, bf16[64,2048]{1,0:T(8,128)(2,1)S(1)}, u32[]{:S(2)}, u32[]{:S(2)}) collective-permute-start(bf16[64,2048]{1,0:T(8,128)(2,1)} %param.17), channel_id=1, source_target_pairs={{0,2},{1,6},{2,3},{3,7},{4,0},{5,4},{6,1},{7,5},{8,10},{9,14},{10,... | collective-permute-start | bytes 786440 | tf_op jit(solution)/shard_map/ppermute | solution.py:334
  101.5 14.7 %collective-permute-done.6 = bf16[2,128,2048]{2,1,0:T(8,128)(2,1)} collective-permute-done((bf16[2,128,2048]{2,1,0:T(8,128)(2,1)S(1)}, bf16[2,128,2048]{2,1,0:T(8,128)(2,1)}, u32[]{:S(2)}, u32[]{:S(2)}) %collective-permute-start.6) | collective-permute-done | bytes 1048608 | tf_op jit(solution)/shard_map/ppermute | solution.py:334
  119.1 25.7 %collective-permute-done.21 = bf16[256,2816]{1,0:T(8,128)(2,1)S(1)} collective-permute-done((bf16[256,2816]{1,0:T(8,128)(2,1)S(1)}, bf16[256,2816]{1,0:T(8,128)(2,1)S(1)}, u32[]{:S(2)}, u32[]{:S(2)}) %collective-permute-start.21) | collective-permute-done | bytes 1441824 | tf_op jit(solution)/shard_map/ppermute | solution.py:334
  147.6 21.1 %collective-permute-start.10 = (bf16[4,8,64]{2,1,0:T(8,128)(2,1)S(1)}, bf16[4,8,64]{2,1,0:T(8,128)(2,1)S(1)}, u32[]{:S(2)}, u32[]{:S(2)}) collective-permute-start(bf16[4,8,64]{2,1,0:T(8,128)(2,1)S(1)} %fusion.54), channel_id=1, source_target_pairs={{0,1},{1,0},{2,3},{3,2},{4,5},{5,4},{6,7},{7,6},{8,9},{9,8},{10,11... | collective-permute-start | bytes 12296 | tf_op jit(solution)/shard_map/ppermute | solution.py:334
  191.3 20.9 %recur_forward.1 = (f32[4,2,128,512]{3,2,1,0:T(8,128)S(1)}, bf16[4,2,128,512]{3,2,1,0:T(8,128)(2,1)S(1)}, bf16[16,8,128,128]{3,2,1,0:T(8,128)(2,1)S(1)}) custom-call(s32[1]{0:T(128)} %bitcast.own_ref, f32[4,2,128,1536]{3,2,1,0:T(8,128)S(1)} %fusion.10.proj_ref, f32[1,512]{1,0:T(1,128)S(1)} %reshape.160.bound_ref, f32[1,128]{1,0:T(1,128)S(1)} %reshape.154.gain_ref), custom_call_target="tpu_custom_call" | custom-call | flops 1 | bytes 1 | tf_op jit(solution)/shard_map/recur_forward/pallas_call | solution.py:220
  237.9 22.9 %collective-permute-done.16 = bf16[2,128,2048]{2,1,0:T(8,128)(2,1)} collective-permute-done((bf16[2,128,2048]{2,1,0:T(8,128)(2,1)}, bf16[2,128,2048]{2,1,0:T(8,128)(2,1)}, u32[]{:S(2)}, u32[]{:S(2)}) %collective-permute-start.16) | collective-permute-done | bytes 1048608 | tf_op jit(solution)/shard_map/ppermute | solution.py:334
  266.4 23.7 %collective-permute-done.26 = bf16[2,128,2048]{2,1,0:T(8,128)(2,1)S(1)} collective-permute-done((bf16[2,128,2048]{2,1,0:T(8,128)(2,1)S(1)}, bf16[2,128,2048]{2,1,0:T(8,128)(2,1)S(1)}, u32[]{:S(2)}, u32[]{:S(2)}) %collective-permute-start.26) | collective-permute-done | bytes 1048608 | tf_op jit(solution)/shard_map/ppermute | solution.py:334
  290.6 20.7 %collective-permute-done.18 = bf16[2,128,2048]{2,1,0:T(8,128)(2,1)S(1)} collective-permute-done((bf16[2,128,2048]{2,1,0:T(8,128)(2,1)S(1)}, bf16[2,128,2048]{2,1,0:T(8,128)(2,1)S(1)}, u32[]{:S(2)}, u32[]{:S(2)}) %collective-permute-start.18) | collective-permute-done | bytes 1048608 | tf_op jit(solution)/shard_map/ppermute | solution.py:334
  316.9 17.2 %fusion.4 = f32[4,2,128,2816]{3,2,1,0:T(8,128)S(1)} fusion(bf16[4,2,128,2048]{3,2,1,0:T(8,128)(2,1)} %pad_maximum_fusion.2, bf16[2048,2816]{1,0:T(8,128)(2,1)} %all-gather.9.cloned.1.call-done), kind=kOutput, calls=%fused_computation.7 | convolution fusion | flops 11811160064 | bytes 27262976 | tf_op jit(solution)/shard_map/dot_general | solution.py:390
  349.3 13.3 %multiply_convert_fusion.1 = (bf16[4,2,128,1408]{3,2,1,0:T(8,128)(2,1)S(1)}, bf16[4,2,128,1408]{3,2,1,0:T(8,128)(2,1)S(1)}) fusion(f32[4,2,128,2816]{3,2,1,0:T(8,128)} %copy-done.13, bf16[4,2,128,2048]{3,2,1,0:T(8,128)(2,1)} %pad_maximum_fusion.3, bf16[1408,2048]{1,0:T(8,128)(2,1)} %all-gather.11.cloned.1.call-done), kind=kOutput, calls=%fused_computation.23 | convolution fusion | flops 5924323328 | bytes 27262976 | tf_op jit(solution)/shard_map/dot_general | solution.py:390
  362.6 11.3 %fusion.21 = bf16[2,2,128,2048]{3,2,1,0:T(8,128)(2,1)S(1)} fusion(bf16[2048,2816]{1,0:T(8,128)(2,1)} %all-gather.9.cloned.1.call-done, bf16[4,2,128,1408]{3,2,1,0:T(8,128)(2,1)S(1)} %get-tuple-element.87, bf16[4,2,128,1408]{3,2,1,0:T(8,128)(2,1)S(1)} %get-tuple-element.86), kind=kOutput, calls=%fused_computation.32 | convolution fusion | flops 5918162944 | bytes 19398656 | tf_op jit(solution)/shard_map/dot_general | solution.py:390
  374.4 10.0 %fusion.18 = bf16[2,2,128,2048]{3,2,1,0:T(8,128)(2,1)} fusion(bf16[2048,2816]{1,0:T(8,128)(2,1)} %all-gather.9.cloned.1.call-done, bf16[4,2,128,1408]{3,2,1,0:T(8,128)(2,1)S(1)} %get-tuple-element.87, bf16[4,2,128,1408]{3,2,1,0:T(8,128)(2,1)S(1)} %get-tuple-element.86), kind=kOutput, calls=%fused_computation.31 | convolution fusion | flops 5918162944 | bytes 19398656 | tf_op jit(solution)/shard_map/dot_general | solution.py:390
  389.5 15.2 %bitcast_convert_fusion = bf16[2048,2816]{1,0:T(8,128)(2,1)} fusion(bf16[4,2,128,2048]{3,2,1,0:T(8,128)(2,1)S(1)} %copy-done.16, bf16[4,2,128,2816]{3,2,1,0:T(8,128)(2,1)S(1)} %pad_maximum_fusion), kind=kOutput, calls=%fused_computation | convolution fusion | flops 11816927232 | bytes 21495808 | tf_op jit(solution)/shard_map/dot_general | solution.py:417
  404.7 12.8 %reduce-scatter.5.cloned.1.call-done = bf16[352,2048]{1,0:T(8,128)(2,1)} async-done(((bf16[1408,2048]{1,0:T(8,128)(2,1)}), bf16[352,2048]{1,0:T(8,128)(2,1)}) %reduce-scatter.5.cloned.1.call-update) | async-done | bytes 1441808 | tf_op jit(solution)/shard_map/reduce_scatter | solution.py:361
  421.9 22.9 %collective-permute-done.34 = bf16[2,128,2048]{2,1,0:T(8,128)(2,1)S(1)} collective-permute-done((bf16[2,128,2048]{2,1,0:T(8,128)(2,1)S(1)}, bf16[2,128,2048]{2,1,0:T(8,128)(2,1)S(1)}, u32[]{:S(2)}, u32[]{:S(2)}) %collective-permute-start.34) | collective-permute-done | bytes 1048608 | tf_op jit(solution)/shard_map/ppermute | solution.py:334
  455.7 18.6 %collective-permute-done.36 = bf16[2,128,2048]{2,1,0:T(8,128)(2,1)S(1)} collective-permute-done((bf16[2,128,2048]{2,1,0:T(8,128)(2,1)S(1)}, bf16[2,128,2048]{2,1,0:T(8,128)(2,1)S(1)}, u32[]{:S(2)}, u32[]{:S(2)}) %collective-permute-start.36) | collective-permute-done | bytes 1048608 | tf_op jit(solution)/shard_map/ppermute | solution.py:334
  483.3 27.9 %collective-permute-done.39 = bf16[176,2048]{1,0:T(8,128)(2,1)S(1)} collective-permute-done((bf16[176,2048]{1,0:T(8,128)(2,1)S(1)}, bf16[176,2048]{1,0:T(8,128)(2,1)S(1)}, u32[]{:S(2)}, u32[]{:S(2)}) %collective-permute-start.39) | collective-permute-done | bytes 720928 | tf_op jit(solution)/shard_map/ppermute | solution.py:334
  516.4 31.3 %recur_backward.1 = (bf16[4,2,128,1536]{3,2,1,0:T(8,128)(2,1)S(1)}, f32[1,512]{1,0:T(1,128)S(1)}, f32[1,128]{1,0:T(1,128)S(1)}) custom-call(s32[1]{0:T(128)} %bitcast.own_ref, f32[4,2,128,1536]{3,2,1,0:T(8,128)S(1)} %bitcast.177, f32[4,2,128,512]{3,2,1,0:T(8,128)S(1)} %get-tuple-element.43.mixed_ref, f32[4,2,128,512]{3,2,1,0:T(8,128)S(1)} %fusion.48.out_ref, ...), custom_call_target="tpu_custom_call" | custom-call | flops 1 | bytes 1 | tf_op jit(solution)/shard_map/recur_backward/pallas_call | solution.py:262
  557.1 10.3 %bitcast_convert_fusion.1 = bf16[2048,1536]{1,0:T(8,128)(2,1)} fusion(bf16[4,2,128,1536]{3,2,1,0:T(8,128)(2,1)S(1)} %get-tuple-element.50, bf16[1,2,128,2048]{3,2,1,0:T(8,128)(2,1)S(1)} %bitcast.217, bf16[1,2,128,2048]{3,2,1,0:T(8,128)(2,1)} %bitcast.3, bf16[1,2,128,2048]{3,2,1,0:T(8,128)(2,1)S(1)} %bitcast.215, bf16[1,2,128,2048]{3,2,1,0:T(8,128)(2,1)S(1)} %copy-done.36), kind=kOutput, calls=%fused_computation.1 | convolution fusion | flops 6451888128 | bytes 13631488 | tf_op jit(solution)/shard_map/dot_general | solution.py:417
  580.3 56.6 %reduce-scatter.9.cloned.1.call-done = bf16[512,1536]{1,0:T(8,128)(2,1)} async-done(((bf16[2048,1536]{1,0:T(8,128)(2,1)}), bf16[512,1536]{1,0:T(8,128)(2,1)}) %reduce-scatter.9.cloned.1.call-update) | async-done | bytes 1572880 | tf_op jit(solution)/shard_map/reduce_scatter | solution.py:361
  667.5 40.0 %collective-permute-done.45 = bf16[256,2816]{1,0:T(8,128)(2,1)S(1)} collective-permute-done((bf16[256,2816]{1,0:T(8,128)(2,1)S(1)}, bf16[256,2816]{1,0:T(8,128)(2,1)S(1)}, u32[]{:S(2)}, u32[]{:S(2)}) %collective-permute-start.45) | collective-permute-done | bytes 1441824 | tf_op jit(solution)/shard_map/ppermute | solution.py:334
  720.8 32.9 %collective-permute-done.47 = f32[6272]{0:T(1024)S(1)} collective-permute-done((f32[6272]{0:T(1024)S(1)}, f32[6272]{0:T(1024)S(1)}, u32[]{:S(2)}, u32[]{:S(2)}) %collective-permute-start.47) | collective-permute-done | bytes 25120 | tf_op jit(solution)/shard_map/ppermute | solution.py:334
  770.7 16.8 %collective-permute-done.52 = bf16[256,1536]{1,0:T(8,128)(2,1)} collective-permute-done((bf16[256,1536]{1,0:T(8,128)(2,1)}, bf16[256,1536]{1,0:T(8,128)(2,1)}, u32[]{:S(2)}, u32[]{:S(2)}) %collective-permute-start.52) | collective-permute-done | bytes 786464 | tf_op jit(solution)/shard_map/ppermute | solution.py:334
  (357 shorter events, 253.1 us)
Async XLA Ops:
  7.2 174.7 %all-gather.5.cloned.1.call-start = ((), (), s32[]{:S(2)}) async-start(), calls=%async_computation.4 | async-start | bytes 7864320 | tf_op jit(solution)/shard_map/all_gather | solution.py:358
  29.5 187.4 %all-gather.7.cloned.1.call-start = ((), (), s32[]{:S(2)}) async-start(), calls=%async_computation.5 | async-start | bytes 2621440 | tf_op jit(solution)/shard_map/all_gather | solution.py:358
  43.9 47.6 %collective-permute-start.12 = (bf16[64,2048]{1,0:T(8,128)(2,1)}, bf16[64,2048]{1,0:T(8,128)(2,1)S(1)}, u32[]{:S(2)}, u32[]{:S(2)}) collective-permute-start(bf16[64,2048]{1,0:T(8,128)(2,1)} %param.17), channel_id=1, source_target_pairs={{0,2},{1,6},{2,3},{3,7},{4,0},{5,4},{6,1},{7,5},{8,10},{9,14},{10,... | collective-permute-start | bytes 786440 | tf_op jit(solution)/shard_map/ppermute | solution.py:334
  92.4 224.5 %all-gather.9.cloned.1.call-start = ((), (), s32[]{:S(2)}) async-start(), calls=%async_computation.6 | async-start | bytes 14417920 | tf_op jit(solution)/shard_map/all_gather | solution.py:358
  92.6 52.2 %collective-permute-start.21 = (bf16[256,2816]{1,0:T(8,128)(2,1)S(1)}, bf16[256,2816]{1,0:T(8,128)(2,1)S(1)}, u32[]{:S(2)}, u32[]{:S(2)}) collective-permute-start(bf16[256,2816]{1,0:T(8,128)(2,1)S(1)} %bitcast.185), channel_id=1, source_target_pairs={{0,2},{1,6},{2,3},{3,7},{4,0},{5,4},{6,1},{7,5},{8,10},{9,14},{10,... | collective-permute-start | bytes 4325384 | tf_op jit(solution)/shard_map/ppermute | solution.py:334
  99.4 45.4 %collective-permute-start.20 = (bf16[256,2816]{1,0:T(8,128)(2,1)S(1)}, bf16[256,2816]{1,0:T(8,128)(2,1)S(1)}, u32[]{:S(2)}, u32[]{:S(2)}) collective-permute-start(bf16[256,2816]{1,0:T(8,128)(2,1)S(1)} %bitcast.186), channel_id=1, source_target_pairs={{0,0},{1,4},{2,1},{3,5},{4,2},{5,6},{6,3},{7,7},{8,8},{9,12},{10,9... | collective-permute-start | bytes 4325384 | tf_op jit(solution)/shard_map/ppermute | solution.py:334
  146.8 202.5 %all-gather.11.cloned.1.call-start = ((), (), s32[]{:S(2)}) async-start(), calls=%async_computation.7 | async-start | bytes 7208960 | tf_op jit(solution)/shard_map/all_gather | solution.py:358
  175.0 46.6 %collective-permute-start.22 = (bf16[176,2048]{1,0:T(8,128)(2,1)}, bf16[176,2048]{1,0:T(8,128)(2,1)}, u32[]{:S(2)}, u32[]{:S(2)}) collective-permute-start(bf16[176,2048]{1,0:T(8,128)(2,1)} %param.20), channel_id=1, source_target_pairs={{0,0},{1,4},{2,1},{3,5},{4,2},{5,6},{6,3},{7,7},{8,8},{9,12},{10,9... | collective-permute-start | bytes 2162696 | tf_op jit(solution)/shard_map/ppermute | solution.py:334
  237.6 179.9 %reduce-scatter.5.cloned.1.call-start = ((), (), s32[]{:S(2)}) async-start(), calls=%async_computation.8 | async-start | bytes 7208960 | tf_op jit(solution)/shard_map/reduce_scatter | solution.py:361
  264.5 46.8 %collective-permute-start.18 = (bf16[2,128,2048]{2,1,0:T(8,128)(2,1)S(1)}, bf16[2,128,2048]{2,1,0:T(8,128)(2,1)S(1)}, u32[]{:S(2)}, u32[]{:S(2)}) collective-permute-start(bf16[2,128,2048]{2,1,0:T(8,128)(2,1)S(1)} %multiply_convert_fusion.4), channel_id=1, source_target_pairs={{0,1},{1,0},{2,3},{3,2},{4,5},{5,4},{6,7},{7,6},{8,9},{9,8},{10,11... | collective-permute-start | bytes 3145736 | tf_op jit(solution)/shard_map/ppermute | solution.py:334
  266.4 45.2 %collective-permute-start.25 = (bf16[2,128,2048]{2,1,0:T(8,128)(2,1)S(1)}, bf16[2,128,2048]{2,1,0:T(8,128)(2,1)S(1)}, u32[]{:S(2)}, u32[]{:S(2)}) collective-permute-start(bf16[2,128,2048]{2,1,0:T(8,128)(2,1)S(1)} %get-tuple-element.115), channel_id=1, source_target_pairs={{0,4},{1,5},{2,6},{3,7},{4,0},{5,1},{6,2},{7,3},{8,12},{9,13},{10,... | collective-permute-start | bytes 3145736 | tf_op jit(solution)/shard_map/ppermute | solution.py:334
  348.7 218.6 %reduce-scatter.7.cloned.1.call-start = ((), (), s32[]{:S(2)}) async-start(), calls=%async_computation.9 | async-start | bytes 14417920 | tf_op jit(solution)/shard_map/reduce_scatter | solution.py:361
  417.5 219.3 %reduce-scatter.9.cloned.1.call-start = ((), (), s32[]{:S(2)}) async-start(), calls=%async_computation.10 | async-start | bytes 7864320 | tf_op jit(solution)/shard_map/reduce_scatter | solution.py:361
  567.4 197.9 %reduce-scatter.11.cloned.1.call-start = ((), (), s32[]{:S(2)}) async-start(), calls=%async_computation.11 | async-start | bytes 2621440 | tf_op jit(solution)/shard_map/reduce_scatter | solution.py:361
  571.0 73.1 %collective-permute-start.28 = (bf16[2,128,2048]{2,1,0:T(8,128)(2,1)}, bf16[2,128,2048]{2,1,0:T(8,128)(2,1)}, u32[]{:S(2)}, u32[]{:S(2)}) collective-permute-start(bf16[2,128,2048]{2,1,0:T(8,128)(2,1)} %slice_bitcast_fusion.10), channel_id=1, source_target_pairs={{0,4},{1,5},{2,6},{3,7},{4,0},{5,1},{6,2},{7,3},{8,12},{9,13},{10,... | collective-permute-start | bytes 3145736 | tf_op jit(solution)/shard_map/ppermute | solution.py:334
  572.1 64.8 %collective-permute-start.40 = (bf16[2,128,2048]{2,1,0:T(8,128)(2,1)}, bf16[2,128,2048]{2,1,0:T(8,128)(2,1)}, u32[]{:S(2)}, u32[]{:S(2)}) collective-permute-start(bf16[2,128,2048]{2,1,0:T(8,128)(2,1)} %slice_bitcast_fusion.2), channel_id=1, source_target_pairs={{0,4},{1,5},{2,6},{3,7},{4,0},{5,1},{6,2},{7,3},{8,12},{9,13},{10,... | collective-permute-start | bytes 3145736 | tf_op jit(solution)/shard_map/ppermute | solution.py:334
  574.0 62.9 %collective-permute-start.42 = (bf16[2,128,2048]{2,1,0:T(8,128)(2,1)}, bf16[2,128,2048]{2,1,0:T(8,128)(2,1)}, u32[]{:S(2)}, u32[]{:S(2)}) collective-permute-start(bf16[2,128,2048]{2,1,0:T(8,128)(2,1)} %fusion.36), channel_id=1, source_target_pairs={{0,1},{1,0},{2,3},{3,2},{4,5},{5,4},{6,7},{7,6},{8,9},{9,8},{10,11... | collective-permute-start | bytes 3145736 | tf_op jit(solution)/shard_map/ppermute | solution.py:334
  574.5 69.6 %collective-permute-start.30 = (bf16[2,128,2048]{2,1,0:T(8,128)(2,1)S(1)}, bf16[2,128,2048]{2,1,0:T(8,128)(2,1)}, u32[]{:S(2)}, u32[]{:S(2)}) collective-permute-start(bf16[2,128,2048]{2,1,0:T(8,128)(2,1)S(1)} %fusion.40), channel_id=1, source_target_pairs={{0,1},{1,0},{2,3},{3,2},{4,5},{5,4},{6,7},{7,6},{8,9},{9,8},{10,11... | collective-permute-start | bytes 3145736 | tf_op jit(solution)/shard_map/ppermute | solution.py:334
  640.4 67.1 %collective-permute-start.45 = (bf16[256,2816]{1,0:T(8,128)(2,1)S(1)}, bf16[256,2816]{1,0:T(8,128)(2,1)S(1)}, u32[]{:S(2)}, u32[]{:S(2)}) collective-permute-start(bf16[256,2816]{1,0:T(8,128)(2,1)S(1)} %get-tuple-element.89), channel_id=1, source_target_pairs={{0,4},{1,6},{2,0},{3,2},{4,5},{5,7},{6,1},{7,3},{8,12},{9,14},{10,... | collective-permute-start | bytes 4325384 | tf_op jit(solution)/shard_map/ppermute | solution.py:334
  648.5 111.6 %collective-permute-start.31 = (bf16[2,128,2048]{2,1,0:T(8,128)(2,1)}, bf16[2,128,2048]{2,1,0:T(8,128)(2,1)}, u32[]{:S(2)}, u32[]{:S(2)}) collective-permute-start(bf16[2,128,2048]{2,1,0:T(8,128)(2,1)} %get-tuple-element.93), channel_id=1, source_target_pairs={{0,0},{1,2},{2,4},{3,6},{4,1},{5,3},{6,5},{7,7},{8,8},{9,10},{10,1... | collective-permute-start | bytes 3145736 | tf_op jit(solution)/shard_map/ppermute | solution.py:334
  658.0 102.0 %collective-permute-start.43 = (bf16[2,128,2048]{2,1,0:T(8,128)(2,1)}, bf16[2,128,2048]{2,1,0:T(8,128)(2,1)}, u32[]{:S(2)}, u32[]{:S(2)}) collective-permute-start(bf16[2,128,2048]{2,1,0:T(8,128)(2,1)} %get-tuple-element.92), channel_id=1, source_target_pairs={{0,0},{1,2},{2,4},{3,6},{4,1},{5,3},{6,5},{7,7},{8,8},{9,10},{10,1... | collective-permute-start | bytes 3145736 | tf_op jit(solution)/shard_map/ppermute | solution.py:334
  712.1 41.6 %collective-permute-start.47 = (f32[6272]{0:T(1024)S(1)}, f32[6272]{0:T(1024)S(1)}, u32[]{:S(2)}, u32[]{:S(2)}) collective-permute-start(f32[6272]{0:T(1024)S(1)} %add.208), channel_id=1, source_target_pairs={{0,2},{1,3},{2,0},{3,1},{4,6},{5,7},{6,4},{7,5},{8,10},{9,11},{10,... | collective-permute-start | bytes 75272 | tf_op jit(solution)/shard_map/ppermute | solution.py:334
  713.3 57.3 %collective-permute-start.51 = (bf16[256,1536]{1,0:T(8,128)(2,1)}, bf16[256,1536]{1,0:T(8,128)(2,1)}, u32[]{:S(2)}, u32[]{:S(2)}) collective-permute-start(bf16[256,1536]{1,0:T(8,128)(2,1)} %get-tuple-element.94), channel_id=1, source_target_pairs={{0,0},{1,2},{2,4},{3,6},{4,1},{5,3},{6,5},{7,7},{8,8},{9,10},{10,1... | collective-permute-start | bytes 2359304 | tf_op jit(solution)/shard_map/ppermute | solution.py:334
  720.8 66.7 %collective-permute-start.52 = (bf16[256,1536]{1,0:T(8,128)(2,1)}, bf16[256,1536]{1,0:T(8,128)(2,1)}, u32[]{:S(2)}, u32[]{:S(2)}) collective-permute-start(bf16[256,1536]{1,0:T(8,128)(2,1)} %get-tuple-element.95), channel_id=1, source_target_pairs={{0,4},{1,6},{2,0},{3,2},{4,5},{5,7},{6,1},{7,3},{8,12},{9,14},{10,... | collective-permute-start | bytes 2359304 | tf_op jit(solution)/shard_map/ppermute | solution.py:334
  (106 other events, 1561.4 us)
Sparse Core Ops, SparseCore 0:
  29.7 88.8 all-gather.4
  121.0 35.3 all-gather.6
  158.8 121.8 all-gather.8
  283.0 65.7 all-gather.10
  351.6 65.8 reduce-scatter.4
  420.4 112.0 reduce-scatter.6
  567.5 69.2 reduce-scatter.8
  639.8 35.1 reduce-scatter.10

commit v3 on v2

--- a/solution.py
+++ b/solution.py
@@ -362,10 +362,14 @@
             whole, "dp", scatter_dimension=0, tiled=True, axis_index_groups=groups
         )
 
-    def return_grad(pair, swap):
+    def return_grad(pair, swap, *earlier):
         rows = pair.shape[0] // 2
         first, second = ordered(pair[:rows], pair[rows:], swap)
-        return move(first, returns[0]).astype(F32) + move(second, returns[1]).astype(F32)
+        first = move(after(first, *earlier), returns[0])
+        return first, move(after(second, first), returns[1])
+
+    def whole_grad(parts):
+        return parts[0].astype(F32) + parts[1].astype(F32)
 
     def gather_rows(own):
         near = move(own, core_swap)
@@ -375,12 +379,12 @@
     def scatter_far(far_pair):
         return (far_pair[0].astype(F32) + move(far_pair[1], core_swap).astype(F32)).astype(BF)
 
-    def scatter_own(far, own_pair):
+    def scatter_own(arrived, own_pair):
         near = own_pair[0].astype(F32) + move(own_pair[1], core_swap).astype(F32)
-        return near + move(far, z_swap).astype(F32)
+        return near + arrived.astype(F32)
 
     def scatter_rows(far_pair, own_pair):
-        return scatter_own(scatter_far(far_pair), own_pair)
+        return scatter_own(move(scatter_far(far_pair), z_swap), own_pair)
 
     def split_rows(compute, *arrays):
         half = arrays[0].shape[0] // 2
@@ -471,7 +475,7 @@
         sig_gate = jax.nn.sigmoid(gate_part)
         hidden = (gate_part * sig_gate * up_part).astype(BF)
         down_whole = weight_grad(hidden, branch_in)
-        down_pair = scatter_grad(down_whole)
+        down_pair = scatter_grad(after(down_whole, down_mat))
         down_grad = return_grad(down_pair, swap)
         hidden_grad = dot_rows(after(branch_in, down_whole), down_mat, 1)
         gate_grad = hidden_grad * up_part * sig_gate * (1.0 + gate_part * (1.0 - sig_gate))
@@ -479,33 +483,36 @@
         both_grad = jnp.concatenate([gate_grad, up_grad], axis=-1).astype(BF)
         second_parts = split_rows(lambda part: dot_rows(part, gates_mat, 1).astype(BF), both_grad)
         second_far = scatter_far(second_parts[0])
-        second_grad = scatter_own(second_far, second_parts[1])
         gates_whole = weight_grad(second_in, after(both_grad, second_far, *second_parts))
-        second_grad = after(second_grad, gates_whole)
+        second_far = move(second_far, z_swap)
+        gates_pair = scatter_grad(after(gates_whole, down_pair, second_far))
+        second_grad = after(scatter_own(second_far, second_parts[1]), gates_whole)
         middle_grad, feed_terms = norm_back(middle, scale_two, feed_vec, second_grad)
         middle_grad = middle_grad + upstream
         feed_parts = split_rows(lambda part: dot_rows(part, down_mat, 0).astype(BF), hidden)
         attn_in = after(gather_rows(middle_grad.astype(BF)), *feed_parts)
-        feed_out = scatter_rows(*feed_parts)
-        block_out = move((valid * (middle + feed_out)).astype(BF), returns[0])
-        out_head = dot_rows(after(attn_in, down_grad), merge_mat, 1)
+        feed_far = move(after(scatter_far(feed_parts[0]), attn_in), z_swap)
+        feed_out = scatter_own(feed_far, feed_parts[1])
+        block_out = move(after((valid * (middle + feed_out)).astype(BF), *down_grad), returns[0])
+        out_head = dot_rows(attn_in, merge_mat, 1)
         proj_grad, bound_sum, head_sum = recur_backward(
             own, projected, mixed, out_head, states, bound_vec, head_vec
         )
         first_parts = split_rows(lambda part: dot_rows(part, mixer_mat, 1).astype(BF), proj_grad)
-        first_grad = scatter_rows(*first_parts)
+        first_far = move(scatter_far(first_parts[0]), z_swap)
+        first_grad = scatter_own(first_far, first_parts[1])
         merge_whole = weight_grad(head_out, attn_in)
         mixer_whole = weight_grad(first_in, proj_grad)
-        first_grad = after(first_grad, merge_whole, mixer_whole)
+        mixer_pair = scatter_grad(after(mixer_whole, gates_pair, *first_parts, *down_grad, block_out))
+        gates_grad = return_grad(gates_pair, swap, block_out)
+        first_grad = after(first_grad, merge_whole, mixer_whole, gates_grad[0])
         masked_grad, norm_terms = norm_back(masked, scale_one, norm_vec, first_grad)
-        input_grad = move((valid * (masked_grad + middle_grad)).astype(BF), returns[0])
-
-        gates_pair = scatter_grad(after(gates_whole, down_pair))
-        mixer_pair = scatter_grad(after(mixer_whole, gates_pair, *first_parts))
-        merge_pair = scatter_grad(after(merge_whole, mixer_pair))
-        gates_grad = return_grad(gates_pair, swap)
-        merge_grad = return_grad(merge_pair, swap)
-        mixer_grad = return_grad(mixer_pair, swap)
+        input_rows = (valid * (masked_grad + middle_grad)).astype(BF)
+
+        merge_pair = scatter_grad(after(merge_whole, mixer_pair, gates_grad[1]))
+        input_grad = move(after(input_rows, *gates_grad), returns[0])
+        mixer_grad = return_grad(mixer_pair, swap, input_grad)
+        merge_grad = return_grad(merge_pair, swap, *mixer_grad)
 
         bound_all = jnp.zeros((tensor_size, bound_sum.shape[1]), F32)
         bound_all = lax.dynamic_update_slice_in_dim(bound_all, bound_sum, role, 0)
@@ -516,7 +523,7 @@
             bound_all.reshape(-1),
         ]
         ends = np.cumsum([part.shape[0] for part in sums])
-        summed = sum_steps(after(jnp.concatenate(sums), down_grad, gates_grad), [*low_steps, *high_steps])
+        summed = sum_steps(jnp.concatenate(sums), [*low_steps, *high_steps])
 
         def shard_of(vector, count, at):
             return lax.dynamic_slice_in_dim(vector, at * count, count, 0)
@@ -525,13 +532,13 @@
             block_out,
             input_grad,
             shard_of(summed[: ends[0]], norm_gain.shape[0], dp_at),
-            mixer_grad.reshape(mixer_in.shape),
+            whole_grad(mixer_grad).reshape(mixer_in.shape),
             shard_of(summed[ends[2] :], lower_bound.shape[0], z_at * dp_size + dp_at),
             shard_of(summed[ends[1] : ends[2]], head_gain.shape[0], dp_at),
-            merge_grad,
+            whole_grad(merge_grad),
             shard_of(summed[ends[0] : ends[1]], feed_gain.shape[0], dp_at),
-            gates_grad.reshape(gate_up.shape),
-            down_grad,
+            whole_grad(gates_grad).reshape(gate_up.shape),
+            whole_grad(down_grad),
         )
 
     return local

time: 823 us -> 751 us (0.913)
  waiting for transfers between devices: 380 us -> 238 us
  starting transfers between devices: 157 us -> 214 us
  other arithmetic: 48.1 us -> 56.7 us
    ppermute x55, waiting for transfers between devices: 311 us -> 236 us  [move(): return lax.ppermute(array, AXES, pairs)]
    reduce_scatter x4, waiting for transfers between devices: 69.3 us -> 1.62 us  [scatter_grad(): lax.psum_scatter(whole, 'dp', scatter_dimension=0, tiled=True, axis_index...]
    ppermute x55, starting transfers between devices: 155 us -> 213 us  [move(): return lax.ppermute(array, AXES, pairs)]
    unnamed x143 -> x179, local copies, waits for them, and re-layouts: 21.3 us -> 22.3 us
  transfers between devices with their start and end apart: 63 -> 63, of which waited for: 26 -> 25; matrix products, arithmetic and copies ran while one was open for 23% -> 27% of each run, Pallas kernels for 6% -> 7%
where the time goes in v3:
time: 751 us; the launch traced here: 741 us
  waiting for transfers between devices  238 us (32%)
  starting transfers between devices  214 us (28%)
  matrix products  129 us (17%)
  other arithmetic  56.7 us (8%)
  Pallas kernels  52.2 us (7%)
  local copies, waits for them, and re-layouts  34.7 us (5%)
  between operations  16 us (2%)
    ppermute x55, waiting for transfers between devices, move(): return lax.ppermute(array, AXES, pairs)  236 us
    ppermute x55, starting transfers between devices, move(): return lax.ppermute(array, AXES, pairs)  213 us
    dot_general x12, matrix products, dot_rows(): lax.dot_general(first_mat, second_mat, (((first_mat.ndim - 1,), (second_d...  91.3 us
    dot_general x4, matrix products, weight_grad(): lax.dot_general(first_mat.reshape(-1, first_mat.shape[-1]), second_mat.re...  37.5 us
    pallas_call x1, Pallas kernels, recur_backward(): pl.pallas_call(backward_body, grid_spec=pltpu.PrefetchScalarGridSpec(num_...  31.3 us
    unnamed x179, local copies, waits for them, and re-layouts  22.3 us
    pallas_call x1, Pallas kernels, recur_forward(): pl.pallas_call(forward_body, grid_spec=pltpu.PrefetchScalarGridSpec(num_s...  20.9 us
  transfers between devices with their start and end apart: 63, of which 25 were waited for; matrix products, arithmetic and copies ran while one was open for 27% of the time, Pallas kernels for 7%

profile of v3, /device:TPU:0, one launch (start us, length us, event | category | flops | bytes accessed | tf_op | source)
XLA Modules:
  0.0 740.6 jit_solution(6841559734044574371)
XLA Ops:
  13.7 14.4 %collective-permute-done.8 = bf16[256,1536]{1,0:T(8,128)(2,1)S(1)} collective-permute-done((bf16[256,1536]{1,0:T(8,128)(2,1)S(1)}, bf16[256,1536]{1,0:T(8,128)(2,1)S(1)}, u32[]{:S(2)}, u32[]{:S(2)}) %collective-permute-start.8) | collective-permute-done | bytes 786464 | tf_op jit(solution)/shard_map/ppermute | solution.py:334
  43.9 41.9 %collective-permute-start.12 = (bf16[64,2048]{1,0:T(8,128)(2,1)}, bf16[64,2048]{1,0:T(8,128)(2,1)S(1)}, u32[]{:S(2)}, u32[]{:S(2)}) collective-permute-start(bf16[64,2048]{1,0:T(8,128)(2,1)} %param.17), channel_id=1, source_target_pairs={{0,2},{1,6},{2,3},{3,7},{4,0},{5,4},{6,1},{7,5},{8,10},{9,14},{10,... | collective-permute-start | bytes 786440 | tf_op jit(solution)/shard_map/ppermute | solution.py:334
  101.5 14.7 %collective-permute-done.6 = bf16[2,128,2048]{2,1,0:T(8,128)(2,1)} collective-permute-done((bf16[2,128,2048]{2,1,0:T(8,128)(2,1)S(1)}, bf16[2,128,2048]{2,1,0:T(8,128)(2,1)}, u32[]{:S(2)}, u32[]{:S(2)}) %collective-permute-start.6) | collective-permute-done | bytes 1048608 | tf_op jit(solution)/shard_map/ppermute | solution.py:334
  119.1 25.7 %collective-permute-done.21 = bf16[256,2816]{1,0:T(8,128)(2,1)S(1)} collective-permute-done((bf16[256,2816]{1,0:T(8,128)(2,1)S(1)}, bf16[256,2816]{1,0:T(8,128)(2,1)S(1)}, u32[]{:S(2)}, u32[]{:S(2)}) %collective-permute-start.21) | collective-permute-done | bytes 1441824 | tf_op jit(solution)/shard_map/ppermute | solution.py:334
  147.6 21.1 %collective-permute-start.10 = (bf16[4,8,64]{2,1,0:T(8,128)(2,1)S(1)}, bf16[4,8,64]{2,1,0:T(8,128)(2,1)S(1)}, u32[]{:S(2)}, u32[]{:S(2)}) collective-permute-start(bf16[4,8,64]{2,1,0:T(8,128)(2,1)S(1)} %fusion.54), channel_id=1, source_target_pairs={{0,1},{1,0},{2,3},{3,2},{4,5},{5,4},{6,7},{7,6},{8,9},{9,8},{10,11... | collective-permute-start | bytes 12296 | tf_op jit(solution)/shard_map/ppermute | solution.py:334
  191.3 20.9 %recur_forward.1 = (f32[4,2,128,512]{3,2,1,0:T(8,128)S(1)}, bf16[4,2,128,512]{3,2,1,0:T(8,128)(2,1)S(1)}, bf16[16,8,128,128]{3,2,1,0:T(8,128)(2,1)S(1)}) custom-call(s32[1]{0:T(128)} %bitcast.own_ref, f32[4,2,128,1536]{3,2,1,0:T(8,128)S(1)} %fusion.10.proj_ref, f32[1,512]{1,0:T(1,128)S(1)} %reshape.160.bound_ref, f32[1,128]{1,0:T(1,128)S(1)} %reshape.154.gain_ref), custom_call_target="tpu_custom_call" | custom-call | flops 1 | bytes 1 | tf_op jit(solution)/shard_map/recur_forward/pallas_call | solution.py:220
  221.6 9.4 %collective-permute-start.24 = (bf16[2,128,2048]{2,1,0:T(8,128)(2,1)}, bf16[2,128,2048]{2,1,0:T(8,128)(2,1)}, u32[]{:S(2)}, u32[]{:S(2)}) collective-permute-start(bf16[2,128,2048]{2,1,0:T(8,128)(2,1)} %param.21), channel_id=1, source_target_pairs={{0,0},{1,4},{2,1},{3,5},{4,2},{5,6},{6,3},{7,7},{8,8},{9,12},{10,9... | collective-permute-start | bytes 3145736 | tf_op jit(solution)/shard_map/ppermute | solution.py:334
  237.8 23.0 %collective-permute-done.16 = bf16[2,128,2048]{2,1,0:T(8,128)(2,1)} collective-permute-done((bf16[2,128,2048]{2,1,0:T(8,128)(2,1)}, bf16[2,128,2048]{2,1,0:T(8,128)(2,1)}, u32[]{:S(2)}, u32[]{:S(2)}) %collective-permute-start.16) | collective-permute-done | bytes 1048608 | tf_op jit(solution)/shard_map/ppermute | solution.py:334
  266.4 23.7 %collective-permute-done.26 = bf16[2,128,2048]{2,1,0:T(8,128)(2,1)S(1)} collective-permute-done((bf16[2,128,2048]{2,1,0:T(8,128)(2,1)S(1)}, bf16[2,128,2048]{2,1,0:T(8,128)(2,1)S(1)}, u32[]{:S(2)}, u32[]{:S(2)}) %collective-permute-start.26) | collective-permute-done | bytes 1048608 | tf_op jit(solution)/shard_map/ppermute | solution.py:334
  290.6 20.7 %collective-permute-done.18 = bf16[2,128,2048]{2,1,0:T(8,128)(2,1)S(1)} collective-permute-done((bf16[2,128,2048]{2,1,0:T(8,128)(2,1)S(1)}, bf16[2,128,2048]{2,1,0:T(8,128)(2,1)S(1)}, u32[]{:S(2)}, u32[]{:S(2)}) %collective-permute-start.18) | collective-permute-done | bytes 1048608 | tf_op jit(solution)/shard_map/ppermute | solution.py:334
  316.9 17.2 %fusion.4 = f32[4,2,128,2816]{3,2,1,0:T(8,128)S(1)} fusion(bf16[4,2,128,2048]{3,2,1,0:T(8,128)(2,1)} %pad_maximum_fusion.2, bf16[2048,2816]{1,0:T(8,128)(2,1)} %all-gather.9.cloned.1.call-done), kind=kOutput, calls=%fused_computation.7 | convolution fusion | flops 11811160064 | bytes 27262976 | tf_op jit(solution)/shard_map/dot_general | solution.py:394
  349.3 13.3 %multiply_convert_fusion.1 = (bf16[4,2,128,1408]{3,2,1,0:T(8,128)(2,1)S(1)}, bf16[4,2,128,1408]{3,2,1,0:T(8,128)(2,1)S(1)}) fusion(f32[4,2,128,2816]{3,2,1,0:T(8,128)} %copy-done.15, bf16[4,2,128,2048]{3,2,1,0:T(8,128)(2,1)} %pad_maximum_fusion.3, bf16[1408,2048]{1,0:T(8,128)(2,1)} %all-gather.11.cloned.1.call-done), kind=kOutput, calls=%fused_computation.23 | convolution fusion | flops 5924323328 | bytes 27262976 | tf_op jit(solution)/shard_map/dot_general | solution.py:394
  362.6 11.3 %fusion.21 = bf16[2,2,128,2048]{3,2,1,0:T(8,128)(2,1)S(1)} fusion(bf16[2048,2816]{1,0:T(8,128)(2,1)} %all-gather.9.cloned.1.call-done, bf16[4,2,128,1408]{3,2,1,0:T(8,128)(2,1)S(1)} %get-tuple-element.105, bf16[4,2,128,1408]{3,2,1,0:T(8,128)(2,1)S(1)} %get-tuple-element.104), kind=kOutput, calls=%fused_computation.32 | convolution fusion | flops 5918162944 | bytes 19398656 | tf_op jit(solution)/shard_map/dot_general | solution.py:394
  375.4 10.2 %fusion.18 = bf16[2,2,128,2048]{3,2,1,0:T(8,128)(2,1)} fusion(bf16[2048,2816]{1,0:T(8,128)(2,1)} %all-gather.9.cloned.1.call-done, bf16[4,2,128,1408]{3,2,1,0:T(8,128)(2,1)S(1)} %get-tuple-element.105, bf16[4,2,128,1408]{3,2,1,0:T(8,128)(2,1)S(1)} %get-tuple-element.104), kind=kOutput, calls=%fused_computation.31 | convolution fusion | flops 5918162944 | bytes 19398656 | tf_op jit(solution)/shard_map/dot_general | solution.py:394
  391.2 15.2 %bitcast_convert_fusion = bf16[2048,2816]{1,0:T(8,128)(2,1)} fusion(bf16[4,2,128,2048]{3,2,1,0:T(8,128)(2,1)S(1)} %copy-done.18, bf16[4,2,128,2816]{3,2,1,0:T(8,128)(2,1)S(1)} %pad_maximum_fusion), kind=kOutput, calls=%fused_computation | convolution fusion | flops 11816927232 | bytes 21495808 | tf_op jit(solution)/shard_map/dot_general | solution.py:421
  406.4 9.5 %collective-permute-done.32 = bf16[2,128,2048]{2,1,0:T(8,128)(2,1)S(1)} collective-permute-done((bf16[2,128,2048]{2,1,0:T(8,128)(2,1)}, bf16[2,128,2048]{2,1,0:T(8,128)(2,1)S(1)}, u32[]{:S(2)}, u32[]{:S(2)}) %collective-permute-start.32) | collective-permute-done | bytes 1048608 | tf_op jit(solution)/shard_map/ppermute | solution.py:334
  437.4 19.8 %collective-permute-done.34 = bf16[2,128,2048]{2,1,0:T(8,128)(2,1)S(1)} collective-permute-done((bf16[2,128,2048]{2,1,0:T(8,128)(2,1)S(1)}, bf16[2,128,2048]{2,1,0:T(8,128)(2,1)S(1)}, u32[]{:S(2)}, u32[]{:S(2)}) %collective-permute-start.34) | collective-permute-done | bytes 1048608 | tf_op jit(solution)/shard_map/ppermute | solution.py:334
  468.5 31.3 %recur_backward.1 = (bf16[4,2,128,1536]{3,2,1,0:T(8,128)(2,1)S(1)}, f32[1,512]{1,0:T(1,128)S(1)}, f32[1,128]{1,0:T(1,128)S(1)}) custom-call(s32[1]{0:T(128)} %bitcast.own_ref, f32[4,2,128,1536]{3,2,1,0:T(8,128)S(1)} %bitcast.177, f32[4,2,128,512]{3,2,1,0:T(8,128)S(1)} %get-tuple-element.60.mixed_ref, f32[4,2,128,512]{3,2,1,0:T(8,128)S(1)} %fusion.48.out_ref, ...), custom_call_target="tpu_custom_call" | custom-call | flops 1 | bytes 1 | tf_op jit(solution)/shard_map/recur_backward/pallas_call | solution.py:262
  502.4 10.4 %bitcast_convert_fusion.1 = bf16[2048,1536]{1,0:T(8,128)(2,1)} fusion(bf16[4,2,128,1536]{3,2,1,0:T(8,128)(2,1)S(1)} %get-tuple-element.62, bf16[1,2,128,2048]{3,2,1,0:T(8,128)(2,1)S(1)} %bitcast.219, bf16[1,2,128,2048]{3,2,1,0:T(8,128)(2,1)} %bitcast.3, bf16[1,2,128,2048]{3,2,1,0:T(8,128)(2,1)S(1)} %bitcast.217, bf16[1,2,128,2048]{3,2,1,0:T(8,128)(2,1)S(1)} %copy-done.35), kind=kOutput, calls=%fused_computation.1 | convolution fusion | flops 6451888128 | bytes 13631488 | tf_op jit(solution)/shard_map/dot_general | solution.py:421
  539.0 12.1 %collective-permute-start.41 = (bf16[2,128,2048]{2,1,0:T(8,128)(2,1)S(1)}, bf16[2,128,2048]{2,1,0:T(8,128)(2,1)S(1)}, u32[]{:S(2)}, u32[]{:S(2)}) collective-permute-start(bf16[2,128,2048]{2,1,0:T(8,128)(2,1)S(1)} %slice_bitcast_fusion), channel_id=1, source_target_pairs={{0,4},{1,5},{2,6},{3,7},{4,0},{5,1},{6,2},{7,3},{8,12},{9,13},{10,... | collective-permute-start | bytes 3145736 | tf_op jit(solution)/shard_map/ppermute | solution.py:334
  552.2 33.2 %collective-permute-start.44 = (bf16[256,2816]{1,0:T(8,128)(2,1)}, bf16[256,2816]{1,0:T(8,128)(2,1)S(1)}, u32[]{:S(2)}, u32[]{:S(2)}) collective-permute-start(bf16[256,2816]{1,0:T(8,128)(2,1)} %get-tuple-element.66), channel_id=1, source_target_pairs={{0,4},{1,6},{2,0},{3,2},{4,5},{5,7},{6,1},{7,3},{8,12},{9,14},{10,... | collective-permute-start | bytes 4325384 | tf_op jit(solution)/shard_map/ppermute | solution.py:334
  590.5 27.6 %collective-permute-done.44 = bf16[256,2816]{1,0:T(8,128)(2,1)S(1)} collective-permute-done((bf16[256,2816]{1,0:T(8,128)(2,1)}, bf16[256,2816]{1,0:T(8,128)(2,1)S(1)}, u32[]{:S(2)}, u32[]{:S(2)}) %collective-permute-start.44) | collective-permute-done | bytes 1441824 | tf_op jit(solution)/shard_map/ppermute | solution.py:334
  637.0 29.4 %collective-permute-start.46 = (f32[6272]{0:T(1024)S(1)}, f32[6272]{0:T(1024)S(1)}, u32[]{:S(2)}, u32[]{:S(2)}) collective-permute-start(f32[6272]{0:T(1024)S(1)} %pad_maximum_fusion.9), channel_id=1, source_target_pairs={{0,1},{1,0},{2,3},{3,2},{4,5},{5,4},{6,7},{7,6},{8,9},{9,8},{10,11... | collective-permute-start | bytes 75272 | tf_op jit(solution)/shard_map/ppermute | solution.py:334
  696.5 13.9 %collective-permute-done.52 = bf16[256,1536]{1,0:T(8,128)(2,1)S(1)} collective-permute-done((bf16[256,1536]{1,0:T(8,128)(2,1)S(1)}, bf16[256,1536]{1,0:T(8,128)(2,1)S(1)}, u32[]{:S(2)}, u32[]{:S(2)}) %collective-permute-start.52) | collective-permute-done | bytes 786464 | tf_op jit(solution)/shard_map/ppermute | solution.py:334
  (394 shorter events, 254.7 us)
Async XLA Ops:
  7.2 174.7 %all-gather.5.cloned.1.call-start = ((), (), s32[]{:S(2)}) async-start(), calls=%async_computation.4 | async-start | bytes 7864320 | tf_op jit(solution)/shard_map/all_gather | solution.py:358
  29.5 187.4 %all-gather.7.cloned.1.call-start = ((), (), s32[]{:S(2)}) async-start(), calls=%async_computation.5 | async-start | bytes 2621440 | tf_op jit(solution)/shard_map/all_gather | solution.py:358
  43.9 47.6 %collective-permute-start.12 = (bf16[64,2048]{1,0:T(8,128)(2,1)}, bf16[64,2048]{1,0:T(8,128)(2,1)S(1)}, u32[]{:S(2)}, u32[]{:S(2)}) collective-permute-start(bf16[64,2048]{1,0:T(8,128)(2,1)} %param.17), channel_id=1, source_target_pairs={{0,2},{1,6},{2,3},{3,7},{4,0},{5,4},{6,1},{7,5},{8,10},{9,14},{10,... | collective-permute-start | bytes 786440 | tf_op jit(solution)/shard_map/ppermute | solution.py:334
  92.4 224.5 %all-gather.9.cloned.1.call-start = ((), (), s32[]{:S(2)}) async-start(), calls=%async_computation.6 | async-start | bytes 14417920 | tf_op jit(solution)/shard_map/all_gather | solution.py:358
  92.6 52.2 %collective-permute-start.21 = (bf16[256,2816]{1,0:T(8,128)(2,1)S(1)}, bf16[256,2816]{1,0:T(8,128)(2,1)S(1)}, u32[]{:S(2)}, u32[]{:S(2)}) collective-permute-start(bf16[256,2816]{1,0:T(8,128)(2,1)S(1)} %bitcast.186), channel_id=1, source_target_pairs={{0,2},{1,6},{2,3},{3,7},{4,0},{5,4},{6,1},{7,5},{8,10},{9,14},{10,... | collective-permute-start | bytes 4325384 | tf_op jit(solution)/shard_map/ppermute | solution.py:334
  99.4 45.4 %collective-permute-start.20 = (bf16[256,2816]{1,0:T(8,128)(2,1)S(1)}, bf16[256,2816]{1,0:T(8,128)(2,1)S(1)}, u32[]{:S(2)}, u32[]{:S(2)}) collective-permute-start(bf16[256,2816]{1,0:T(8,128)(2,1)S(1)} %bitcast.187), channel_id=1, source_target_pairs={{0,0},{1,4},{2,1},{3,5},{4,2},{5,6},{6,3},{7,7},{8,8},{9,12},{10,9... | collective-permute-start | bytes 4325384 | tf_op jit(solution)/shard_map/ppermute | solution.py:334
  146.8 202.0 %all-gather.11.cloned.1.call-start = ((), (), s32[]{:S(2)}) async-start(), calls=%async_computation.7 | async-start | bytes 7208960 | tf_op jit(solution)/shard_map/all_gather | solution.py:358
  175.0 46.6 %collective-permute-start.22 = (bf16[176,2048]{1,0:T(8,128)(2,1)}, bf16[176,2048]{1,0:T(8,128)(2,1)}, u32[]{:S(2)}, u32[]{:S(2)}) collective-permute-start(bf16[176,2048]{1,0:T(8,128)(2,1)} %param.20), channel_id=1, source_target_pairs={{0,0},{1,4},{2,1},{3,5},{4,2},{5,6},{6,3},{7,7},{8,8},{9,12},{10,9... | collective-permute-start | bytes 2162696 | tf_op jit(solution)/shard_map/ppermute | solution.py:334
  181.9 39.7 %collective-permute-start.23 = (bf16[176,2048]{1,0:T(8,128)(2,1)}, bf16[176,2048]{1,0:T(8,128)(2,1)}, u32[]{:S(2)}, u32[]{:S(2)}) collective-permute-start(bf16[176,2048]{1,0:T(8,128)(2,1)} %param.20), channel_id=1, source_target_pairs={{0,2},{1,6},{2,3},{3,7},{4,0},{5,4},{6,1},{7,5},{8,10},{9,14},{10,... | collective-permute-start | bytes 2162696 | tf_op jit(solution)/shard_map/ppermute | solution.py:334
  237.5 180.0 %reduce-scatter.5.cloned.1.call-start = ((), (), s32[]{:S(2)}) async-start(), calls=%async_computation.8 | async-start | bytes 7208960 | tf_op jit(solution)/shard_map/reduce_scatter | solution.py:361
  264.5 46.9 %collective-permute-start.18 = (bf16[2,128,2048]{2,1,0:T(8,128)(2,1)S(1)}, bf16[2,128,2048]{2,1,0:T(8,128)(2,1)S(1)}, u32[]{:S(2)}, u32[]{:S(2)}) collective-permute-start(bf16[2,128,2048]{2,1,0:T(8,128)(2,1)S(1)} %multiply_convert_fusion.4), channel_id=1, source_target_pairs={{0,1},{1,0},{2,3},{3,2},{4,5},{5,4},{6,7},{7,6},{8,9},{9,8},{10,11... | collective-permute-start | bytes 3145736 | tf_op jit(solution)/shard_map/ppermute | solution.py:334
  266.4 45.2 %collective-permute-start.25 = (bf16[2,128,2048]{2,1,0:T(8,128)(2,1)S(1)}, bf16[2,128,2048]{2,1,0:T(8,128)(2,1)S(1)}, u32[]{:S(2)}, u32[]{:S(2)}) collective-permute-start(bf16[2,128,2048]{2,1,0:T(8,128)(2,1)S(1)} %get-tuple-element.131), channel_id=1, source_target_pairs={{0,4},{1,5},{2,6},{3,7},{4,0},{5,1},{6,2},{7,3},{8,12},{9,13},{10,... | collective-permute-start | bytes 3145736 | tf_op jit(solution)/shard_map/ppermute | solution.py:334
  348.8 184.8 %reduce-scatter.7.cloned.1.call-start = ((), (), s32[]{:S(2)}) async-start(), calls=%async_computation.9 | async-start | bytes 14417920 | tf_op jit(solution)/shard_map/reduce_scatter | solution.py:361
  417.5 200.7 %reduce-scatter.9.cloned.1.call-start = ((), (), s32[]{:S(2)}) async-start(), calls=%async_computation.10 | async-start | bytes 7864320 | tf_op jit(solution)/shard_map/reduce_scatter | solution.py:361
  458.3 54.5 %collective-permute-start.28 = (bf16[2,128,2048]{2,1,0:T(8,128)(2,1)}, bf16[2,128,2048]{2,1,0:T(8,128)(2,1)}, u32[]{:S(2)}, u32[]{:S(2)}) collective-permute-start(bf16[2,128,2048]{2,1,0:T(8,128)(2,1)} %slice_bitcast_fusion.10), channel_id=1, source_target_pairs={{0,4},{1,5},{2,6},{3,7},{4,0},{5,1},{6,2},{7,3},{8,12},{9,13},{10,... | collective-permute-start | bytes 3145736 | tf_op jit(solution)/shard_map/ppermute | solution.py:334
  460.6 39.2 %collective-permute-start.37 = (bf16[176,2048]{1,0:T(8,128)(2,1)S(1)}, bf16[176,2048]{1,0:T(8,128)(2,1)S(1)}, u32[]{:S(2)}, u32[]{:S(2)}) collective-permute-start(bf16[176,2048]{1,0:T(8,128)(2,1)S(1)} %get-tuple-element.115), channel_id=1, source_target_pairs={{0,0},{1,2},{2,4},{3,6},{4,1},{5,3},{6,5},{7,7},{8,8},{9,10},{10,1... | collective-permute-start | bytes 2162696 | tf_op jit(solution)/shard_map/ppermute | solution.py:334
  462.0 50.8 %collective-permute-start.36 = (bf16[2,128,2048]{2,1,0:T(8,128)(2,1)S(1)}, bf16[2,128,2048]{2,1,0:T(8,128)(2,1)}, u32[]{:S(2)}, u32[]{:S(2)}) collective-permute-start(bf16[2,128,2048]{2,1,0:T(8,128)(2,1)S(1)} %fusion.40), channel_id=1, source_target_pairs={{0,1},{1,0},{2,3},{3,2},{4,5},{5,4},{6,7},{7,6},{8,9},{9,8},{10,11... | collective-permute-start | bytes 3145736 | tf_op jit(solution)/shard_map/ppermute | solution.py:334
  533.7 161.0 %reduce-scatter.11.cloned.1.call-start = ((), (), s32[]{:S(2)}) async-start(), calls=%async_computation.11 | async-start | bytes 2621440 | tf_op jit(solution)/shard_map/reduce_scatter | solution.py:361
  539.0 46.4 %collective-permute-start.41 = (bf16[2,128,2048]{2,1,0:T(8,128)(2,1)S(1)}, bf16[2,128,2048]{2,1,0:T(8,128)(2,1)S(1)}, u32[]{:S(2)}, u32[]{:S(2)}) collective-permute-start(bf16[2,128,2048]{2,1,0:T(8,128)(2,1)S(1)} %slice_bitcast_fusion), channel_id=1, source_target_pairs={{0,4},{1,5},{2,6},{3,7},{4,0},{5,1},{6,2},{7,3},{8,12},{9,13},{10,... | collective-permute-start | bytes 3145736 | tf_op jit(solution)/shard_map/ppermute | solution.py:334
  552.1 66.1 %collective-permute-start.40 = (bf16[2,128,2048]{2,1,0:T(8,128)(2,1)}, bf16[2,128,2048]{2,1,0:T(8,128)(2,1)}, u32[]{:S(2)}, u32[]{:S(2)}) collective-permute-start(bf16[2,128,2048]{2,1,0:T(8,128)(2,1)} %slice_bitcast_fusion.2), channel_id=1, source_target_pairs={{0,4},{1,5},{2,6},{3,7},{4,0},{5,1},{6,2},{7,3},{8,12},{9,13},{10,... | collective-permute-start | bytes 3145736 | tf_op jit(solution)/shard_map/ppermute | solution.py:334
  552.2 66.0 %collective-permute-start.44 = (bf16[256,2816]{1,0:T(8,128)(2,1)}, bf16[256,2816]{1,0:T(8,128)(2,1)S(1)}, u32[]{:S(2)}, u32[]{:S(2)}) collective-permute-start(bf16[256,2816]{1,0:T(8,128)(2,1)} %get-tuple-element.66), channel_id=1, source_target_pairs={{0,4},{1,6},{2,0},{3,2},{4,5},{5,7},{6,1},{7,3},{8,12},{9,14},{10,... | collective-permute-start | bytes 4325384 | tf_op jit(solution)/shard_map/ppermute | solution.py:334
  586.8 40.2 %collective-permute-start.42 = (bf16[2,128,2048]{2,1,0:T(8,128)(2,1)}, bf16[2,128,2048]{2,1,0:T(8,128)(2,1)}, u32[]{:S(2)}, u32[]{:S(2)}) collective-permute-start(bf16[2,128,2048]{2,1,0:T(8,128)(2,1)} %fusion.36), channel_id=1, source_target_pairs={{0,1},{1,0},{2,3},{3,2},{4,5},{5,4},{6,7},{7,6},{8,9},{9,8},{10,11... | collective-permute-start | bytes 3145736 | tf_op jit(solution)/shard_map/ppermute | solution.py:334
  636.1 53.2 %collective-permute-start.51 = (bf16[256,1536]{1,0:T(8,128)(2,1)S(1)}, bf16[256,1536]{1,0:T(8,128)(2,1)S(1)}, u32[]{:S(2)}, u32[]{:S(2)}) collective-permute-start(bf16[256,1536]{1,0:T(8,128)(2,1)S(1)} %get-tuple-element.71), channel_id=1, source_target_pairs={{0,0},{1,2},{2,4},{3,6},{4,1},{5,3},{6,5},{7,7},{8,8},{9,10},{10,1... | collective-permute-start | bytes 2359304 | tf_op jit(solution)/shard_map/ppermute | solution.py:334
  637.0 31.6 %collective-permute-start.46 = (f32[6272]{0:T(1024)S(1)}, f32[6272]{0:T(1024)S(1)}, u32[]{:S(2)}, u32[]{:S(2)}) collective-permute-start(f32[6272]{0:T(1024)S(1)} %pad_maximum_fusion.9), channel_id=1, source_target_pairs={{0,1},{1,0},{2,3},{3,2},{4,5},{5,4},{6,7},{7,6},{8,9},{9,8},{10,11... | collective-permute-start | bytes 75272 | tf_op jit(solution)/shard_map/ppermute | solution.py:334
  (124 other events, 2512.1 us)
Sparse Core Ops, SparseCore 0:
  29.7 88.8 all-gather.4
  121.0 35.3 all-gather.6
  158.8 121.8 all-gather.8
  283.0 65.7 all-gather.10
  351.6 65.8 reduce-scatter.4
  420.4 112.1 reduce-scatter.6
  535.6 78.5 reduce-scatter.8
  618.3 34.6 reduce-scatter.10

commit v4 on v3

--- a/solution.py
+++ b/solution.py
@@ -433,7 +433,8 @@
         packed = jnp.zeros((dp_size, vector_ends[-1]), BF)
         packed = lax.dynamic_update_slice_in_dim(packed, jnp.concatenate(vectors)[None], dp_at, 0)
         packed = sum_steps(packed, high_steps)
-        tok = move(after(tokens, packed), spreads[0])
+        mixer_pair = [after(part, packed) for part in mixer_pair]
+        tok = move(after(tokens, *mixer_pair), spreads[0])
         merge_pair = spread_weight(after(head_merge, tok))
 
         bounds = jnp.zeros((tensor_size, dp_size, lower_bound.shape[0]), BF)
@@ -509,7 +510,7 @@
         masked_grad, norm_terms = norm_back(masked, scale_one, norm_vec, first_grad)
         input_rows = (valid * (masked_grad + middle_grad)).astype(BF)
 
-        merge_pair = scatter_grad(after(merge_whole, mixer_pair, gates_grad[1]))
+        merge_pair = scatter_grad(after(merge_whole, mixer_pair))
         input_grad = move(after(input_rows, *gates_grad), returns[0])
         mixer_grad = return_grad(mixer_pair, swap, input_grad)
         merge_grad = return_grad(merge_pair, swap, *mixer_grad)
@@ -523,7 +524,7 @@
             bound_all.reshape(-1),
         ]
         ends = np.cumsum([part.shape[0] for part in sums])
-        summed = sum_steps(jnp.concatenate(sums), [*low_steps, *high_steps])
+        summed = sum_steps(jnp.concatenate(sums), [*high_steps, *low_steps])
 
         def shard_of(vector, count, at):
             return lax.dynamic_slice_in_dim(vector, at * count, count, 0)

time: 751 us -> 726 us (0.967)
  waiting for transfers between devices: 238 us -> 208 us
    ppermute x55, waiting for transfers between devices: 236 us -> 182 us  [move(): return lax.ppermute(array, AXES, pairs)]
    reduce_scatter x4, waiting for transfers between devices: 1.62 us -> 26.3 us  [scatter_grad(): lax.psum_scatter(whole, 'dp', scatter_dimension=0, tiled=True, axis_index...]
  transfers between devices with their start and end apart: 63 -> 63, of which waited for: 25 -> 24; matrix products, arithmetic and copies ran while one was open for 27% -> 28% of each run, Pallas kernels for 7% -> 7%
where the time goes in v4:
time: 726 us; the launch traced here: 716 us
  starting transfers between devices  217 us (30%)
  waiting for transfers between devices  208 us (29%)
  matrix products  128 us (18%)
  other arithmetic  54.7 us (8%)
  Pallas kernels  52.2 us (7%)
  local copies, waits for them, and re-layouts  39.3 us (5%)
  between operations  16 us (2%)
    ppermute x55, starting transfers between devices, move(): return lax.ppermute(array, AXES, pairs)  216 us
    ppermute x55, waiting for transfers between devices, move(): return lax.ppermute(array, AXES, pairs)  182 us
    dot_general x12, matrix products, dot_rows(): lax.dot_general(first_mat, second_mat, (((first_mat.ndim - 1,), (second_d...  90.9 us
    dot_general x4, matrix products, weight_grad(): lax.dot_general(first_mat.reshape(-1, first_mat.shape[-1]), second_mat.re...  37.5 us
    pallas_call x1, Pallas kernels, recur_backward(): pl.pallas_call(backward_body, grid_spec=pltpu.PrefetchScalarGridSpec(num_...  31.3 us
    reduce_scatter x4, waiting for transfers between devices, scatter_grad(): lax.psum_scatter(whole, 'dp', scatter_dimension=0, tiled=True, axis_index...  26.3 us
    unnamed x179, local copies, waits for them, and re-layouts  24.3 us
    pallas_call x1, Pallas kernels, recur_forward(): pl.pallas_call(forward_body, grid_spec=pltpu.PrefetchScalarGridSpec(num_s...  20.9 us
  transfers between devices with their start and end apart: 63, of which 24 were waited for; matrix products, arithmetic and copies ran while one was open for 28% of the time, Pallas kernels for 7%

profile of v4, /device:TPU:0, one launch (start us, length us, event | category | flops | bytes accessed | tf_op | source)
XLA Modules:
  0.0 715.8 jit_solution(1201772687965905971)
XLA Ops:
  36.2 41.4 %collective-permute-start.12 = (bf16[64,2048]{1,0:T(8,128)(2,1)}, bf16[64,2048]{1,0:T(8,128)(2,1)S(1)}, u32[]{:S(2)}, u32[]{:S(2)}) collective-permute-start(bf16[64,2048]{1,0:T(8,128)(2,1)} %param.17), channel_id=1, source_target_pairs={{0,2},{1,6},{2,3},{3,7},{4,0},{5,4},{6,1},{7,5},{8,10},{9,14},{10,... | collective-permute-start | bytes 786440 | tf_op jit(solution)/shard_map/ppermute | solution.py:334
  86.0 12.0 %collective-permute-start.21 = (bf16[256,2816]{1,0:T(8,128)(2,1)S(1)}, bf16[256,2816]{1,0:T(8,128)(2,1)S(1)}, u32[]{:S(2)}, u32[]{:S(2)}) collective-permute-start(bf16[256,2816]{1,0:T(8,128)(2,1)S(1)} %bitcast.187), channel_id=1, source_target_pairs={{0,2},{1,6},{2,3},{3,7},{4,0},{5,4},{6,1},{7,5},{8,10},{9,14},{10,... | collective-permute-start | bytes 4325384 | tf_op jit(solution)/shard_map/ppermute | solution.py:334
  98.0 13.9 %collective-permute-done.8 = bf16[2,128,2048]{2,1,0:T(8,128)(2,1)} collective-permute-done((bf16[2,128,2048]{2,1,0:T(8,128)(2,1)S(1)}, bf16[2,128,2048]{2,1,0:T(8,128)(2,1)}, u32[]{:S(2)}, u32[]{:S(2)}) %collective-permute-start.8) | collective-permute-done | bytes 1048608 | tf_op jit(solution)/shard_map/ppermute | solution.py:334
  115.7 22.2 %collective-permute-done.21 = bf16[256,2816]{1,0:T(8,128)(2,1)S(1)} collective-permute-done((bf16[256,2816]{1,0:T(8,128)(2,1)S(1)}, bf16[256,2816]{1,0:T(8,128)(2,1)S(1)}, u32[]{:S(2)}, u32[]{:S(2)}) %collective-permute-start.21) | collective-permute-done | bytes 1441824 | tf_op jit(solution)/shard_map/ppermute | solution.py:334
  140.7 23.4 %collective-permute-start.10 = (bf16[4,8,64]{2,1,0:T(8,128)(2,1)S(1)}, bf16[4,8,64]{2,1,0:T(8,128)(2,1)S(1)}, u32[]{:S(2)}, u32[]{:S(2)}) collective-permute-start(bf16[4,8,64]{2,1,0:T(8,128)(2,1)S(1)} %fusion.54), channel_id=1, source_target_pairs={{0,1},{1,0},{2,3},{3,2},{4,5},{5,4},{6,7},{7,6},{8,9},{9,8},{10,11... | collective-permute-start | bytes 12296 | tf_op jit(solution)/shard_map/ppermute | solution.py:334
  186.7 20.9 %recur_forward.1 = (f32[4,2,128,512]{3,2,1,0:T(8,128)S(1)}, bf16[4,2,128,512]{3,2,1,0:T(8,128)(2,1)S(1)}, bf16[16,8,128,128]{3,2,1,0:T(8,128)(2,1)S(1)}) custom-call(s32[1]{0:T(128)} %bitcast.1.own_ref, f32[4,2,128,1536]{3,2,1,0:T(8,128)S(1)} %fusion.10.proj_ref, f32[1,512]{1,0:T(1,128)S(1)} %reshape.160.bound_ref, f32[1,128]{1,0:T(1,128)S(1)} %reshape.154.gain_ref), custom_call_target="tpu_custom_call" | custom-call | flops 1 | bytes 1 | tf_op jit(solution)/shard_map/recur_forward/pallas_call | solution.py:220
  217.1 9.6 %collective-permute-start.24 = (bf16[2,128,2048]{2,1,0:T(8,128)(2,1)}, bf16[2,128,2048]{2,1,0:T(8,128)(2,1)}, u32[]{:S(2)}, u32[]{:S(2)}) collective-permute-start(bf16[2,128,2048]{2,1,0:T(8,128)(2,1)} %param.21), channel_id=1, source_target_pairs={{0,0},{1,4},{2,1},{3,5},{4,2},{5,6},{6,3},{7,7},{8,8},{9,12},{10,9... | collective-permute-start | bytes 3145736 | tf_op jit(solution)/shard_map/ppermute | solution.py:334
  233.4 22.9 %collective-permute-done.16 = bf16[2,128,2048]{2,1,0:T(8,128)(2,1)} collective-permute-done((bf16[2,128,2048]{2,1,0:T(8,128)(2,1)}, bf16[2,128,2048]{2,1,0:T(8,128)(2,1)}, u32[]{:S(2)}, u32[]{:S(2)}) %collective-permute-start.16) | collective-permute-done | bytes 1048608 | tf_op jit(solution)/shard_map/ppermute | solution.py:334
  261.9 23.7 %collective-permute-done.26 = bf16[2,128,2048]{2,1,0:T(8,128)(2,1)S(1)} collective-permute-done((bf16[2,128,2048]{2,1,0:T(8,128)(2,1)S(1)}, bf16[2,128,2048]{2,1,0:T(8,128)(2,1)S(1)}, u32[]{:S(2)}, u32[]{:S(2)}) %collective-permute-start.26) | collective-permute-done | bytes 1048608 | tf_op jit(solution)/shard_map/ppermute | solution.py:334
  286.1 20.7 %collective-permute-done.18 = bf16[2,128,2048]{2,1,0:T(8,128)(2,1)S(1)} collective-permute-done((bf16[2,128,2048]{2,1,0:T(8,128)(2,1)S(1)}, bf16[2,128,2048]{2,1,0:T(8,128)(2,1)S(1)}, u32[]{:S(2)}, u32[]{:S(2)}) %collective-permute-start.18) | collective-permute-done | bytes 1048608 | tf_op jit(solution)/shard_map/ppermute | solution.py:334
  312.0 17.2 %fusion.4 = f32[4,2,128,2816]{3,2,1,0:T(8,128)S(1)} fusion(bf16[4,2,128,2048]{3,2,1,0:T(8,128)(2,1)} %pad_maximum_fusion.2, bf16[2048,2816]{1,0:T(8,128)(2,1)} %all-gather.9.cloned.1.call-done), kind=kOutput, calls=%fused_computation.7 | convolution fusion | flops 11811160064 | bytes 27262976 | tf_op jit(solution)/shard_map/dot_general | solution.py:394
  344.4 13.3 %multiply_convert_fusion.1 = (bf16[4,2,128,1408]{3,2,1,0:T(8,128)(2,1)S(1)}, bf16[4,2,128,1408]{3,2,1,0:T(8,128)(2,1)S(1)}) fusion(f32[4,2,128,2816]{3,2,1,0:T(8,128)} %copy-done.15, bf16[4,2,128,2048]{3,2,1,0:T(8,128)(2,1)} %pad_maximum_fusion.3, bf16[1408,2048]{1,0:T(8,128)(2,1)} %all-gather.11.cloned.1.call-done), kind=kOutput, calls=%fused_computation.23 | convolution fusion | flops 5924323328 | bytes 27262976 | tf_op jit(solution)/shard_map/dot_general | solution.py:394
  357.7 11.2 %fusion.21 = bf16[2,2,128,2048]{3,2,1,0:T(8,128)(2,1)S(1)} fusion(bf16[2048,2816]{1,0:T(8,128)(2,1)} %all-gather.9.cloned.1.call-done, bf16[4,2,128,1408]{3,2,1,0:T(8,128)(2,1)S(1)} %get-tuple-element.109, bf16[4,2,128,1408]{3,2,1,0:T(8,128)(2,1)S(1)} %get-tuple-element.108), kind=kOutput, calls=%fused_computation.32 | convolution fusion | flops 5918162944 | bytes 19398656 | tf_op jit(solution)/shard_map/dot_general | solution.py:394
  370.5 10.4 %fusion.18 = bf16[2,2,128,2048]{3,2,1,0:T(8,128)(2,1)} fusion(bf16[2048,2816]{1,0:T(8,128)(2,1)} %all-gather.9.cloned.1.call-done, bf16[4,2,128,1408]{3,2,1,0:T(8,128)(2,1)S(1)} %get-tuple-element.109, bf16[4,2,128,1408]{3,2,1,0:T(8,128)(2,1)S(1)} %get-tuple-element.108), kind=kOutput, calls=%fused_computation.31 | convolution fusion | flops 5918162944 | bytes 19398656 | tf_op jit(solution)/shard_map/dot_general | solution.py:394
  386.3 15.2 %bitcast_convert_fusion = bf16[2048,2816]{1,0:T(8,128)(2,1)} fusion(bf16[4,2,128,2048]{3,2,1,0:T(8,128)(2,1)S(1)} %copy-done.18, bf16[4,2,128,2816]{3,2,1,0:T(8,128)(2,1)S(1)} %pad_maximum_fusion), kind=kOutput, calls=%fused_computation | convolution fusion | flops 11816927232 | bytes 21495808 | tf_op jit(solution)/shard_map/dot_general | solution.py:421
  401.5 9.5 %collective-permute-done.32 = bf16[2,128,2048]{2,1,0:T(8,128)(2,1)S(1)} collective-permute-done((bf16[2,128,2048]{2,1,0:T(8,128)(2,1)}, bf16[2,128,2048]{2,1,0:T(8,128)(2,1)S(1)}, u32[]{:S(2)}, u32[]{:S(2)}) %collective-permute-start.32) | collective-permute-done | bytes 1048608 | tf_op jit(solution)/shard_map/ppermute | solution.py:334
  431.6 19.8 %collective-permute-done.34 = bf16[2,128,2048]{2,1,0:T(8,128)(2,1)S(1)} collective-permute-done((bf16[2,128,2048]{2,1,0:T(8,128)(2,1)S(1)}, bf16[2,128,2048]{2,1,0:T(8,128)(2,1)S(1)}, u32[]{:S(2)}, u32[]{:S(2)}) %collective-permute-start.34) | collective-permute-done | bytes 1048608 | tf_op jit(solution)/shard_map/ppermute | solution.py:334
  462.7 31.3 %recur_backward.1 = (bf16[4,2,128,1536]{3,2,1,0:T(8,128)(2,1)S(1)}, f32[1,512]{1,0:T(1,128)S(1)}, f32[1,128]{1,0:T(1,128)S(1)}) custom-call(s32[1]{0:T(128)} %bitcast.1.own_ref, f32[4,2,128,1536]{3,2,1,0:T(8,128)S(1)} %bitcast.177, f32[4,2,128,512]{3,2,1,0:T(8,128)S(1)} %get-tuple-element.64.mixed_ref, f32[4,2,128,512]{3,2,1,0:T(8,128)S(1)} %fusion.48.out_ref, ...), custom_call_target="tpu_custom_call" | custom-call | flops 1 | bytes 1 | tf_op jit(solution)/shard_map/recur_backward/pallas_call | solution.py:262
  496.6 10.4 %bitcast_convert_fusion.1 = bf16[2048,1536]{1,0:T(8,128)(2,1)} fusion(bf16[4,2,128,1536]{3,2,1,0:T(8,128)(2,1)S(1)} %get-tuple-element.66, bf16[1,2,128,2048]{3,2,1,0:T(8,128)(2,1)S(1)} %bitcast.219, bf16[1,2,128,2048]{3,2,1,0:T(8,128)(2,1)} %bitcast.4, bf16[1,2,128,2048]{3,2,1,0:T(8,128)(2,1)S(1)} %bitcast.217, bf16[1,2,128,2048]{3,2,1,0:T(8,128)(2,1)S(1)} %copy-done.35), kind=kOutput, calls=%fused_computation.1 | convolution fusion | flops 6451888128 | bytes 13631488 | tf_op jit(solution)/shard_map/dot_general | solution.py:421
  529.4 12.0 %collective-permute-start.41 = (bf16[2,128,2048]{2,1,0:T(8,128)(2,1)S(1)}, bf16[2,128,2048]{2,1,0:T(8,128)(2,1)S(1)}, u32[]{:S(2)}, u32[]{:S(2)}) collective-permute-start(bf16[2,128,2048]{2,1,0:T(8,128)(2,1)S(1)} %slice_bitcast_fusion), channel_id=1, source_target_pairs={{0,4},{1,5},{2,6},{3,7},{4,0},{5,1},{6,2},{7,3},{8,12},{9,13},{10,... | collective-permute-start | bytes 3145736 | tf_op jit(solution)/shard_map/ppermute | solution.py:334
  555.8 27.1 %collective-permute-start.44 = (bf16[256,2816]{1,0:T(8,128)(2,1)}, bf16[256,2816]{1,0:T(8,128)(2,1)}, u32[]{:S(2)}, u32[]{:S(2)}) collective-permute-start(bf16[256,2816]{1,0:T(8,128)(2,1)} %get-tuple-element.70), channel_id=1, source_target_pairs={{0,4},{1,6},{2,0},{3,2},{4,5},{5,7},{6,1},{7,3},{8,12},{9,14},{10,... | collective-permute-start | bytes 4325384 | tf_op jit(solution)/shard_map/ppermute | solution.py:334
  582.9 25.6 %reduce-scatter.9.cloned.1.call-done = bf16[512,1536]{1,0:T(8,128)(2,1)} async-done(((bf16[2048,1536]{1,0:T(8,128)(2,1)}), bf16[512,1536]{1,0:T(8,128)(2,1)}) %reduce-scatter.9.cloned.1.call-update) | async-done | bytes 1572880 | tf_op jit(solution)/shard_map/reduce_scatter | solution.py:361
  618.4 28.6 %collective-permute-start.46 = (f32[6272]{0:T(1024)S(1)}, f32[6272]{0:T(1024)S(1)}, u32[]{:S(2)}, u32[]{:S(2)}) collective-permute-start(f32[6272]{0:T(1024)S(1)} %pad_maximum_fusion.9), channel_id=1, source_target_pairs={{0,4},{1,5},{2,6},{3,7},{4,0},{5,1},{6,2},{7,3},{8,12},{9,13},{10,... | collective-permute-start | bytes 75272 | tf_op jit(solution)/shard_map/ppermute | solution.py:334
  673.2 13.1 %collective-permute-done.52 = bf16[256,1536]{1,0:T(8,128)(2,1)S(1)} collective-permute-done((bf16[256,1536]{1,0:T(8,128)(2,1)S(1)}, bf16[256,1536]{1,0:T(8,128)(2,1)S(1)}, u32[]{:S(2)}, u32[]{:S(2)}) %collective-permute-start.52) | collective-permute-done | bytes 786464 | tf_op jit(solution)/shard_map/ppermute | solution.py:334
  (394 shorter events, 244.7 us)
Async XLA Ops:
  7.2 170.1 %all-gather.5.cloned.1.call-start = ((), (), s32[]{:S(2)}) async-start(), calls=%async_computation.4 | async-start | bytes 7864320 | tf_op jit(solution)/shard_map/all_gather | solution.py:358
  33.7 179.4 %all-gather.7.cloned.1.call-start = ((), (), s32[]{:S(2)}) async-start(), calls=%async_computation.5 | async-start | bytes 2621440 | tf_op jit(solution)/shard_map/all_gather | solution.py:358
  36.2 47.9 %collective-permute-start.12 = (bf16[64,2048]{1,0:T(8,128)(2,1)}, bf16[64,2048]{1,0:T(8,128)(2,1)S(1)}, u32[]{:S(2)}, u32[]{:S(2)}) collective-permute-start(bf16[64,2048]{1,0:T(8,128)(2,1)} %param.17), channel_id=1, source_target_pairs={{0,2},{1,6},{2,3},{3,7},{4,0},{5,4},{6,1},{7,5},{8,10},{9,14},{10,... | collective-permute-start | bytes 786440 | tf_op jit(solution)/shard_map/ppermute | solution.py:334
  80.5 31.3 %collective-permute-start.8 = (bf16[2,128,2048]{2,1,0:T(8,128)(2,1)S(1)}, bf16[2,128,2048]{2,1,0:T(8,128)(2,1)}, u32[]{:S(2)}, u32[]{:S(2)}) collective-permute-start(bf16[2,128,2048]{2,1,0:T(8,128)(2,1)S(1)} %multiply_convert_fusion.5), channel_id=1, source_target_pairs={{0,1},{1,0},{2,3},{3,2},{4,5},{5,4},{6,7},{7,6},{8,9},{9,8},{10,11... | collective-permute-start | bytes 3145736 | tf_op jit(solution)/shard_map/ppermute | solution.py:334
  85.0 227.0 %all-gather.9.cloned.1.call-start = ((), (), s32[]{:S(2)}) async-start(), calls=%async_computation.6 | async-start | bytes 14417920 | tf_op jit(solution)/shard_map/all_gather | solution.py:358
  85.2 29.5 %collective-permute-start.20 = (bf16[256,2816]{1,0:T(8,128)(2,1)S(1)}, bf16[256,2816]{1,0:T(8,128)(2,1)S(1)}, u32[]{:S(2)}, u32[]{:S(2)}) collective-permute-start(bf16[256,2816]{1,0:T(8,128)(2,1)S(1)} %bitcast.186), channel_id=1, source_target_pairs={{0,0},{1,4},{2,1},{3,5},{4,2},{5,6},{6,3},{7,7},{8,8},{9,12},{10,9... | collective-permute-start | bytes 4325384 | tf_op jit(solution)/shard_map/ppermute | solution.py:334
  86.0 51.9 %collective-permute-start.21 = (bf16[256,2816]{1,0:T(8,128)(2,1)S(1)}, bf16[256,2816]{1,0:T(8,128)(2,1)S(1)}, u32[]{:S(2)}, u32[]{:S(2)}) collective-permute-start(bf16[256,2816]{1,0:T(8,128)(2,1)S(1)} %bitcast.187), channel_id=1, source_target_pairs={{0,2},{1,6},{2,3},{3,7},{4,0},{5,4},{6,1},{7,5},{8,10},{9,14},{10,... | collective-permute-start | bytes 4325384 | tf_op jit(solution)/shard_map/ppermute | solution.py:334
  139.9 204.0 %all-gather.11.cloned.1.call-start = ((), (), s32[]{:S(2)}) async-start(), calls=%async_computation.7 | async-start | bytes 7208960 | tf_op jit(solution)/shard_map/all_gather | solution.py:358
  170.4 46.7 %collective-permute-start.22 = (bf16[176,2048]{1,0:T(8,128)(2,1)}, bf16[176,2048]{1,0:T(8,128)(2,1)}, u32[]{:S(2)}, u32[]{:S(2)}) collective-permute-start(bf16[176,2048]{1,0:T(8,128)(2,1)} %param.20), channel_id=1, source_target_pairs={{0,0},{1,4},{2,1},{3,5},{4,2},{5,6},{6,3},{7,7},{8,8},{9,12},{10,9... | collective-permute-start | bytes 2162696 | tf_op jit(solution)/shard_map/ppermute | solution.py:334
  177.3 39.8 %collective-permute-start.23 = (bf16[176,2048]{1,0:T(8,128)(2,1)}, bf16[176,2048]{1,0:T(8,128)(2,1)}, u32[]{:S(2)}, u32[]{:S(2)}) collective-permute-start(bf16[176,2048]{1,0:T(8,128)(2,1)} %param.20), channel_id=1, source_target_pairs={{0,2},{1,6},{2,3},{3,7},{4,0},{5,4},{6,1},{7,5},{8,10},{9,14},{10,... | collective-permute-start | bytes 2162696 | tf_op jit(solution)/shard_map/ppermute | solution.py:334
  233.1 178.5 %reduce-scatter.5.cloned.1.call-start = ((), (), s32[]{:S(2)}) async-start(), calls=%async_computation.8 | async-start | bytes 7208960 | tf_op jit(solution)/shard_map/reduce_scatter | solution.py:361
  260.1 46.8 %collective-permute-start.18 = (bf16[2,128,2048]{2,1,0:T(8,128)(2,1)S(1)}, bf16[2,128,2048]{2,1,0:T(8,128)(2,1)S(1)}, u32[]{:S(2)}, u32[]{:S(2)}) collective-permute-start(bf16[2,128,2048]{2,1,0:T(8,128)(2,1)S(1)} %multiply_convert_fusion.4), channel_id=1, source_target_pairs={{0,1},{1,0},{2,3},{3,2},{4,5},{5,4},{6,7},{7,6},{8,9},{9,8},{10,11... | collective-permute-start | bytes 3145736 | tf_op jit(solution)/shard_map/ppermute | solution.py:334
  261.9 45.2 %collective-permute-start.25 = (bf16[2,128,2048]{2,1,0:T(8,128)(2,1)S(1)}, bf16[2,128,2048]{2,1,0:T(8,128)(2,1)S(1)}, u32[]{:S(2)}, u32[]{:S(2)}) collective-permute-start(bf16[2,128,2048]{2,1,0:T(8,128)(2,1)S(1)} %get-tuple-element.135), channel_id=1, source_target_pairs={{0,4},{1,5},{2,6},{3,7},{4,0},{5,1},{6,2},{7,3},{8,12},{9,13},{10,... | collective-permute-start | bytes 3145736 | tf_op jit(solution)/shard_map/ppermute | solution.py:334
  343.9 183.9 %reduce-scatter.7.cloned.1.call-start = ((), (), s32[]{:S(2)}) async-start(), calls=%async_computation.9 | async-start | bytes 14417920 | tf_op jit(solution)/shard_map/reduce_scatter | solution.py:361
  411.7 196.7 %reduce-scatter.9.cloned.1.call-start = ((), (), s32[]{:S(2)}) async-start(), calls=%async_computation.10 | async-start | bytes 7864320 | tf_op jit(solution)/shard_map/reduce_scatter | solution.py:361
  452.5 54.5 %collective-permute-start.28 = (bf16[2,128,2048]{2,1,0:T(8,128)(2,1)}, bf16[2,128,2048]{2,1,0:T(8,128)(2,1)}, u32[]{:S(2)}, u32[]{:S(2)}) collective-permute-start(bf16[2,128,2048]{2,1,0:T(8,128)(2,1)} %slice_bitcast_fusion.10), channel_id=1, source_target_pairs={{0,4},{1,5},{2,6},{3,7},{4,0},{5,1},{6,2},{7,3},{8,12},{9,13},{10,... | collective-permute-start | bytes 3145736 | tf_op jit(solution)/shard_map/ppermute | solution.py:334
  454.8 39.2 %collective-permute-start.37 = (bf16[176,2048]{1,0:T(8,128)(2,1)S(1)}, bf16[176,2048]{1,0:T(8,128)(2,1)S(1)}, u32[]{:S(2)}, u32[]{:S(2)}) collective-permute-start(bf16[176,2048]{1,0:T(8,128)(2,1)S(1)} %get-tuple-element.119), channel_id=1, source_target_pairs={{0,0},{1,2},{2,4},{3,6},{4,1},{5,3},{6,5},{7,7},{8,8},{9,10},{10,1... | collective-permute-start | bytes 2162696 | tf_op jit(solution)/shard_map/ppermute | solution.py:334
  456.2 50.8 %collective-permute-start.36 = (bf16[2,128,2048]{2,1,0:T(8,128)(2,1)S(1)}, bf16[2,128,2048]{2,1,0:T(8,128)(2,1)}, u32[]{:S(2)}, u32[]{:S(2)}) collective-permute-start(bf16[2,128,2048]{2,1,0:T(8,128)(2,1)S(1)} %fusion.40), channel_id=1, source_target_pairs={{0,1},{1,0},{2,3},{3,2},{4,5},{5,4},{6,7},{7,6},{8,9},{9,8},{10,11... | collective-permute-start | bytes 3145736 | tf_op jit(solution)/shard_map/ppermute | solution.py:334
  527.9 143.6 %reduce-scatter.11.cloned.1.call-start = ((), (), s32[]{:S(2)}) async-start(), calls=%async_computation.11 | async-start | bytes 2621440 | tf_op jit(solution)/shard_map/reduce_scatter | solution.py:361
  543.7 64.8 %collective-permute-start.40 = (bf16[2,128,2048]{2,1,0:T(8,128)(2,1)}, bf16[2,128,2048]{2,1,0:T(8,128)(2,1)}, u32[]{:S(2)}, u32[]{:S(2)}) collective-permute-start(bf16[2,128,2048]{2,1,0:T(8,128)(2,1)} %slice_bitcast_fusion.2), channel_id=1, source_target_pairs={{0,4},{1,5},{2,6},{3,7},{4,0},{5,1},{6,2},{7,3},{8,12},{9,13},{10,... | collective-permute-start | bytes 3145736 | tf_op jit(solution)/shard_map/ppermute | solution.py:334
  549.8 58.7 %collective-permute-start.42 = (bf16[2,128,2048]{2,1,0:T(8,128)(2,1)}, bf16[2,128,2048]{2,1,0:T(8,128)(2,1)}, u32[]{:S(2)}, u32[]{:S(2)}) collective-permute-start(bf16[2,128,2048]{2,1,0:T(8,128)(2,1)} %fusion.36), channel_id=1, source_target_pairs={{0,1},{1,0},{2,3},{3,2},{4,5},{5,4},{6,7},{7,6},{8,9},{9,8},{10,11... | collective-permute-start | bytes 3145736 | tf_op jit(solution)/shard_map/ppermute | solution.py:334
  555.8 59.9 %collective-permute-start.44 = (bf16[256,2816]{1,0:T(8,128)(2,1)}, bf16[256,2816]{1,0:T(8,128)(2,1)}, u32[]{:S(2)}, u32[]{:S(2)}) collective-permute-start(bf16[256,2816]{1,0:T(8,128)(2,1)} %get-tuple-element.70), channel_id=1, source_target_pairs={{0,4},{1,6},{2,0},{3,2},{4,5},{5,7},{6,1},{7,3},{8,12},{9,14},{10,... | collective-permute-start | bytes 4325384 | tf_op jit(solution)/shard_map/ppermute | solution.py:334
  617.5 44.2 %collective-permute-start.51 = (bf16[256,1536]{1,0:T(8,128)(2,1)S(1)}, bf16[256,1536]{1,0:T(8,128)(2,1)S(1)}, u32[]{:S(2)}, u32[]{:S(2)}) collective-permute-start(bf16[256,1536]{1,0:T(8,128)(2,1)S(1)} %get-tuple-element.75), channel_id=1, source_target_pairs={{0,0},{1,2},{2,4},{3,6},{4,1},{5,3},{6,5},{7,7},{8,8},{9,10},{10,1... | collective-permute-start | bytes 2359304 | tf_op jit(solution)/shard_map/ppermute | solution.py:334
  618.4 29.4 %collective-permute-start.46 = (f32[6272]{0:T(1024)S(1)}, f32[6272]{0:T(1024)S(1)}, u32[]{:S(2)}, u32[]{:S(2)}) collective-permute-start(f32[6272]{0:T(1024)S(1)} %pad_maximum_fusion.9), channel_id=1, source_target_pairs={{0,4},{1,5},{2,6},{3,7},{4,0},{5,1},{6,2},{7,3},{8,12},{9,13},{10,... | collective-permute-start | bytes 75272 | tf_op jit(solution)/shard_map/ppermute | solution.py:334
  (124 other events, 2420.9 us)
Sparse Core Ops, SparseCore 0:
  33.8 86.6 all-gather.4
  122.9 35.3 all-gather.6
  160.7 114.1 all-gather.8
  277.2 65.7 all-gather.10
  345.8 65.8 reduce-scatter.4
  414.6 112.1 reduce-scatter.6
  529.8 78.5 reduce-scatter.8
  612.0 35.1 reduce-scatter.10
